TPU v7x, 32 devices: a whole 2x2x4 slice. The times are simulated.
32 devices in a mesh: fsdp: 2 (over x), ctx: 4 (over y, core), tp: 4 (over z).
Axes of the slice: x: 2, y: 2, z: 4, core: 2. Of those that a mesh axis runs over, the one named last changes fastest.
Arguments:
- latents: float32 [4, 256, 16], P('fsdp', 'ctx'), may hold values from -6 to 6
- noise: float32 [4, 256, 16], P('fsdp', 'ctx'), may hold values from -6 to 6
- var_target: float32 [4, 256, 16], P('fsdp', 'ctx'), may hold values from -6 to 6
- timesteps: int32 [4], P('fsdp'), may hold values from 0 to 999
- labels: int32 [4], P('fsdp'), may hold values from 0 to 1000
- attend_weight: float32 [4, 1024, 3, 1024], P(None, 'fsdp', None, 'tp'), may hold values from -0.1875 to 0.1875
- attend_mean: float32 [4, 1024, 3, 1024], P(None, 'fsdp', None, 'tp'), may hold values from -0.00044727084 to 0.00044727084
- attend_square: float32 [4, 1024, 3, 1024], P(None, 'fsdp', None, 'tp'), may hold values from 1.2503201e-08 to 5.0012805e-08
- hidden_weight: float32 [4, 1024, 4, 1024], P(None, 'fsdp', None, 'tp'), may hold values from -0.1875 to 0.1875
- hidden_mean: float32 [4, 1024, 4, 1024], P(None, 'fsdp', None, 'tp'), may hold values from -0.00044727084 to 0.00044727084
- hidden_square: float32 [4, 1024, 4, 1024], P(None, 'fsdp', None, 'tp'), may hold values from 1.2503201e-08 to 5.0012805e-08
- output_weight: float32 [4, 1024, 5, 1024], P(None, 'fsdp', None, 'tp'), may hold values from -0.1875 to 0.1875
- output_mean: float32 [4, 1024, 5, 1024], P(None, 'fsdp', None, 'tp'), may hold values from -0.00044727084 to 0.00044727084
- output_square: float32 [4, 1024, 5, 1024], P(None, 'fsdp', None, 'tp'), may hold values from 1.2503201e-08 to 5.0012805e-08
- patch_weight: float32 [1024, 16], P('fsdp'), may hold values from -1.5 to 1.5
- patch_mean: float32 [1024, 16], P('fsdp'), may hold values from -0.00044727084 to 0.00044727084
- patch_square: float32 [1024, 16], P('fsdp'), may hold values from 1.2503201e-08 to 5.0012805e-08
- freq_weight: float32 [1024, 256], P('fsdp'), may hold values from -0.375 to 0.375
- freq_mean: float32 [1024, 256], P('fsdp'), may hold values from -0.00044727084 to 0.00044727084
- freq_square: float32 [1024, 256], P('fsdp'), may hold values from 1.2503201e-08 to 5.0012805e-08
- time_weight: float32 [1024, 1024], P('fsdp'), may hold values from -0.1875 to 0.1875
- time_mean: float32 [1024, 1024], P('fsdp'), may hold values from -0.00044727084 to 0.00044727084
- time_square: float32 [1024, 1024], P('fsdp'), may hold values from 1.2503201e-08 to 5.0012805e-08
- label_table: float32 [1024, 1001], P('fsdp'), may hold values from -1.5 to 1.5
- label_mean: float32 [1024, 1001], P('fsdp'), may hold values from -0.00044727084 to 0.00044727084
- label_square: float32 [1024, 1001], P('fsdp'), may hold values from 1.2503201e-08 to 5.0012805e-08
- cond_weight: float32 [1024, 26624], P('fsdp', 'tp'), may hold values from -0.1875 to 0.1875
- cond_mean: float32 [1024, 26624], P('fsdp', 'tp'), may hold values from -0.00044727084 to 0.00044727084
- cond_square: float32 [1024, 26624], P('fsdp', 'tp'), may hold values from 1.2503201e-08 to 5.0012805e-08
- head_weight: float32 [1024, 32], P('fsdp'), may hold values from -0.1875 to 0.1875
- head_mean: float32 [1024, 32], P('fsdp'), may hold values from -0.00044727084 to 0.00044727084
- head_square: float32 [1024, 32], P('fsdp'), may hold values from 1.2503201e-08 to 5.0012805e-08
Outputs:
- loss: float32 [], replicated
- grad_norm: float32 [], replicated
- attend_next: float32 [4, 1024, 3, 1024], P(None, 'fsdp', None, 'tp')
- attend_mean_next: float32 [4, 1024, 3, 1024], P(None, 'fsdp', None, 'tp')
- attend_square_next: float32 [4, 1024, 3, 1024], P(None, 'fsdp', None, 'tp')
- hidden_next: float32 [4, 1024, 4, 1024], P(None, 'fsdp', None, 'tp')
- hidden_mean_next: float32 [4, 1024, 4, 1024], P(None, 'fsdp', None, 'tp')
- hidden_square_next: float32 [4, 1024, 4, 1024], P(None, 'fsdp', None, 'tp')
- output_next: float32 [4, 1024, 5, 1024], P(None, 'fsdp', None, 'tp')
- output_mean_next: float32 [4, 1024, 5, 1024], P(None, 'fsdp', None, 'tp')
- output_square_next: float32 [4, 1024, 5, 1024], P(None, 'fsdp', None, 'tp')
- patch_next: float32 [1024, 16], P('fsdp')
- patch_mean_next: float32 [1024, 16], P('fsdp')
- patch_square_next: float32 [1024, 16], P('fsdp')
- freq_next: float32 [1024, 256], P('fsdp')
- freq_mean_next: float32 [1024, 256], P('fsdp')
- freq_square_next: float32 [1024, 256], P('fsdp')
- time_next: float32 [1024, 1024], P('fsdp')
- time_mean_next: float32 [1024, 1024], P('fsdp')
- time_square_next: float32 [1024, 1024], P('fsdp')
- label_next: float32 [1024, 1001], P('fsdp')
- label_mean_next: float32 [1024, 1001], P('fsdp')
- label_square_next: float32 [1024, 1001], P('fsdp')
- cond_next: float32 [1024, 26624], P('fsdp', 'tp')
- cond_mean_next: float32 [1024, 26624], P('fsdp', 'tp')
- cond_square_next: float32 [1024, 26624], P('fsdp', 'tp')
- head_next: float32 [1024, 32], P('fsdp')
- head_mean_next: float32 [1024, 32], P('fsdp')
- head_square_next: float32 [1024, 32], P('fsdp')
All inputs are finite; a program needn't handle non-finite values.
Results may differ from a plain program's by a relative error of at most 0.0065.
The roundings to bfloat16 on the way count: a program that leaves them out, or rounds other values in their place, can miss the bound.
Values may be sent and summed in bfloat16 or wider, within the bound.
A program may use at most 576 MiB of HBM per device.

v0:
```python
import math

import jax
import jax.numpy as jnp
from jax import lax
from jax.sharding import PartitionSpec as P

HEAD_DIM = 64
FREQ = 256
GRID = 16
STEP = 5


HIGH = lax.Precision.HIGHEST
RATE = 0.05
DECAY = 0.1
BETA = 0.5
EPSILON = 1e-08
CLIP = 1.0


def modln(h, shift, scale):
    mean = jnp.mean(h, -1, keepdims=True)
    cent = h - mean
    var = jnp.mean(cent * cent, -1, keepdims=True)
    return cent * lax.rsqrt(var + 1e-06) * (1.0 + scale) + shift


def gelu_tanh(v):
    return jax.nn.gelu(v, approximate=True)


def noise_level(steps):
    phase = (steps.astype(jnp.float32) / 1000.0 + 0.008) / 1.008 * (0.5 * math.pi)
    return jnp.cos(phase) ** 2


def time_freqs(steps):
    half = FREQ // 2
    rates = jnp.exp(-math.log(10000.0) * jnp.arange(half, dtype=jnp.float32) / half)
    angles = steps.astype(jnp.float32)[:, None] * rates[None, :]
    return jnp.concatenate([jnp.cos(angles), jnp.sin(angles)], -1)


def positions(first, count, width):
    index = first + jnp.arange(count, dtype=jnp.int32)
    row = (index // GRID).astype(jnp.float32)
    column = (index % GRID).astype(jnp.float32)
    quarter = width // 4
    rates = jnp.power(10000.0, -jnp.arange(quarter, dtype=jnp.float32) / quarter)
    across = column[:, None] * rates[None, :]
    down = row[:, None] * rates[None, :]
    return jnp.concatenate([jnp.sin(across), jnp.cos(across), jnp.sin(down), jnp.cos(down)], -1)


def adamw(weight, mean, square, grad):
    mean_next = BETA * mean + (1.0 - BETA) * grad
    square_next = BETA * square + (1.0 - BETA) * grad * grad
    fixed_mean = mean_next / (1.0 - BETA**STEP)
    fixed_square = square_next / (1.0 - BETA**STEP)
    weight_next = weight - RATE * (fixed_mean / (jnp.sqrt(fixed_square) + EPSILON) + DECAY * weight)
    return [weight_next, mean_next, square_next]


def tp_total(part):
    return lax.psum(part, "tp")


def tp_back(part):
    return lax.psum(part, "tp")


def gather_layer(attend, hidden, output):
    return (
        lax.all_gather(attend.astype(jnp.bfloat16), "fsdp", axis=0, tiled=True),
        lax.all_gather(hidden.astype(jnp.bfloat16), "fsdp", axis=0, tiled=True),
        lax.all_gather(output.astype(jnp.bfloat16), "fsdp", axis=0, tiled=True),
    )


def reduce_layer(d_attend, d_hidden, d_output):
    shards = (
        lax.psum_scatter(d_attend, "fsdp", scatter_dimension=0, tiled=True),
        lax.psum_scatter(d_hidden, "fsdp", scatter_dimension=0, tiled=True),
        lax.psum_scatter(d_output, "fsdp", scatter_dimension=0, tiled=True),
    )
    return lax.psum((shards[0], shards[1], shards[2]), "ctx")


def layer_parts(h, mods, weights):
    attend, hidden, output = weights
    count, rows, width = h.shape
    local = attend.shape[2]
    heads = local // HEAD_DIM
    scale = 1.0 / math.sqrt(HEAD_DIM)
    u_in = modln(h, mods[:, 0, None], mods[:, 1, None]).astype(jnp.bfloat16)
    qkv = jnp.einsum("gsd,dke->gske", u_in, attend, preferred_element_type=jnp.float32).astype(
        jnp.bfloat16
    )
    keys, values = (
        lax.all_gather(qkv[:, :, 1], "ctx", axis=1, tiled=True),
        lax.all_gather(qkv[:, :, 2], "ctx", axis=1, tiled=True),
    )
    query = qkv[:, :, 0].reshape(count, rows, heads, HEAD_DIM)
    keys = keys.reshape(count, -1, heads, HEAD_DIM)
    values = values.reshape(count, -1, heads, HEAD_DIM)
    scores = jnp.einsum("gqhe,gkhe->ghqk", query, keys, preferred_element_type=jnp.float32) * scale
    top = jnp.max(scores, -1, keepdims=True)
    expo = jnp.exp(scores - top)
    probs = expo / jnp.sum(expo, -1, keepdims=True)
    probs_low = probs.astype(jnp.bfloat16)
    attended = (
        jnp.einsum("ghqk,gkhe->gqhe", probs_low, values, preferred_element_type=jnp.float32)
        .astype(jnp.bfloat16)
        .reshape(count, rows, local)
    )
    branch_a = tp_total(
        jnp.einsum("gsc,dc->gsd", attended, output[:, 0], preferred_element_type=jnp.float32)
    )
    h_mid = h + mods[:, 2, None] * branch_a
    w_in = modln(h_mid, mods[:, 3, None], mods[:, 4, None]).astype(jnp.bfloat16)
    pre = jnp.einsum("gsd,dkc->gskc", w_in, hidden, preferred_element_type=jnp.float32).reshape(
        count, rows, 4 * local
    )
    act = gelu_tanh(pre).astype(jnp.bfloat16)
    out_mlp = output[:, 1:].reshape(width, 4 * local)
    branch_m = tp_total(jnp.einsum("gsk,dk->gsd", act, out_mlp, preferred_element_type=jnp.float32))
    h_out = h_mid + mods[:, 5, None] * branch_m
    return (
        h_out,
        u_in,
        qkv,
        query,
        keys,
        values,
        probs,
        probs_low,
        attended,
        branch_a,
        h_mid,
        w_in,
        pre,
        act,
        out_mlp,
        branch_m,
    )


def layer_backward(h, mods, weights, grad_out):
    attend, hidden, output = weights
    (
        h_out,
        u_in,
        qkv,
        query,
        keys,
        values,
        probs,
        probs_low,
        attended,
        branch_a,
        h_mid,
        w_in,
        pre,
        act,
        out_mlp,
        branch_m,
    ) = layer_parts(h, mods, weights)
    count, rows, width = h.shape
    local = attend.shape[2]
    heads = local // HEAD_DIM
    scale = 1.0 / math.sqrt(HEAD_DIM)
    d_gate_m = jnp.sum(grad_out * branch_m, 1)
    d_branch = (mods[:, 5, None] * grad_out).astype(jnp.bfloat16)
    d_act = jnp.einsum("gsd,dk->gsk", d_branch, out_mlp, preferred_element_type=jnp.float32)
    d_out_mlp = jnp.einsum("gsd,gsk->dk", d_branch, act, preferred_element_type=jnp.float32)
    _, gelu_back = jax.vjp(gelu_tanh, pre)
    d_pre = gelu_back(d_act)[0].astype(jnp.bfloat16).reshape(count, rows, 4, local)
    d_hidden = jnp.einsum("gsd,gskc->dkc", w_in, d_pre, preferred_element_type=jnp.float32)
    d_w = tp_back(jnp.einsum("gskc,dkc->gsd", d_pre, hidden, preferred_element_type=jnp.float32))
    _, norm_back = jax.vjp(modln, h_mid, mods[:, 3, None], mods[:, 4, None])
    d_mid, d_shift_m, d_scale_m = norm_back(d_w)
    d_mid = d_mid + grad_out
    d_gate_a = jnp.sum(d_mid * branch_a, 1)
    d_branch_a = (mods[:, 2, None] * d_mid).astype(jnp.bfloat16)
    d_att = jnp.einsum(
        "gsd,dc->gsc", d_branch_a, output[:, 0], preferred_element_type=jnp.float32
    ).astype(jnp.bfloat16)
    d_out_att = jnp.einsum("gsd,gsc->dc", d_branch_a, attended, preferred_element_type=jnp.float32)
    d_att = d_att.reshape(count, rows, heads, HEAD_DIM)
    d_probs = jnp.einsum("gqhe,gkhe->ghqk", d_att, values, preferred_element_type=jnp.float32)
    d_values = jnp.einsum("ghqk,gqhe->gkhe", probs_low, d_att, preferred_element_type=jnp.float32)
    d_scores = (probs * (d_probs - jnp.sum(d_probs * probs, -1, keepdims=True))).astype(
        jnp.bfloat16
    )
    d_query = (
        jnp.einsum("ghqk,gkhe->gqhe", d_scores, keys, preferred_element_type=jnp.float32) * scale
    ).astype(jnp.bfloat16)
    d_keys = (
        jnp.einsum("ghqk,gqhe->gkhe", d_scores, query, preferred_element_type=jnp.float32) * scale
    )
    d_keys, d_values = (
        lax.psum_scatter(
            d_keys.reshape(count, -1, local).astype(jnp.bfloat16),
            "ctx",
            scatter_dimension=1,
            tiled=True,
        ).astype(jnp.float32),
        lax.psum_scatter(
            d_values.reshape(count, -1, local).astype(jnp.bfloat16),
            "ctx",
            scatter_dimension=1,
            tiled=True,
        ).astype(jnp.float32),
    )
    d_qkv = jnp.stack(
        [
            d_query.reshape(count, rows, local),
            d_keys.astype(jnp.bfloat16),
            d_values.astype(jnp.bfloat16),
        ],
        2,
    )
    d_attend = jnp.einsum("gsd,gske->dke", u_in, d_qkv, preferred_element_type=jnp.float32)
    d_u = tp_back(jnp.einsum("gske,dke->gsd", d_qkv, attend, preferred_element_type=jnp.float32))
    _, norm_back = jax.vjp(modln, h, mods[:, 0, None], mods[:, 1, None])
    d_h, d_shift_a, d_scale_a = norm_back(d_u)
    d_mods = jnp.stack(
        [d_shift_a[:, 0], d_scale_a[:, 0], d_gate_a, d_shift_m[:, 0], d_scale_m[:, 0], d_gate_m], 1
    )
    d_output = jnp.concatenate([d_out_att[:, None], d_out_mlp.reshape(width, 4, local)], 1)
    return (d_h + d_mid, d_mods, (d_attend, d_hidden, d_output))


def per_device(
    latents,
    noise,
    var_target,
    timesteps,
    labels,
    attend_weight,
    attend_mean,
    attend_square,
    hidden_weight,
    hidden_mean,
    hidden_square,
    output_weight,
    output_mean,
    output_square,
    patch_weight,
    patch_mean,
    patch_square,
    freq_weight,
    freq_mean,
    freq_square,
    time_weight,
    time_mean,
    time_square,
    label_table,
    label_mean,
    label_square,
    cond_weight,
    cond_mean,
    cond_square,
    head_weight,
    head_mean,
    head_square,
):
    stem = (
        lax.all_gather(patch_weight.astype(jnp.bfloat16), "fsdp", axis=0, tiled=True),
        lax.all_gather(freq_weight.astype(jnp.bfloat16), "fsdp", axis=0, tiled=True),
        lax.all_gather(time_weight.astype(jnp.bfloat16), "fsdp", axis=0, tiled=True),
        lax.all_gather(label_table.astype(jnp.bfloat16), "fsdp", axis=0, tiled=True),
        lax.all_gather(cond_weight.astype(jnp.bfloat16), "fsdp", axis=0, tiled=True),
        lax.all_gather(head_weight.astype(jnp.bfloat16), "fsdp", axis=0, tiled=True),
    )
    patch_full, freq_full, time_full, table_full, cond_full, head_full = stem
    count, rows, _ = latents.shape
    width = patch_full.shape[0]
    layers = attend_weight.shape[0]
    level = noise_level(timesteps)[:, None, None]
    noisy = (jnp.sqrt(level) * latents + jnp.sqrt(1.0 - level) * noise).astype(jnp.bfloat16)
    first = lax.axis_index("ctx") * rows
    h = (
        jnp.einsum("gsp,dp->gsd", noisy, patch_full, preferred_element_type=jnp.float32)
        + positions(first, rows, width)[None]
    )
    freqs = time_freqs(timesteps).astype(jnp.bfloat16)
    act = jnp.dot(freqs, freq_full.T, preferred_element_type=jnp.float32)
    swish = jax.nn.silu(act).astype(jnp.bfloat16)
    temb = jnp.dot(swish, time_full.T, preferred_element_type=jnp.float32)
    onehot = (labels[:, None] == jnp.arange(table_full.shape[1], dtype=jnp.int32)[None]).astype(
        jnp.bfloat16
    )
    cvec = temb + jnp.dot(onehot, table_full.T, preferred_element_type=jnp.float32)
    cond_in = jax.nn.silu(cvec).astype(jnp.bfloat16)
    mods = lax.all_gather(
        jnp.dot(cond_in, cond_full, preferred_element_type=jnp.float32), "tp", axis=1, tiled=True
    ).reshape(count, -1, width)
    inputs = []
    kept = []
    for layer in range(layers):
        weights = gather_layer(attend_weight[layer], hidden_weight[layer], output_weight[layer])
        inputs.append(h)
        kept.append(weights)
        h = layer_parts(h, mods[:, 6 * layer : 6 * layer + 6], weights)[0]
    final_in = modln(h, mods[:, 6 * layers, None], mods[:, 6 * layers + 1, None]).astype(
        jnp.bfloat16
    )
    pred = jnp.einsum("gsd,dp->gsp", final_in, head_full, preferred_element_type=jnp.float32)
    diff = pred - jnp.concatenate([noise, var_target], -1)
    loss_local = jnp.sum(diff * diff) / lax.axis_size("tp")
    loss = lax.psum(loss_local, ("fsdp", "ctx", "tp"))
    d_pred = (2.0 * diff).astype(jnp.bfloat16)
    d_head = jnp.einsum("gsd,gsp->dp", final_in, d_pred, preferred_element_type=jnp.float32)
    d_final = jnp.einsum("gsp,dp->gsd", d_pred, head_full, preferred_element_type=jnp.float32)
    _, norm_back = jax.vjp(modln, h, mods[:, 6 * layers, None], mods[:, 6 * layers + 1, None])
    d_h, d_shift_f, d_scale_f = norm_back(d_final)
    mod_grads = [None] * layers
    layer_shards = [None] * layers
    for layer in reversed(range(layers)):
        weights = gather_layer(attend_weight[layer], hidden_weight[layer], output_weight[layer])
        d_h, d_layer_mods, grads = layer_backward(
            inputs[layer], mods[:, 6 * layer : 6 * layer + 6], weights, d_h
        )
        mod_grads[layer] = d_layer_mods
        layer_shards[layer] = reduce_layer(grads[0], grads[1], grads[2])
    d_mods = jnp.concatenate(mod_grads + [d_shift_f, d_scale_f], 1).reshape(count, -1)
    columns = cond_full.shape[1]
    d_local = lax.dynamic_slice_in_dim(d_mods, lax.axis_index("tp") * columns, columns, 1)
    d_silu = tp_back(
        jnp.dot(d_local, cond_full.T, precision=HIGH, preferred_element_type=jnp.float32)
    )
    _, silu_back = jax.vjp(jax.nn.silu, cvec)
    d_cvec = silu_back(d_silu)[0]
    d_swish = jnp.dot(d_cvec, time_full, precision=HIGH, preferred_element_type=jnp.float32)
    _, act_back = jax.vjp(jax.nn.silu, act)
    d_act = act_back(d_swish)[0]
    d_patch = jnp.einsum("gsd,gsp->dp", d_h, noisy.astype(jnp.float32), precision=HIGH)
    d_cond = jnp.dot(cond_in.astype(jnp.float32).T, d_local, precision=HIGH)
    d_table = jnp.dot(d_cvec.T, onehot.astype(jnp.float32), precision=HIGH)
    d_time = jnp.dot(d_cvec.T, swish.astype(jnp.float32), precision=HIGH)
    d_freq = jnp.dot(d_act.T, freqs.astype(jnp.float32), precision=HIGH)
    stem_parts = (
        lax.psum_scatter(d_patch, "fsdp", scatter_dimension=0, tiled=True),
        lax.psum_scatter(d_freq, "fsdp", scatter_dimension=0, tiled=True),
        lax.psum_scatter(d_time, "fsdp", scatter_dimension=0, tiled=True),
        lax.psum_scatter(d_table, "fsdp", scatter_dimension=0, tiled=True),
        lax.psum_scatter(d_cond, "fsdp", scatter_dimension=0, tiled=True),
        lax.psum_scatter(d_head, "fsdp", scatter_dimension=0, tiled=True),
    )
    stem_parts = lax.psum(
        (stem_parts[0], stem_parts[1], stem_parts[2], stem_parts[3], stem_parts[4], stem_parts[5]),
        "ctx",
    )
    layer_sq = sum((jnp.sum(g * g) for shard in layer_shards for g in shard))
    cond_sq = jnp.sum(stem_parts[4] * stem_parts[4])
    other_sq = sum((jnp.sum(stem_parts[k] * stem_parts[k]) for k in (0, 1, 2, 3, 5)))
    local_sq = (layer_sq + cond_sq + other_sq / lax.axis_size("tp")) / lax.axis_size("ctx")
    total_sq = lax.psum(local_sq, ("fsdp", "ctx", "tp"))
    grad_norm = jnp.sqrt(total_sq)
    clip = jnp.minimum(1.0, CLIP / (grad_norm + 1e-06))
    grads_all = (
        jnp.stack([s[0] for s in layer_shards]),
        jnp.stack([s[1] for s in layer_shards]),
        jnp.stack([s[2] for s in layer_shards]),
        stem_parts[0],
        stem_parts[1],
        stem_parts[2],
        stem_parts[3],
        stem_parts[4],
        stem_parts[5],
    )
    olds = (
        (attend_weight, attend_mean, attend_square),
        (hidden_weight, hidden_mean, hidden_square),
        (output_weight, output_mean, output_square),
        (patch_weight, patch_mean, patch_square),
        (freq_weight, freq_mean, freq_square),
        (time_weight, time_mean, time_square),
        (label_table, label_mean, label_square),
        (cond_weight, cond_mean, cond_square),
        (head_weight, head_mean, head_square),
    )
    updated = []
    for trio, grad in zip(olds, grads_all):
        updated.extend(adamw(trio[0], trio[1], trio[2], grad * clip))
    return (loss, grad_norm, *updated)


def solution(mesh):
    placed = (
        P("fsdp", "ctx", None),
        P("fsdp", "ctx", None),
        P("fsdp", "ctx", None),
        P("fsdp"),
        P("fsdp"),
        P(None, "fsdp", None, "tp"),
        P(None, "fsdp", None, "tp"),
        P(None, "fsdp", None, "tp"),
        P(None, "fsdp", None, "tp"),
        P(None, "fsdp", None, "tp"),
        P(None, "fsdp", None, "tp"),
        P(None, "fsdp", None, "tp"),
        P(None, "fsdp", None, "tp"),
        P(None, "fsdp", None, "tp"),
        P("fsdp", None),
        P("fsdp", None),
        P("fsdp", None),
        P("fsdp", None),
        P("fsdp", None),
        P("fsdp", None),
        P("fsdp", None),
        P("fsdp", None),
        P("fsdp", None),
        P("fsdp", None),
        P("fsdp", None),
        P("fsdp", None),
        P("fsdp", "tp"),
        P("fsdp", "tp"),
        P("fsdp", "tp"),
        P("fsdp", None),
        P("fsdp", None),
        P("fsdp", None),
    )
    return jax.shard_map(
        per_device,
        mesh=mesh,
        in_specs=placed,
        out_specs=(
            P(),
            P(),
            P(None, "fsdp", None, "tp"),
            P(None, "fsdp", None, "tp"),
            P(None, "fsdp", None, "tp"),
            P(None, "fsdp", None, "tp"),
            P(None, "fsdp", None, "tp"),
            P(None, "fsdp", None, "tp"),
            P(None, "fsdp", None, "tp"),
            P(None, "fsdp", None, "tp"),
            P(None, "fsdp", None, "tp"),
            P("fsdp", None),
            P("fsdp", None),
            P("fsdp", None),
            P("fsdp", None),
            P("fsdp", None),
            P("fsdp", None),
            P("fsdp", None),
            P("fsdp", None),
            P("fsdp", None),
            P("fsdp", None),
            P("fsdp", None),
            P("fsdp", None),
            P("fsdp", "tp"),
            P("fsdp", "tp"),
            P("fsdp", "tp"),
            P("fsdp", None),
            P("fsdp", None),
            P("fsdp", None),
        ),
        check_vma=False,
    )
```

profile of v0, /device:TPU:0, one launch (start us, length us, event | category | flops | bytes accessed | tf_op | source)
XLA Modules:
  0.0 3744.2 jit_solution(7233193188170873005)
XLA Ops:
  85.9 164.2 %all-gather.40.cloned.1.call-done = bf16[1024,6656]{1,0:T(8,128)(2,1)} async-done(((bf16[512,6656]{1,0:T(8,128)(2,1)}), bf16[1024,6656]{1,0:T(8,128)(2,1)}) %all-gather.40.cloned.1.call-update) | async-done | bytes 13631504 | tf_op jit(solution)/shard_map/all_gather | solution.py:274
  403.1 36.1 all-reduce.22.cloned.1.call-done
  512.4 38.4 %all-reduce.24.cloned.1.call-done = f32[2,64,1024]{2,1,0:T(8,128)} async-done(((f32[2,64,1024]{2,1,0:T(8,128)}), f32[2,64,1024]{2,1,0:T(8,128)}) %all-reduce.24.cloned.1.call-update) | async-done | bytes 524304 | tf_op jit(solution)/shard_map/psum | solution.py:66
  591.2 37.2 all-reduce.26.cloned.1.call-done
  703.3 36.4 all-reduce.28.cloned.1.call-done
  1017.2 38.4 %all-reduce.36.cloned.1.call-done = f32[2,64,1024]{2,1,0:T(8,128)} async-done(((f32[2,64,1024]{2,1,0:T(8,128)}), f32[2,64,1024]{2,1,0:T(8,128)}) %all-reduce.36.cloned.1.call-update) | async-done | bytes 524304 | tf_op jit(solution)/shard_map/psum | solution.py:70
  1168.7 38.4 %all-reduce.40.cloned.1.call-done = f32[2,64,1024]{2,1,0:T(8,128)} async-done(((f32[2,64,1024]{2,1,0:T(8,128)}), f32[2,64,1024]{2,1,0:T(8,128)}) %all-reduce.40.cloned.1.call-update) | async-done | bytes 524304 | tf_op jit(solution)/shard_map/psum | solution.py:70
  1319.1 38.4 %all-reduce.44.cloned.1.call-done = f32[2,64,1024]{2,1,0:T(8,128)} async-done(((f32[2,64,1024]{2,1,0:T(8,128)}), f32[2,64,1024]{2,1,0:T(8,128)}) %all-reduce.44.cloned.1.call-update) | async-done | bytes 524304 | tf_op jit(solution)/shard_map/psum | solution.py:70
  1469.7 38.4 %all-reduce.48.cloned.1.call-done = f32[2,64,1024]{2,1,0:T(8,128)} async-done(((f32[2,64,1024]{2,1,0:T(8,128)}), f32[2,64,1024]{2,1,0:T(8,128)}) %all-reduce.48.cloned.1.call-update) | async-done | bytes 524304 | tf_op jit(solution)/shard_map/psum | solution.py:70
  1748.1 45.7 %reduce-scatter.55.cloned.1.call-done = f32[512,3,256]{2,0,1:T(8,128)} async-done(((f32[1024,3,256]{2,0,1:T(8,128)}), f32[512,3,256]{2,0,1:T(8,128)}) %reduce-scatter.55.cloned.1.call-update) | async-done | bytes 1572880 | tf_op jit(solution)/shard_map/reduce_scatter | solution.py:83
  1793.8 57.1 %reduce-scatter.57.cloned.1.call-done = f32[512,4,256]{2,0,1:T(8,128)} async-done(((f32[1024,4,256]{2,0,1:T(8,128)}), f32[512,4,256]{2,0,1:T(8,128)}) %reduce-scatter.57.cloned.1.call-update) | async-done | bytes 2097168 | tf_op jit(solution)/shard_map/reduce_scatter | solution.py:84
  1850.8 46.1 %reduce-scatter.49.cloned.1.call-done = f32[512,3,256]{2,0,1:T(8,128)} async-done(((f32[1024,3,256]{2,0,1:T(8,128)}), f32[512,3,256]{2,0,1:T(8,128)}) %reduce-scatter.49.cloned.1.call-update) | async-done | bytes 1572880 | tf_op jit(solution)/shard_map/reduce_scatter | solution.py:83
  1897.0 68.4 %reduce-scatter.65.cloned.1.call-done = f32[512,5,256]{2,0,1:T(8,128)} async-done(((f32[1024,5,256]{2,0,1:T(8,128)}), f32[512,5,256]{2,0,1:T(8,128)}) %reduce-scatter.65.cloned.1.call-update) | async-done | bytes 2621456 | tf_op jit(solution)/shard_map/reduce_scatter | solution.py:85
  1965.4 57.2 %reduce-scatter.51.cloned.1.call-done = f32[512,4,256]{2,0,1:T(8,128)} async-done(((f32[1024,4,256]{2,0,1:T(8,128)}), f32[512,4,256]{2,0,1:T(8,128)}) %reduce-scatter.51.cloned.1.call-update) | async-done | bytes 2097168 | tf_op jit(solution)/shard_map/reduce_scatter | solution.py:84
  2022.6 46.1 %reduce-scatter.43.cloned.1.call-done = f32[512,3,256]{2,0,1:T(8,128)} async-done(((f32[1024,3,256]{2,0,1:T(8,128)}), f32[512,3,256]{2,0,1:T(8,128)}) %reduce-scatter.43.cloned.1.call-update) | async-done | bytes 1572880 | tf_op jit(solution)/shard_map/reduce_scatter | solution.py:83
  2068.6 68.7 %reduce-scatter.59.cloned.1.call-done = f32[512,5,256]{2,0,1:T(8,128)} async-done(((f32[1024,5,256]{2,0,1:T(8,128)}), f32[512,5,256]{2,0,1:T(8,128)}) %reduce-scatter.59.cloned.1.call-update) | async-done | bytes 2621456 | tf_op jit(solution)/shard_map/reduce_scatter | solution.py:85
  2137.3 57.1 %reduce-scatter.45.cloned.1.call-done = f32[512,4,256]{2,0,1:T(8,128)} async-done(((f32[1024,4,256]{2,0,1:T(8,128)}), f32[512,4,256]{2,0,1:T(8,128)}) %reduce-scatter.45.cloned.1.call-update) | async-done | bytes 2097168 | tf_op jit(solution)/shard_map/reduce_scatter | solution.py:84
  2194.4 68.7 %reduce-scatter.53.cloned.1.call-done = f32[512,5,256]{2,0,1:T(8,128)} async-done(((f32[1024,5,256]{2,0,1:T(8,128)}), f32[512,5,256]{2,0,1:T(8,128)}) %reduce-scatter.53.cloned.1.call-update) | async-done | bytes 2621456 | tf_op jit(solution)/shard_map/reduce_scatter | solution.py:85
  2263.1 56.4 %reduce-scatter.75.cloned.1.call-done = f32[512,1001]{0,1:T(8,128)} async-done(((f32[1024,1001]{0,1:T(8,128)}), f32[512,1001]{0,1:T(8,128)}) %reduce-scatter.75.cloned.1.call-update) | async-done | bytes 2050064 | tf_op jit(solution)/shard_map/reduce_scatter | solution.py:348
  2319.4 57.2 %reduce-scatter.73.cloned.1.call-done = f32[512,1024]{1,0:T(8,128)} async-done(((f32[1024,1024]{1,0:T(8,128)}), f32[512,1024]{1,0:T(8,128)}) %reduce-scatter.73.cloned.1.call-update) | async-done | bytes 2097168 | tf_op jit(solution)/shard_map/reduce_scatter | solution.py:347
  2376.7 68.7 %reduce-scatter.47.cloned.1.call-done = f32[512,5,256]{2,0,1:T(8,128)} async-done(((f32[1024,5,256]{2,0,1:T(8,128)}), f32[512,5,256]{2,0,1:T(8,128)}) %reduce-scatter.47.cloned.1.call-update) | async-done | bytes 2621456 | tf_op jit(solution)/shard_map/reduce_scatter | solution.py:85
  2445.4 304.2 %reduce-scatter.67.cloned.1.call-done = f32[512,6656]{1,0:T(8,128)} async-done(((f32[1024,6656]{1,0:T(8,128)}), f32[512,6656]{1,0:T(8,128)}) %reduce-scatter.67.cloned.1.call-update) | async-done | bytes 13631504 | tf_op jit(solution)/shard_map/reduce_scatter | solution.py:349
  2774.1 729.0 %all-reduce.52.cloned.1.call-done = (f32[512,3,256]{2,0,1:T(8,128)}, f32[512,4,256]{2,0,1:T(8,128)}, f32[512,5,256]{2,0,1:T(8,128)}, f32[512,3,256]{2,0,1:T(8,12...) async-done(((f32[512,3,256]{2,0,1:T(8,128)}, ...) | async-done | bytes 43534352 | tf_op jit(solution)/shard_map/psum | solution.py:87
  3550.3 39.4 %all-reduce = (f32[]{:T(128)}, f32[]{:T(128)}) all-reduce(f32[]{:T(128)S(6)} %div.414, f32[]{:T(128)S(6)} %div.443), channel_id=1, replica_groups=mesh['fsdp'=2,'ctx'=4,'tp'=4] {'fsdp','ctx','tp'}, use_global_device_ids=true, to_apply=%region_35.36 | all-reduce | flops 2 | bytes 16 | tf_op jit(solution)/shard_map/psum | solution.py:313
  (984 shorter events, 1477.0 us)
Async XLA Ops:
  11.3 238.7 %all-gather.40.cloned.1.call-start = ((), (), s32[]{:S(2)}) async-start(), calls=%async_computation.28 | async-start | bytes 20447232 | tf_op jit(solution)/shard_map/all_gather | solution.py:274
  19.9 259.4 %all-gather.42.cloned.1.call-start = ((), (), s32[]{:S(2)}) async-start(), calls=%async_computation.71 | async-start | bytes 2359296 | tf_op jit(solution)/shard_map/all_gather | solution.py:75
  25.3 295.0 %all-gather.44.cloned.1.call-start = ((), (), s32[]{:S(2)}) async-start(), calls=%async_computation.72 | async-start | bytes 3932160 | tf_op jit(solution)/shard_map/all_gather | solution.py:77
  32.5 328.9 %all-reduce.20.cloned.1.call-start = ((), (), s32[]{:S(2)}) async-start(), calls=%async_computation.29 | async-start | bytes 1048576 | tf_op jit(solution)/shard_map/psum | solution.py:66
  402.0 148.8 %all-reduce.24.cloned.1.call-start = ((), (), s32[]{:S(2)}) async-start(), calls=%async_computation.31 | async-start | bytes 1048576 | tf_op jit(solution)/shard_map/psum | solution.py:66
  591.1 148.6 %all-reduce.28.cloned.1.call-start = ((), (), s32[]{:S(2)}) async-start(), calls=%async_computation.33 | async-start | bytes 1048576 | tf_op jit(solution)/shard_map/psum | solution.py:66
  780.9 148.8 %all-reduce.32.cloned.1.call-start = ((), (), s32[]{:S(2)}) async-start(), calls=%async_computation.35 | async-start | bytes 1048576 | tf_op jit(solution)/shard_map/psum | solution.py:66
  1571.2 148.2 %reduce-scatter.77.cloned.1.call-start = ((), (), s32[]{:S(2)}) async-start(), calls=%async_computation.70 | async-start | bytes 196608 | tf_op jit(solution)/shard_map/reduce_scatter | solution.py:350
  1576.8 148.2 %reduce-scatter.63.cloned.1.call-start = ((), (), s32[]{:S(2)}) async-start(), calls=%async_computation.62 | async-start | bytes 6291456 | tf_op jit(solution)/shard_map/reduce_scatter | solution.py:84
  1581.5 166.5 %reduce-scatter.71.cloned.1.call-start = ((), (), s32[]{:S(2)}) async-start(), calls=%async_computation.67 | async-start | bytes 1572864 | tf_op jit(solution)/shard_map/reduce_scatter | solution.py:346
  1653.5 197.4 %reduce-scatter.57.cloned.1.call-start = ((), (), s32[]{:S(2)}) async-start(), calls=%async_computation.59 | async-start | bytes 6291456 | tf_op jit(solution)/shard_map/reduce_scatter | solution.py:84
  1657.1 239.9 %reduce-scatter.49.cloned.1.call-start = ((), (), s32[]{:S(2)}) async-start(), calls=%async_computation.55 | async-start | bytes 4718592 | tf_op jit(solution)/shard_map/reduce_scatter | solution.py:83
  1660.3 305.1 %reduce-scatter.65.cloned.1.call-start = ((), (), s32[]{:S(2)}) async-start(), calls=%async_computation.63 | async-start | bytes 7864320 | tf_op jit(solution)/shard_map/reduce_scatter | solution.py:85
  1665.4 357.1 %reduce-scatter.51.cloned.1.call-start = ((), (), s32[]{:S(2)}) async-start(), calls=%async_computation.56 | async-start | bytes 6291456 | tf_op jit(solution)/shard_map/reduce_scatter | solution.py:84
  1669.3 399.4 %reduce-scatter.43.cloned.1.call-start = ((), (), s32[]{:S(2)}) async-start(), calls=%async_computation.52 | async-start | bytes 4718592 | tf_op jit(solution)/shard_map/reduce_scatter | solution.py:83
  1672.5 464.9 %reduce-scatter.59.cloned.1.call-start = ((), (), s32[]{:S(2)}) async-start(), calls=%async_computation.60 | async-start | bytes 7864320 | tf_op jit(solution)/shard_map/reduce_scatter | solution.py:85
  1677.7 516.7 %reduce-scatter.45.cloned.1.call-start = ((), (), s32[]{:S(2)}) async-start(), calls=%async_computation.53 | async-start | bytes 6291456 | tf_op jit(solution)/shard_map/reduce_scatter | solution.py:84
  1681.4 581.6 %reduce-scatter.53.cloned.1.call-start = ((), (), s32[]{:S(2)}) async-start(), calls=%async_computation.57 | async-start | bytes 7864320 | tf_op jit(solution)/shard_map/reduce_scatter | solution.py:85
  1687.0 632.5 %reduce-scatter.75.cloned.1.call-start = ((), (), s32[]{:S(2)}) async-start(), calls=%async_computation.69 | async-start | bytes 6193152 | tf_op jit(solution)/shard_map/reduce_scatter | solution.py:348
  1691.6 685.1 %reduce-scatter.73.cloned.1.call-start = ((), (), s32[]{:S(2)}) async-start(), calls=%async_computation.68 | async-start | bytes 6291456 | tf_op jit(solution)/shard_map/reduce_scatter | solution.py:347
  1696.2 749.2 %reduce-scatter.47.cloned.1.call-start = ((), (), s32[]{:S(2)}) async-start(), calls=%async_computation.54 | async-start | bytes 7864320 | tf_op jit(solution)/shard_map/reduce_scatter | solution.py:85
  1701.8 1047.8 %reduce-scatter.67.cloned.1.call-start = ((), (), s32[]{:S(2)}) async-start(), calls=%async_computation.65 | async-start | bytes 40894464 | tf_op jit(solution)/shard_map/reduce_scatter | solution.py:349
  1717.1 1045.1 %reduce-scatter.69.cloned.1.call-start = ((), (), s32[]{:S(2)}) async-start(), calls=%async_computation.66 | async-start | bytes 98304 | tf_op jit(solution)/shard_map/reduce_scatter | solution.py:345
  1719.3 1783.8 %all-reduce.52.cloned.1.call-start = ((), (), s32[]{:S(2)}) async-start(), calls=%async_computation.83 | async-start | bytes 87097344 | tf_op jit(solution)/shard_map/psum | solution.py:87
  (283 other events, 7865.3 us)
Sparse Core Ops, SparseCore 0:
  10.3 39.2 all-gather.35
  86.0 164.0 all-gather.39
  281.2 39.0 all-gather.43
  470.5 39.0 all-gather.49
  659.5 39.0 all-gather.55
  849.3 39.0 all-gather.61
  891.3 38.2 all-reduce.31
  969.9 38.3 all-reduce.33
  1624.3 43.3 reduce-scatter.60
  1670.7 54.2 reduce-scatter.62
  1750.4 43.3 reduce-scatter.54
  1796.5 54.3 reduce-scatter.56
  1853.6 43.3 reduce-scatter.48
  1899.7 65.6 reduce-scatter.64
  1968.2 54.3 reduce-scatter.50
  2025.3 43.3 reduce-scatter.42
  2071.6 65.6 reduce-scatter.58
  2140.0 54.3 reduce-scatter.44
  2197.4 65.6 reduce-scatter.52
  2265.8 53.5 reduce-scatter.74
  2322.3 54.3 reduce-scatter.72
  2379.6 65.6 reduce-scatter.46
  2447.7 301.8 reduce-scatter.66
  2766.5 736.4 all-reduce.51
  (34 shorter events, 1008.0 us)
where the time goes:
time: 3760 us; the launch traced here: 3740 us
  waiting for transfers between devices  2960 us (79%)
  other arithmetic  247 us (7%)
  matrix products  187 us (5%)
  local copies, waits for them, and re-layouts  167 us (4%)
  blocking collectives  148 us (4%)
    psum x1, waiting for transfers between devices, reduce_layer(): return lax.psum((shards[0], shards[1], shards[2]), 'ctx')  729 us
    reduce_scatter x1, waiting for transfers between devices, per_device(): lax.psum_scatter(d_cond, 'fsdp', scatter_dimension=0, tiled=True)  304 us
    reduce_scatter x4, waiting for transfers between devices, reduce_layer(): lax.psum_scatter(d_output, 'fsdp', scatter_dimension=0, tiled=True)  274 us
    psum x8, waiting for transfers between devices, tp_total(): return lax.psum(part, 'tp')  272 us
    psum x8, waiting for transfers between devices, tp_back(): return lax.psum(part, 'tp')  270 us
    reduce_scatter x4, waiting for transfers between devices, reduce_layer(): lax.psum_scatter(d_hidden, 'fsdp', scatter_dimension=0, tiled=True)  177 us
    all_gather x1, waiting for transfers between devices, per_device(): lax.all_gather(cond_weight.astype(jnp.bfloat16), 'fsdp', axis=0, tiled=True)  164 us
    reduce_scatter x4, waiting for transfers between devices, reduce_layer(): lax.psum_scatter(d_attend, 'fsdp', scatter_dimension=0, tiled=True)  138 us
  transfers between devices with their start and end apart: 58, of which 55 were waited for; matrix products, arithmetic and copies ran while one was open for 7% of the time, Pallas kernels for 0%

commit v1 on v0

v1 whole, which is shorter than its diff:
```python
import math

import jax
import jax.numpy as jnp
from jax import lax
from jax.sharding import PartitionSpec as P

HEAD_DIM = 64
FREQ = 256
GRID = 16
STEP = 5


HIGH = lax.Precision.HIGHEST
RATE = 0.05
DECAY = 0.1
BETA = 0.5
EPSILON = 1e-08
CLIP = 1.0
LOW = jnp.bfloat16


def modln(h, shift, scale):
    mean = jnp.mean(h, -1, keepdims=True)
    cent = h - mean
    var = jnp.mean(cent * cent, -1, keepdims=True)
    return cent * lax.rsqrt(var + 1e-06) * (1.0 + scale) + shift


def gelu_tanh(v):
    return jax.nn.gelu(v, approximate=True)


def noise_level(steps):
    phase = (steps.astype(jnp.float32) / 1000.0 + 0.008) / 1.008 * (0.5 * math.pi)
    return jnp.cos(phase) ** 2


def time_freqs(steps):
    half = FREQ // 2
    rates = jnp.exp(-math.log(10000.0) * jnp.arange(half, dtype=jnp.float32) / half)
    angles = steps.astype(jnp.float32)[:, None] * rates[None, :]
    return jnp.concatenate([jnp.cos(angles), jnp.sin(angles)], -1)


def positions(first, count, width):
    index = first + jnp.arange(count, dtype=jnp.int32)
    row = (index // GRID).astype(jnp.float32)
    column = (index % GRID).astype(jnp.float32)
    quarter = width // 4
    rates = jnp.power(10000.0, -jnp.arange(quarter, dtype=jnp.float32) / quarter)
    across = column[:, None] * rates[None, :]
    down = row[:, None] * rates[None, :]
    return jnp.concatenate([jnp.sin(across), jnp.cos(across), jnp.sin(down), jnp.cos(down)], -1)


def adamw(weight, mean, square, grad):
    mean_next = BETA * mean + (1.0 - BETA) * grad
    square_next = BETA * square + (1.0 - BETA) * grad * grad
    fixed_mean = mean_next / (1.0 - BETA**STEP)
    fixed_square = square_next / (1.0 - BETA**STEP)
    weight_next = weight - RATE * (fixed_mean / (jnp.sqrt(fixed_square) + EPSILON) + DECAY * weight)
    return [weight_next, mean_next, square_next]


def rank_sum(left, right):
    total = left[0][:, None] * right[0][None, :]
    for k in range(1, left.shape[0]):
        total = total + left[k][:, None] * right[k][None, :]
    return total


def rank_square(left, right):
    one = jnp.einsum("nd,md->nm", left, left, precision=HIGH)
    two = jnp.einsum("nd,md->nm", right, right, precision=HIGH)
    return jnp.sum(one * two)


def tp_total(part):
    return lax.psum(part.astype(LOW), "tp").astype(jnp.float32)


def gather_layer(attend, hidden, output):
    return (
        lax.all_gather(attend.astype(LOW), "fsdp", axis=0, tiled=True),
        lax.all_gather(hidden.astype(LOW), "fsdp", axis=0, tiled=True),
        lax.all_gather(output.astype(LOW), "fsdp", axis=0, tiled=True),
    )


def reduce_layer(grads):
    shards = [
        lax.psum_scatter(g.astype(LOW), "fsdp", scatter_dimension=0, tiled=True) for g in grads
    ]
    return [lax.psum(s, "ctx").astype(jnp.float32) for s in shards]


def layer_forward(h, mods, weights):
    attend, hidden, output = weights
    count, rows, width = h.shape
    local = attend.shape[2]
    heads = local // HEAD_DIM
    scale = 1.0 / math.sqrt(HEAD_DIM)
    u_in = modln(h, mods[:, 0, None], mods[:, 1, None]).astype(LOW)
    qkv = jnp.einsum("gsd,dke->gske", u_in, attend, preferred_element_type=jnp.float32).astype(LOW)
    both = lax.all_gather(qkv[:, :, 1:], "ctx", axis=1, tiled=True)
    query = qkv[:, :, 0].reshape(count, rows, heads, HEAD_DIM)
    keys = both[:, :, 0].reshape(count, -1, heads, HEAD_DIM)
    values = both[:, :, 1].reshape(count, -1, heads, HEAD_DIM)
    scores = jnp.einsum("gqhe,gkhe->ghqk", query, keys, preferred_element_type=jnp.float32) * scale
    top = jnp.max(scores, -1, keepdims=True)
    expo = jnp.exp(scores - top)
    probs = expo / jnp.sum(expo, -1, keepdims=True)
    probs_low = probs.astype(LOW)
    attended = (
        jnp.einsum("ghqk,gkhe->gqhe", probs_low, values, preferred_element_type=jnp.float32)
        .astype(LOW)
        .reshape(count, rows, local)
    )
    branch_a = tp_total(
        jnp.einsum("gsc,dc->gsd", attended, output[:, 0], preferred_element_type=jnp.float32)
    )
    h_mid = h + mods[:, 2, None] * branch_a
    w_in = modln(h_mid, mods[:, 3, None], mods[:, 4, None]).astype(LOW)
    pre = jnp.einsum("gsd,dkc->gskc", w_in, hidden, preferred_element_type=jnp.float32).reshape(
        count, rows, 4 * local
    )
    act = gelu_tanh(pre).astype(LOW)
    out_mlp = output[:, 1:].reshape(width, 4 * local)
    branch_m = tp_total(jnp.einsum("gsk,dk->gsd", act, out_mlp, preferred_element_type=jnp.float32))
    h_out = h_mid + mods[:, 5, None] * branch_m
    kept = (h, u_in, query, keys, values, probs, probs_low, attended, branch_a, h_mid, w_in, pre)
    return h_out, kept + (act, out_mlp, branch_m)


def layer_backward(kept, mods, weights, grad_out):
    attend, hidden, output = weights
    (h, u_in, query, keys, values, probs, probs_low, attended, branch_a, h_mid, w_in, pre) = kept[:12]
    act, out_mlp, branch_m = kept[12:]
    count, rows, width = h.shape
    local = attend.shape[2]
    scale = 1.0 / math.sqrt(HEAD_DIM)
    d_gate_m = jnp.sum(grad_out * branch_m, 1)
    d_branch = (mods[:, 5, None] * grad_out).astype(LOW)
    d_act = jnp.einsum("gsd,dk->gsk", d_branch, out_mlp, preferred_element_type=jnp.float32)
    d_out_mlp = jnp.einsum("gsd,gsk->dk", d_branch, act, preferred_element_type=jnp.float32)
    _, gelu_back = jax.vjp(gelu_tanh, pre)
    d_pre = gelu_back(d_act)[0].astype(LOW).reshape(count, rows, 4, local)
    d_hidden = jnp.einsum("gsd,gskc->dkc", w_in, d_pre, preferred_element_type=jnp.float32)
    d_w = tp_total(jnp.einsum("gskc,dkc->gsd", d_pre, hidden, preferred_element_type=jnp.float32))
    _, norm_back = jax.vjp(modln, h_mid, mods[:, 3, None], mods[:, 4, None])
    d_mid, d_shift_m, d_scale_m = norm_back(d_w)
    d_mid = d_mid + grad_out
    d_gate_a = jnp.sum(d_mid * branch_a, 1)
    d_branch_a = (mods[:, 2, None] * d_mid).astype(LOW)
    d_att = jnp.einsum(
        "gsd,dc->gsc", d_branch_a, output[:, 0], preferred_element_type=jnp.float32
    ).astype(LOW)
    d_out_att = jnp.einsum("gsd,gsc->dc", d_branch_a, attended, preferred_element_type=jnp.float32)
    d_att = d_att.reshape(count, rows, -1, HEAD_DIM)
    d_probs = jnp.einsum("gqhe,gkhe->ghqk", d_att, values, preferred_element_type=jnp.float32)
    d_values = jnp.einsum("ghqk,gqhe->gkhe", probs_low, d_att, preferred_element_type=jnp.float32)
    d_scores = (probs * (d_probs - jnp.sum(d_probs * probs, -1, keepdims=True))).astype(LOW)
    d_query = (
        jnp.einsum("ghqk,gkhe->gqhe", d_scores, keys, preferred_element_type=jnp.float32) * scale
    ).astype(LOW)
    d_keys = (
        jnp.einsum("ghqk,gqhe->gkhe", d_scores, query, preferred_element_type=jnp.float32) * scale
    )
    d_both = lax.psum_scatter(
        jnp.stack(
            [d_keys.reshape(count, -1, local), d_values.reshape(count, -1, local)], 2
        ).astype(LOW),
        "ctx",
        scatter_dimension=1,
        tiled=True,
    )
    d_qkv = jnp.concatenate([d_query.reshape(count, rows, 1, local), d_both], 2)
    d_attend = jnp.einsum("gsd,gske->dke", u_in, d_qkv, preferred_element_type=jnp.float32)
    d_u = tp_total(jnp.einsum("gske,dke->gsd", d_qkv, attend, preferred_element_type=jnp.float32))
    _, norm_back = jax.vjp(modln, h, mods[:, 0, None], mods[:, 1, None])
    d_h, d_shift_a, d_scale_a = norm_back(d_u)
    d_mods = jnp.stack(
        [d_shift_a[:, 0], d_scale_a[:, 0], d_gate_a, d_shift_m[:, 0], d_scale_m[:, 0], d_gate_m], 1
    )
    d_output = jnp.concatenate([d_out_att[:, None], d_out_mlp.reshape(width, 4, local)], 1)
    return (d_h + d_mid, d_mods, (d_attend, d_hidden, d_output))


def per_device(
    latents,
    noise,
    var_target,
    timesteps,
    labels,
    attend_weight,
    attend_mean,
    attend_square,
    hidden_weight,
    hidden_mean,
    hidden_square,
    output_weight,
    output_mean,
    output_square,
    patch_weight,
    patch_mean,
    patch_square,
    freq_weight,
    freq_mean,
    freq_square,
    time_weight,
    time_mean,
    time_square,
    label_table,
    label_mean,
    label_square,
    cond_weight,
    cond_mean,
    cond_square,
    head_weight,
    head_mean,
    head_square,
):
    count, rows, patch_in = latents.shape
    layers, shard = attend_weight.shape[:2]
    columns = cond_weight.shape[1]

    steps_all = lax.all_gather(timesteps, "fsdp", axis=0, tiled=True)
    labels_all = lax.all_gather(labels, "fsdp", axis=0, tiled=True)
    freqs = time_freqs(steps_all).astype(LOW)
    act = jnp.dot(freqs, freq_weight.astype(LOW).T, preferred_element_type=jnp.float32)
    swish = lax.all_gather(jax.nn.silu(act).astype(LOW), "fsdp", axis=1, tiled=True)
    time_low = time_weight.astype(LOW)
    temb = jnp.dot(swish, time_low.T, preferred_element_type=jnp.float32)
    onehot = (labels_all[:, None] == jnp.arange(label_table.shape[1], dtype=jnp.int32)[None]).astype(
        LOW
    )
    cvec = temb + jnp.dot(onehot, label_table.astype(LOW).T, preferred_element_type=jnp.float32)
    cond_in = jax.nn.silu(cvec).astype(LOW)
    cond_low = cond_weight.astype(LOW)
    mods = lax.psum_scatter(
        jnp.dot(cond_in, cond_low, preferred_element_type=jnp.float32),
        "fsdp",
        scatter_dimension=0,
        tiled=True,
    )
    patch_head = lax.all_gather(
        jnp.concatenate([patch_weight, head_weight], 1).astype(LOW), "fsdp", axis=0, tiled=True
    )
    patch_full, head_full = patch_head[:, :patch_in], patch_head[:, patch_in:]
    width = patch_full.shape[0]
    mods = lax.all_gather(mods, "tp", axis=1, tiled=True).reshape(count, -1, width)

    level = noise_level(timesteps)[:, None, None]
    noisy = (jnp.sqrt(level) * latents + jnp.sqrt(1.0 - level) * noise).astype(LOW)
    first = lax.axis_index("ctx") * rows
    h = (
        jnp.einsum("gsp,dp->gsd", noisy, patch_full, preferred_element_type=jnp.float32)
        + positions(first, rows, width)[None]
    )
    kept = []
    weights = []
    for layer in range(layers):
        weights.append(
            gather_layer(attend_weight[layer], hidden_weight[layer], output_weight[layer])
        )
        h, saved = layer_forward(h, mods[:, 6 * layer : 6 * layer + 6], weights[layer])
        kept.append(saved)
    final_in = modln(h, mods[:, 6 * layers, None], mods[:, 6 * layers + 1, None]).astype(LOW)
    pred = jnp.einsum("gsd,dp->gsp", final_in, head_full, preferred_element_type=jnp.float32)
    diff = pred - jnp.concatenate([noise, var_target], -1)
    loss = lax.psum(jnp.sum(diff * diff), ("fsdp", "ctx"))
    d_pred = (2.0 * diff).astype(LOW)
    d_head = jnp.einsum("gsd,gsp->dp", final_in, d_pred, preferred_element_type=jnp.float32)
    d_final = jnp.einsum("gsp,dp->gsd", d_pred, head_full, preferred_element_type=jnp.float32)
    _, norm_back = jax.vjp(modln, h, mods[:, 6 * layers, None], mods[:, 6 * layers + 1, None])
    d_h, d_shift_f, d_scale_f = norm_back(d_final)
    mod_grads = [None] * layers
    layer_shards = [None] * layers
    for layer in reversed(range(layers)):
        d_h, mod_grads[layer], grads = layer_backward(
            kept[layer], mods[:, 6 * layer : 6 * layer + 6], weights[layer], d_h
        )
        layer_shards[layer] = reduce_layer(grads)

    d_mods = jnp.concatenate(mod_grads + [d_shift_f, d_scale_f], 1).reshape(count, -1)
    d_cols = lax.dynamic_slice_in_dim(d_mods, lax.axis_index("tp") * columns, columns, 1)
    d_cols = lax.all_gather(lax.psum(d_cols, "ctx"), "fsdp", axis=0, tiled=True)
    d_silu = lax.psum(
        jnp.dot(d_cols, cond_low.astype(jnp.float32).T, precision=HIGH), "tp"
    )
    _, silu_back = jax.vjp(jax.nn.silu, cvec)
    d_cvec = silu_back(d_silu)[0]
    d_swish = lax.psum_scatter(
        jnp.dot(d_cvec, time_low.astype(jnp.float32), precision=HIGH),
        "fsdp",
        scatter_dimension=1,
        tiled=True,
    )
    _, act_back = jax.vjp(jax.nn.silu, act)
    d_act = act_back(d_swish)[0]
    d_patch = jnp.einsum("gsd,gsp->dp", d_h, noisy.astype(jnp.float32), precision=HIGH)
    d_small = lax.psum(
        lax.psum_scatter(
            jnp.concatenate([d_patch, d_head], 1), "fsdp", scatter_dimension=0, tiled=True
        ),
        "ctx",
    )
    lefts = {"freq": d_act, "time": d_cvec, "label": d_cvec, "cond": cond_in.astype(jnp.float32)}
    rights = {
        "freq": freqs.astype(jnp.float32),
        "time": swish.astype(jnp.float32),
        "label": onehot.astype(jnp.float32),
        "cond": d_cols,
    }

    split_sq = sum(jnp.sum(g * g) for parts in layer_shards for g in parts) + rank_square(
        lefts["cond"], rights["cond"]
    )
    copied_sq = jnp.sum(d_small * d_small) + sum(
        rank_square(lefts[k], rights[k]) for k in ("freq", "time", "label")
    )
    total_sq = lax.psum(split_sq + copied_sq / lax.axis_size("tp"), ("fsdp", "tp"))
    grad_norm = jnp.sqrt(total_sq)
    clip = jnp.minimum(1.0, CLIP / (grad_norm + 1e-06))
    grads_all = (
        jnp.stack([s[0] for s in layer_shards]),
        jnp.stack([s[1] for s in layer_shards]),
        jnp.stack([s[2] for s in layer_shards]),
        d_small[:, :patch_in],
        rank_sum(lefts["freq"], rights["freq"]),
        rank_sum(lefts["time"], rights["time"]),
        rank_sum(lefts["label"], rights["label"]),
        rank_sum(lefts["cond"], rights["cond"]),
        d_small[:, patch_in:],
    )
    olds = (
        (attend_weight, attend_mean, attend_square),
        (hidden_weight, hidden_mean, hidden_square),
        (output_weight, output_mean, output_square),
        (patch_weight, patch_mean, patch_square),
        (freq_weight, freq_mean, freq_square),
        (time_weight, time_mean, time_square),
        (label_table, label_mean, label_square),
        (cond_weight, cond_mean, cond_square),
        (head_weight, head_mean, head_square),
    )
    updated = []
    for trio, grad in zip(olds, grads_all):
        updated.extend(adamw(trio[0], trio[1], trio[2], grad * clip))
    return (loss, grad_norm, *updated)


def solution(mesh):
    image = P("fsdp", "ctx", None)
    layer = P(None, "fsdp", None, "tp")
    rows = P("fsdp", None)
    cond = P("fsdp", "tp")
    weights = (layer,) * 9 + (rows,) * 12 + (cond,) * 3 + (rows,) * 3
    return jax.shard_map(
        per_device,
        mesh=mesh,
        in_specs=(image, image, image, P("fsdp"), P("fsdp")) + weights,
        out_specs=(P(), P()) + weights,
        check_vma=False,
    )
```

time: 3760 us -> 2230 us (0.59)
  waiting for transfers between devices: 2960 us -> 1520 us
    reduce_scatter x26 -> x17, waiting for transfers between devices: 1190 us -> 420 us  [the longest x12 348 us: reduce_layer(): lax.psum_scatter(g.astype(LOW), 'fsdp', scatter_dimension=0, tiled=True)]
    psum x17 -> x18, waiting for transfers between devices: 1270 us -> 766 us  [the longest x16 510 us: tp_total(): return lax.psum(part.astype(LOW), 'tp').astype(jnp.float32)]
    all_gather x15 -> x12, waiting for transfers between devices: 498 us -> 330 us  [the longest x4 132 us: gather_layer(): lax.all_gather(hidden.astype(LOW), 'fsdp', axis=0, tiled=True)]
    dot_general x30 -> x32, matrix products: 88.9 us -> 58.6 us  [the longest x4 8.99 us: layer_forward(): jnp.einsum('gsd,dkc->gskc', w_in, hidden, preferred_element_type=jnp.floa...]
    all_gather x12 -> x8, blocking collectives: 86.6 us -> 58.2 us  [the longest x4 28.8 us: layer_forward(): both = lax.all_gather(qkv[:, :, 1:], 'ctx', axis=1, tiled=True)]
    unnamed x545 -> x557, local copies, waits for them, and re-layouts: 87.6 us -> 76.6 us
  transfers between devices with their start and end apart: 58 -> 49, of which waited for: 55 -> 44; matrix products, arithmetic and copies ran while one was open for 7% -> 8% of each run, Pallas kernels for 0% -> 0%
where the time goes in v1:
time: 2230 us; the launch traced here: 2220 us
  waiting for transfers between devices  1520 us (68%)
  other arithmetic  227 us (10%)
  local copies, waits for them, and re-layouts  160 us (7%)
  matrix products  154 us (7%)
  blocking collectives  119 us (5%)
  between operations  32.7 us (1%)
    psum x16, waiting for transfers between devices, tp_total(): return lax.psum(part.astype(LOW), 'tp').astype(jnp.float32)  510 us
    reduce_scatter x12, waiting for transfers between devices, reduce_layer(): lax.psum_scatter(g.astype(LOW), 'fsdp', scatter_dimension=0, tiled=True)  348 us
    psum x1, waiting for transfers between devices, reduce_layer(): return [lax.psum(s, 'ctx').astype(jnp.float32) for s in shards]  226 us
    all_gather x4, waiting for transfers between devices, gather_layer(): lax.all_gather(hidden.astype(LOW), 'fsdp', axis=0, tiled=True)  132 us
    all_gather x4, waiting for transfers between devices, gather_layer(): lax.all_gather(output.astype(LOW), 'fsdp', axis=0, tiled=True)  106 us
    sub x9, other arithmetic, adamw(): weight - RATE * (fixed_mean / (jnp.sqrt(fixed_square) + EPSILON) + DECAY...  104 us
    all_gather x4, waiting for transfers between devices, gather_layer(): lax.all_gather(attend.astype(LOW), 'fsdp', axis=0, tiled=True)  91.9 us
    unnamed x557, local copies, waits for them, and re-layouts  76.6 us
  transfers between devices with their start and end apart: 49, of which 44 were waited for; matrix products, arithmetic and copies ran while one was open for 8% of the time, Pallas kernels for 0%

profile of v1, /device:TPU:0, one launch (start us, length us, event | category | flops | bytes accessed | tf_op | source)
XLA Modules:
  0.0 2218.4 jit_solution(3936181986967281357)
XLA Ops:
  132.8 31.6 %all-reduce.25.cloned.1.call-done = bf16[2,64,1024]{2,1,0:T(8,128)(2,1)} async-done(((bf16[2,64,1024]{2,1,0:T(8,128)(2,1)}), bf16[2,64,1024]{2,1,0:T(8,128)(2,1)}) %all-reduce.25.cloned.1.call-update) | async-done | bytes 262160 | tf_op jit(solution)/shard_map/psum | solution.py:80
  165.7 33.6 %all-gather.30.cloned.1.call-done = bf16[1,1024,4,256]{3,1,2,0:T(8,128)(2,1)} async-done(((bf16[1,512,4,256]{3,1,2,0:T(8,128)(2,1)}), bf16[1,1024,4,256]{3,1,2,0:T(8,128)(2,1)}) %all-gather.30.cloned.1.call-update) | async-done | bytes 2097168 | tf_op jit(solution)/shard_map/all_gather | solution.py:86
  205.6 33.1 %all-reduce.27.cloned.1.call-done = bf16[2,64,1024]{2,1,0:T(8,128)(2,1)} async-done(((bf16[2,64,1024]{2,1,0:T(8,128)(2,1)}), bf16[2,64,1024]{2,1,0:T(8,128)(2,1)}) %all-reduce.27.cloned.1.call-update) | async-done | bytes 262160 | tf_op jit(solution)/shard_map/psum | solution.py:80
  311.8 35.5 %all-reduce.29.cloned.1.call-done = bf16[2,64,1024]{2,1,0:T(8,128)(2,1)} async-done(((bf16[2,64,1024]{2,1,0:T(8,128)(2,1)}), bf16[2,64,1024]{2,1,0:T(8,128)(2,1)}) %all-reduce.29.cloned.1.call-update) | async-done | bytes 262160 | tf_op jit(solution)/shard_map/psum | solution.py:80
  348.6 33.6 %all-gather.36.cloned.1.call-done = bf16[1,1024,4,256]{3,1,2,0:T(8,128)(2,1)} async-done(((bf16[1,512,4,256]{3,1,2,0:T(8,128)(2,1)}), bf16[1,1024,4,256]{3,1,2,0:T(8,128)(2,1)}) %all-gather.36.cloned.1.call-update) | async-done | bytes 2097168 | tf_op jit(solution)/shard_map/all_gather | solution.py:86
  387.5 34.0 %all-reduce.31.cloned.1.call-done = bf16[2,64,1024]{2,1,0:T(8,128)(2,1)} async-done(((bf16[2,64,1024]{2,1,0:T(8,128)(2,1)}), bf16[2,64,1024]{2,1,0:T(8,128)(2,1)}) %all-reduce.31.cloned.1.call-update) | async-done | bytes 262160 | tf_op jit(solution)/shard_map/psum | solution.py:80
  496.4 33.4 %all-reduce.33.cloned.1.call-done = bf16[2,64,1024]{2,1,0:T(8,128)(2,1)} async-done(((bf16[2,64,1024]{2,1,0:T(8,128)(2,1)}), bf16[2,64,1024]{2,1,0:T(8,128)(2,1)}) %all-reduce.33.cloned.1.call-update) | async-done | bytes 262160 | tf_op jit(solution)/shard_map/psum | solution.py:80
  531.7 33.0 %all-gather.42.cloned.1.call-done = bf16[1,1024,4,256]{3,1,2,0:T(8,128)(2,1)} async-done(((bf16[1,512,4,256]{3,1,2,0:T(8,128)(2,1)}), bf16[1,1024,4,256]{3,1,2,0:T(8,128)(2,1)}) %all-gather.42.cloned.1.call-update) | async-done | bytes 2097168 | tf_op jit(solution)/shard_map/all_gather | solution.py:86
  571.1 33.0 %all-reduce.35.cloned.1.call-done = bf16[2,64,1024]{2,1,0:T(8,128)(2,1)} async-done(((bf16[2,64,1024]{2,1,0:T(8,128)(2,1)}), bf16[2,64,1024]{2,1,0:T(8,128)(2,1)}) %all-reduce.35.cloned.1.call-update) | async-done | bytes 262160 | tf_op jit(solution)/shard_map/psum | solution.py:80
  679.5 32.9 %all-reduce.37.cloned.1.call-done = bf16[2,64,1024]{2,1,0:T(8,128)(2,1)} async-done(((bf16[2,64,1024]{2,1,0:T(8,128)(2,1)}), bf16[2,64,1024]{2,1,0:T(8,128)(2,1)}) %all-reduce.37.cloned.1.call-update) | async-done | bytes 262160 | tf_op jit(solution)/shard_map/psum | solution.py:80
  715.6 31.7 %all-gather.48.cloned.1.call-done = bf16[1,1024,4,256]{3,1,2,0:T(8,128)(2,1)} async-done(((bf16[1,512,4,256]{3,1,2,0:T(8,128)(2,1)}), bf16[1,1024,4,256]{3,1,2,0:T(8,128)(2,1)}) %all-gather.48.cloned.1.call-update) | async-done | bytes 2097168 | tf_op jit(solution)/shard_map/all_gather | solution.py:86
  795.6 35.2 %all-reduce.41.cloned.1.call-done = bf16[2,64,1024]{2,1,0:T(8,128)(2,1)} async-done(((bf16[2,64,1024]{2,1,0:T(8,128)(2,1)}), bf16[2,64,1024]{2,1,0:T(8,128)(2,1)}) %all-reduce.41.cloned.1.call-update) | async-done | bytes 262160 | tf_op jit(solution)/shard_map/psum | solution.py:80
  922.3 35.1 %all-reduce.45.cloned.1.call-done = bf16[2,64,1024]{2,1,0:T(8,128)(2,1)} async-done(((bf16[2,64,1024]{2,1,0:T(8,128)(2,1)}), bf16[2,64,1024]{2,1,0:T(8,128)(2,1)}) %all-reduce.45.cloned.1.call-update) | async-done | bytes 262160 | tf_op jit(solution)/shard_map/psum | solution.py:80
  1048.7 35.1 %all-reduce.49.cloned.1.call-done = bf16[2,64,1024]{2,1,0:T(8,128)(2,1)} async-done(((bf16[2,64,1024]{2,1,0:T(8,128)(2,1)}), bf16[2,64,1024]{2,1,0:T(8,128)(2,1)}) %all-reduce.49.cloned.1.call-update) | async-done | bytes 262160 | tf_op jit(solution)/shard_map/psum | solution.py:80
  1174.6 35.2 %all-reduce.53.cloned.1.call-done = bf16[2,64,1024]{2,1,0:T(8,128)(2,1)} async-done(((bf16[2,64,1024]{2,1,0:T(8,128)(2,1)}), bf16[2,64,1024]{2,1,0:T(8,128)(2,1)}) %all-reduce.53.cloned.1.call-update) | async-done | bytes 262160 | tf_op jit(solution)/shard_map/psum | solution.py:80
  1258.0 33.0 %all-reduce.55.cloned.1.call-done = bf16[2,64,1024]{2,1,0:T(8,128)(2,1)} async-done(((bf16[2,64,1024]{2,1,0:T(8,128)(2,1)}), bf16[2,64,1024]{2,1,0:T(8,128)(2,1)}) %all-reduce.55.cloned.1.call-update) | async-done | bytes 262160 | tf_op jit(solution)/shard_map/psum | solution.py:80
  1376.7 35.5 %reduce-scatter.51.cloned.1.call-done = bf16[512,5,256]{2,0,1:T(8,128)(2,1)} async-done(((bf16[1024,5,256]{2,0,1:T(8,128)(2,1)}), bf16[512,5,256]{2,0,1:T(8,128)(2,1)}) %reduce-scatter.51.cloned.1.call-update) | async-done | bytes 1310736 | tf_op jit(solution)/shard_map/reduce_scatter | solution.py:93
  1412.2 34.8 %reduce-scatter.43.cloned.1.call-done = bf16[512,4,256]{2,0,1:T(8,128)(2,1)} async-done(((bf16[1024,4,256]{2,0,1:T(8,128)(2,1)}), bf16[512,4,256]{2,0,1:T(8,128)(2,1)}) %reduce-scatter.43.cloned.1.call-update) | async-done | bytes 1048592 | tf_op jit(solution)/shard_map/reduce_scatter | solution.py:93
  1475.8 40.6 %reduce-scatter.45.cloned.1.call-done = bf16[512,5,256]{2,0,1:T(8,128)(2,1)} async-done(((bf16[1024,5,256]{2,0,1:T(8,128)(2,1)}), bf16[512,5,256]{2,0,1:T(8,128)(2,1)}) %reduce-scatter.45.cloned.1.call-update) | async-done | bytes 1310736 | tf_op jit(solution)/shard_map/reduce_scatter | solution.py:93
  1516.3 34.7 %reduce-scatter.37.cloned.1.call-done = bf16[512,4,256]{2,0,1:T(8,128)(2,1)} async-done(((bf16[1024,4,256]{2,0,1:T(8,128)(2,1)}), bf16[512,4,256]{2,0,1:T(8,128)(2,1)}) %reduce-scatter.37.cloned.1.call-update) | async-done | bytes 1048592 | tf_op jit(solution)/shard_map/reduce_scatter | solution.py:93
  1580.1 40.3 %reduce-scatter.39.cloned.1.call-done = bf16[512,5,256]{2,0,1:T(8,128)(2,1)} async-done(((bf16[1024,5,256]{2,0,1:T(8,128)(2,1)}), bf16[512,5,256]{2,0,1:T(8,128)(2,1)}) %reduce-scatter.39.cloned.1.call-update) | async-done | bytes 1310736 | tf_op jit(solution)/shard_map/reduce_scatter | solution.py:93
  1620.3 34.8 %reduce-scatter.31.cloned.1.call-done = bf16[512,4,256]{2,0,1:T(8,128)(2,1)} async-done(((bf16[1024,4,256]{2,0,1:T(8,128)(2,1)}), bf16[512,4,256]{2,0,1:T(8,128)(2,1)}) %reduce-scatter.31.cloned.1.call-update) | async-done | bytes 1048592 | tf_op jit(solution)/shard_map/reduce_scatter | solution.py:93
  1683.9 40.4 %reduce-scatter.33.cloned.1.call-done = bf16[512,5,256]{2,0,1:T(8,128)(2,1)} async-done(((bf16[1024,5,256]{2,0,1:T(8,128)(2,1)}), bf16[512,5,256]{2,0,1:T(8,128)(2,1)}) %reduce-scatter.33.cloned.1.call-update) | async-done | bytes 1310736 | tf_op jit(solution)/shard_map/reduce_scatter | solution.py:93
  1777.3 226.2 %all-reduce.61.cloned.1.call-done = (bf16[512,3,256]{2,0,1:T(8,128)(2,1)}, bf16[512,4,256]{2,0,1:T(8,128)(2,1)}, bf16[512,5,256]{2,0,1:T(8,128)(2,1)}, bf16[512,...) async-done(((bf16[512,3,256]{2,0,1:T(8,128)(2,1)}, ...) | async-done | bytes 12582928 | tf_op jit(solution)/shard_map/psum | solution.py:95
  (1024 shorter events, 1159.6 us)
Async XLA Ops:
  44.8 119.6 %all-reduce.25.cloned.1.call-start = ((), (), s32[]{:S(2)}) async-start(), calls=%async_computation.18 | async-start | bytes 524288 | tf_op jit(solution)/shard_map/psum | solution.py:80
  132.7 106.0 %all-reduce.27.cloned.1.call-start = ((), (), s32[]{:S(2)}) async-start(), calls=%async_computation.19 | async-start | bytes 524288 | tf_op jit(solution)/shard_map/psum | solution.py:80
  204.0 105.0 %all-gather.34.cloned.1.call-start = ((), (), s32[]{:S(2)}) async-start(), calls=%async_computation.56 | async-start | bytes 3932160 | tf_op jit(solution)/shard_map/all_gather | solution.py:87
  204.8 142.5 %all-reduce.29.cloned.1.call-start = ((), (), s32[]{:S(2)}) async-start(), calls=%async_computation.20 | async-start | bytes 524288 | tf_op jit(solution)/shard_map/psum | solution.py:80
  311.7 109.9 %all-reduce.31.cloned.1.call-start = ((), (), s32[]{:S(2)}) async-start(), calls=%async_computation.21 | async-start | bytes 524288 | tf_op jit(solution)/shard_map/psum | solution.py:80
  386.7 105.0 %all-gather.40.cloned.1.call-start = ((), (), s32[]{:S(2)}) async-start(), calls=%async_computation.59 | async-start | bytes 3932160 | tf_op jit(solution)/shard_map/all_gather | solution.py:87
  387.4 142.4 %all-reduce.33.cloned.1.call-start = ((), (), s32[]{:S(2)}) async-start(), calls=%async_computation.22 | async-start | bytes 524288 | tf_op jit(solution)/shard_map/psum | solution.py:80
  494.4 109.8 %all-reduce.35.cloned.1.call-start = ((), (), s32[]{:S(2)}) async-start(), calls=%async_computation.23 | async-start | bytes 524288 | tf_op jit(solution)/shard_map/psum | solution.py:80
  569.9 142.5 %all-reduce.37.cloned.1.call-start = ((), (), s32[]{:S(2)}) async-start(), calls=%async_computation.24 | async-start | bytes 524288 | tf_op jit(solution)/shard_map/psum | solution.py:80
  676.8 110.6 %all-reduce.39.cloned.1.call-start = ((), (), s32[]{:S(2)}) async-start(), calls=%async_computation.25 | async-start | bytes 524288 | tf_op jit(solution)/shard_map/psum | solution.py:80
  1255.5 120.6 %reduce-scatter.53.cloned.1.call-start = ((), (), s32[]{:S(2)}) async-start(), calls=%async_computation.50 | async-start | bytes 294912 | tf_op jit(solution)/shard_map/reduce_scatter | solution.py:304
  1303.6 108.6 %reduce-scatter.51.cloned.1.call-start = ((), (), s32[]{:S(2)}) async-start(), calls=%async_computation.48 | async-start | bytes 3932160 | tf_op jit(solution)/shard_map/reduce_scatter | solution.py:93
  1309.0 138.0 %reduce-scatter.43.cloned.1.call-start = ((), (), s32[]{:S(2)}) async-start(), calls=%async_computation.44 | async-start | bytes 3145728 | tf_op jit(solution)/shard_map/reduce_scatter | solution.py:93
  1312.1 163.7 %reduce-scatter.41.cloned.1.call-start = ((), (), s32[]{:S(2)}) async-start(), calls=%async_computation.43 | async-start | bytes 2359296 | tf_op jit(solution)/shard_map/reduce_scatter | solution.py:93
  1314.8 201.5 %reduce-scatter.45.cloned.1.call-start = ((), (), s32[]{:S(2)}) async-start(), calls=%async_computation.45 | async-start | bytes 3932160 | tf_op jit(solution)/shard_map/reduce_scatter | solution.py:93
  1320.3 230.7 %reduce-scatter.37.cloned.1.call-start = ((), (), s32[]{:S(2)}) async-start(), calls=%async_computation.41 | async-start | bytes 3145728 | tf_op jit(solution)/shard_map/reduce_scatter | solution.py:93
  1323.4 256.7 %reduce-scatter.35.cloned.1.call-start = ((), (), s32[]{:S(2)}) async-start(), calls=%async_computation.40 | async-start | bytes 2359296 | tf_op jit(solution)/shard_map/reduce_scatter | solution.py:93
  1325.4 295.0 %reduce-scatter.39.cloned.1.call-start = ((), (), s32[]{:S(2)}) async-start(), calls=%async_computation.42 | async-start | bytes 3932160 | tf_op jit(solution)/shard_map/reduce_scatter | solution.py:93
  1328.6 326.5 %reduce-scatter.31.cloned.1.call-start = ((), (), s32[]{:S(2)}) async-start(), calls=%async_computation.38 | async-start | bytes 3145728 | tf_op jit(solution)/shard_map/reduce_scatter | solution.py:93
  1331.7 352.2 %reduce-scatter.29.cloned.1.call-start = ((), (), s32[]{:S(2)}) async-start(), calls=%async_computation.37 | async-start | bytes 2359296 | tf_op jit(solution)/shard_map/reduce_scatter | solution.py:93
  1333.7 390.6 %reduce-scatter.33.cloned.1.call-start = ((), (), s32[]{:S(2)}) async-start(), calls=%async_computation.39 | async-start | bytes 3932160 | tf_op jit(solution)/shard_map/reduce_scatter | solution.py:93
  1337.2 404.5 %reduce-scatter.55.cloned.1.call-start = ((), (), s32[]{:S(2)}) async-start(), calls=%async_computation.64 | async-start | bytes 786432
  1376.1 399.1 %all-reduce.57.cloned.1.call-start = ((), (), s32[]{:S(2)}) async-start(), calls=%async_computation.51 | async-start | bytes 196608 | tf_op jit(solution)/shard_map/psum | solution.py:303
  1376.6 626.9 %all-reduce.61.cloned.1.call-start = ((), (), s32[]{:S(2)}) async-start(), calls=%async_computation.66 | async-start | bytes 25165824 | tf_op jit(solution)/shard_map/psum | solution.py:95
  (288 other events, 5115.8 us)
Sparse Core Ops, SparseCore 0:
  87.2 39.0 all-gather.27
  129.0 35.3 all-reduce.24
  203.4 35.2 all-reduce.26
  269.9 39.0 all-gather.33
  311.9 35.3 all-reduce.28
  386.2 35.3 all-reduce.30
  452.6 39.0 all-gather.39
  494.5 35.3 all-reduce.32
  568.8 35.3 all-reduce.34
  635.1 39.0 all-gather.45
  677.0 35.3 all-reduce.36
  752.1 35.3 all-reduce.38
  795.7 35.0 all-reduce.40
  877.0 35.3 all-reduce.42
  922.3 35.0 all-reduce.44
  1003.5 35.3 all-reduce.46
  1129.9 35.3 all-reduce.50
  1174.7 35.0 all-reduce.52
  1255.6 35.3 all-reduce.54
  1374.9 37.2 reduce-scatter.50
  1478.7 37.5 reduce-scatter.44
  1582.7 37.5 reduce-scatter.38
  1686.6 37.5 reduce-scatter.32
  1778.8 224.6 all-reduce.60
  (25 shorter events, 670.4 us)

commit v2 on v1

--- a/solution.py
+++ b/solution.py
@@ -1,8 +1,11 @@
+import functools
 import math
 
 import jax
 import jax.numpy as jnp
 from jax import lax
+from jax.experimental import pallas as pl
+from jax.experimental.pallas import tpu as pltpu
 from jax.sharding import PartitionSpec as P
 
 HEAD_DIM = 64
@@ -95,42 +98,299 @@
     return [lax.psum(s, "ctx").astype(jnp.float32) for s in shards]
 
 
-def layer_forward(h, mods, weights):
-    attend, hidden, output = weights
-    count, rows, width = h.shape
-    local = attend.shape[2]
+MESH = pl.DeviceIdType.MESH
+
+
+def dot(left, right):
+    return jnp.dot(left, right, preferred_element_type=jnp.float32)
+
+
+def dot_nt(left, right):
+    return lax.dot_general(left, right, (((1,), (1,)), ((), ())), preferred_element_type=jnp.float32)
+
+
+def dot_tn(left, right):
+    return lax.dot_general(left, right, (((0,), (0,)), ((), ())), preferred_element_type=jnp.float32)
+
+
+def remote(src, dst, sems, where, **device):
+    send, recv = (sems.at[(0, *where)], sems.at[(1, *where)])
+    return pltpu.make_async_remote_copy(
+        src_ref=src, dst_ref=dst, send_sem=send, recv_sem=recv, device_id=device, device_id_type=MESH
+    )
+
+
+def meet(sizes):
+    barrier = pltpu.get_barrier_semaphore()
+    count = 0
+    for axis, size in sizes.items():
+        for step in range(1, size):
+            peer = lax.rem(lax.axis_index(axis) + step, size)
+            pl.semaphore_signal(barrier, inc=1, device_id={axis: peer}, device_id_type=MESH)
+            count += 1
+    pl.semaphore_wait(barrier, count)
+
+
+def norm_parts(h):
+    mean = jnp.mean(h, -1, keepdims=True)
+    cent = h - mean
+    var = jnp.mean(cent * cent, -1, keepdims=True)
+    inv = lax.rsqrt(var + 1e-06)
+    return cent * inv, inv
+
+
+def norm_back(grad, normed, inv, scale):
+    grad_shift = jnp.sum(grad, 1)
+    grad_scale = jnp.sum(grad * normed, 1)
+    inner = grad * (1.0 + scale)
+    mean = jnp.mean(inner, -1, keepdims=True)
+    along = jnp.mean(inner * normed, -1, keepdims=True)
+    return inv * (inner - mean - normed * along), grad_shift, grad_scale
+
+
+def tp_send(part, size, send, first, sems):
+    me = lax.axis_index("tp")
+    send[...] = part.astype(LOW).reshape(send.shape)
+    for step in range(1, size):
+        peer = lax.rem(me + step, size)
+        remote(send.at[peer], first.at[step - 1], sems, (0, step - 1), tp=peer).start()
+
+
+def tp_finish(size, send, first, full, sems):
+    me = lax.axis_index("tp")
+    total = send[me].astype(jnp.float32)
+    for step in range(1, size):
+        peer = lax.rem(me + step, size)
+        remote(send.at[peer], first.at[step - 1], sems, (0, step - 1), tp=peer).wait()
+        total = total + first[step - 1].astype(jnp.float32)
+    full[me] = total.astype(LOW)
+    for step in range(1, size):
+        peer = lax.rem(me + step, size)
+        remote(full.at[me], full.at[me], sems, (1, step - 1), tp=peer).start()
+    for step in range(1, size):
+        peer = lax.rem(me + step, size)
+        source = lax.rem(me + size - step, size)
+        remote(full.at[me], full.at[me], sems, (1, step - 1), tp=peer).wait_send()
+        remote(full.at[source], full.at[source], sems, (1, step - 1), tp=peer).wait_recv()
+
+
+def spread(block, heads):
+    lane = lax.broadcasted_iota(jnp.int32, block.shape, 1) // HEAD_DIM
+    zero = jnp.zeros_like(block)
+    return jnp.concatenate([jnp.where(lane == k, block, zero) for k in range(heads)], 0)
+
+
+def pick(stacked, heads):
+    rows = stacked.shape[0] // heads
+    lane = lax.broadcasted_iota(jnp.int32, (rows, stacked.shape[1]), 1) // HEAD_DIM
+    total = jnp.zeros((rows, stacked.shape[1]), stacked.dtype)
+    for k in range(heads):
+        total = jnp.where(lane == k, stacked[k * rows : (k + 1) * rows], total)
+    return total
+
+
+ROOT_2_PI = math.sqrt(2.0 / math.pi)
+
+
+def gelu_parts(v):
+    inside = jnp.tanh(ROOT_2_PI * (v + 0.044715 * (v * v * v)))
+    value = v * (0.5 * (1.0 + inside))
+    slope = 0.5 * (1.0 + inside) + 0.5 * v * (1.0 - inside * inside) * ROOT_2_PI * (
+        1.0 + 3 * 0.044715 * v * v
+    )
+    return value, slope
+
+
+def forward_kernel(
+    sizes, h0_ref, mods_ref, low_ref, h_out, full_ref,
+    keep_h, keep_mid, keep_a, keep_m, keep_q, keep_kv, keep_p, keep_att, keep_pre,
+    weights, kv, h_ref, send_a, first_a, full_a, send_m, first_m, full_m,
+    x_sems, pair_sems, own_sems, kv_sems, a_sems, m_sems,
+):
+    nf, nc, nt = sizes["fsdp"], sizes["ctx"], sizes["tp"]
+    layer, layers = pl.program_id(0), pl.num_programs(0)
+    total_layers = low_ref.shape[0]
+    f, c = lax.axis_index("fsdp"), lax.axis_index("ctx")
+    core = lax.rem(c, 2)
+    sibling = c + 1 - 2 * core
+    count, rows, width = h_ref.shape
+    local = weights.shape[-1]
     heads = local // HEAD_DIM
     scale = 1.0 / math.sqrt(HEAD_DIM)
-    u_in = modln(h, mods[:, 0, None], mods[:, 1, None]).astype(LOW)
-    qkv = jnp.einsum("gsd,dke->gske", u_in, attend, preferred_element_type=jnp.float32).astype(LOW)
-    both = lax.all_gather(qkv[:, :, 1:], "ctx", axis=1, tiled=True)
-    query = qkv[:, :, 0].reshape(count, rows, heads, HEAD_DIM)
-    keys = both[:, :, 0].reshape(count, -1, heads, HEAD_DIM)
-    values = both[:, :, 1].reshape(count, -1, heads, HEAD_DIM)
-    scores = jnp.einsum("gqhe,gkhe->ghqk", query, keys, preferred_element_type=jnp.float32) * scale
-    top = jnp.max(scores, -1, keepdims=True)
-    expo = jnp.exp(scores - top)
-    probs = expo / jnp.sum(expo, -1, keepdims=True)
-    probs_low = probs.astype(LOW)
-    attended = (
-        jnp.einsum("ghqk,gkhe->gqhe", probs_low, values, preferred_element_type=jnp.float32)
-        .astype(LOW)
-        .reshape(count, rows, local)
-    )
-    branch_a = tp_total(
-        jnp.einsum("gsc,dc->gsd", attended, output[:, 0], preferred_element_type=jnp.float32)
-    )
-    h_mid = h + mods[:, 2, None] * branch_a
-    w_in = modln(h_mid, mods[:, 3, None], mods[:, 4, None]).astype(LOW)
-    pre = jnp.einsum("gsd,dkc->gskc", w_in, hidden, preferred_element_type=jnp.float32).reshape(
-        count, rows, 4 * local
-    )
-    act = gelu_tanh(pre).astype(LOW)
-    out_mlp = output[:, 1:].reshape(width, 4 * local)
-    branch_m = tp_total(jnp.einsum("gsk,dk->gsd", act, out_mlp, preferred_element_type=jnp.float32))
-    h_out = h_mid + mods[:, 5, None] * branch_m
-    kept = (h, u_in, query, keys, values, probs, probs_low, attended, branch_a, h_mid, w_in, pre)
-    return h_out, kept + (act, out_mlp, branch_m)
+
+    def x_copy(k, step):
+        peer = lax.rem(f + step, nf)
+        return remote(
+            low_ref.at[k, :, core], weights.at[k, :, f, core], x_sems, (k, step - 1), fsdp=peer
+        )
+
+    def x_arrived(k, step):
+        source = lax.rem(f + nf - step, nf)
+        block = weights.at[k, :, source, core]
+        remote(block, block, x_sems, (k, step - 1), fsdp=source).wait_recv()
+
+    def pair_copy(k, step, half):
+        source = lax.rem(f + nf - step, nf)
+        block = weights.at[k, :, source, half]
+        return remote(block, block, pair_sems, (k, step - 1), ctx=sibling)
+
+    def own_copy(k):
+        return pltpu.make_async_copy(low_ref.at[k], weights.at[k, :, f], own_sems.at[0, k])
+
+    def store_copy(k):
+        return pltpu.make_async_copy(weights.at[k], full_ref.at[k], own_sems.at[1, k])
+
+    def pass_on(k):
+        for step in range(1, nf):
+            x_arrived(k, step)
+            pair_copy(k, step, core).start()
+
+    @pl.when(layer == 0)
+    def _():
+        meet(sizes)
+        for k in range(total_layers):
+            for step in range(1, nf):
+                x_copy(k, step).start()
+            own_copy(k).start()
+        h_ref[...] = h0_ref[...]
+        pass_on(0)
+
+    def mod(k):
+        return mods_ref[6 * layer + k]
+
+    own_copy(layer).wait()
+    for step in range(1, nf):
+        pair_copy(layer, step, 1 - core).wait_recv()
+    store_copy(layer).start()
+
+    def matrix(k):
+        return weights[layer, k].reshape(width, local)
+
+    h = h_ref[...]
+    keep_h[0] = h
+    normed, _ = norm_parts(h)
+    u_in = (normed * (1.0 + mod(1)) + mod(0)).astype(LOW).reshape(count * rows, width)
+    key = dot(u_in, matrix(1)).astype(LOW)
+    kv[layer, c, :, :, :local] = key.reshape(count, rows, local)
+    value = dot(u_in, matrix(2)).astype(LOW)
+    kv[layer, c, :, :, local:] = value.reshape(count, rows, local)
+    for step in range(1, nc):
+        peer = lax.rem(c + step, nc)
+        block = kv.at[layer, c]
+        remote(block, block, kv_sems, (layer, step - 1), ctx=peer).start()
+    query = dot(u_in, matrix(0)).astype(LOW)
+    keep_q[0] = query.reshape(count, rows, local)
+    for step in range(1, nc):
+        peer = lax.rem(c + step, nc)
+        source = lax.rem(c + nc - step, nc)
+        remote(kv.at[layer, c], kv.at[layer, c], kv_sems, (layer, step - 1), ctx=peer).wait_send()
+        block = kv.at[layer, source]
+        remote(block, block, kv_sems, (layer, step - 1), ctx=peer).wait_recv()
+    keep_kv[0] = kv[layer]
+    for g in range(count):
+        keys = kv[layer, :, g, :, :local].reshape(nc * rows, local)
+        values = kv[layer, :, g, :, local:].reshape(nc * rows, local)
+        stacked = spread(query[g * rows : (g + 1) * rows], heads)
+        scores = dot_nt(stacked, keys) * scale
+        expo = jnp.exp(scores - jnp.max(scores, -1, keepdims=True))
+        probs = expo / jnp.sum(expo, -1, keepdims=True)
+        keep_p[0, g] = probs
+        keep_att[0, g * rows : (g + 1) * rows] = pick(dot(probs.astype(LOW), values), heads).astype(LOW)
+    tp_send(dot_nt(keep_att[0], matrix(7)), nt, send_a, first_a, a_sems)
+    tp_finish(nt, send_a, first_a, full_a, a_sems)
+    branch = full_a[...].reshape(count, rows, width)
+    keep_a[0] = branch
+    h_mid = h_ref[...] + mod(2) * branch.astype(jnp.float32)
+    keep_mid[0] = h_mid
+    normed, _ = norm_parts(h_mid)
+    w_in = (normed * (1.0 + mod(4)) + mod(3)).astype(LOW).reshape(count * rows, width)
+    part = jnp.zeros((count * rows, width), jnp.float32)
+    for k in range(4):
+        pre = dot(w_in, matrix(3 + k))
+        keep_pre[0, k] = pre
+        part = part + dot_nt(gelu_parts(pre)[0].astype(LOW), matrix(8 + k))
+    tp_send(part, nt, send_m, first_m, m_sems)
+
+    @pl.when(layer + 1 < layers)
+    def _():
+        pass_on(layer + 1)
+
+    tp_finish(nt, send_m, first_m, full_m, m_sems)
+    branch = full_m[...].reshape(count, rows, width)
+    keep_m[0] = branch
+    h_ref[...] = keep_mid[0] + mod(5) * branch.astype(jnp.float32)
+
+    @pl.when(layer == layers - 1)
+    def _():
+        h_out[...] = h_ref[...]
+        for k in range(total_layers):
+            store_copy(k).wait()
+            for step in range(1, nf):
+                x_copy(k, step).wait_send()
+                pair_copy(k, step, core).wait_send()
+
+
+def forward(mesh, h0, mods, low):
+    sizes = dict(mesh.shape)
+    nf, nc, nt = sizes["fsdp"], sizes["ctx"], sizes["tp"]
+    count, rows, width = h0.shape
+    layers, blocks, _, half, local = low.shape
+    heads = local // HEAD_DIM
+    tokens = count * rows
+    f32 = jnp.float32
+
+    def kept(shape, dtype):
+        spec = pl.BlockSpec((1, *shape), lambda i: (i,) + (0,) * len(shape))
+        return jax.ShapeDtypeStruct((layers, *shape), dtype), spec
+
+    saves = [
+        kept((count, rows, width), f32),
+        kept((count, rows, width), f32),
+        kept((count, rows, width), LOW),
+        kept((count, rows, width), LOW),
+        kept((count, rows, local), LOW),
+        kept((nc, count, rows, 2 * local), LOW),
+        kept((count, heads * rows, nc * rows), f32),
+        kept((tokens, local), LOW),
+        kept((4, tokens, local), f32),
+    ]
+    anywhere = pl.BlockSpec(memory_space=pl.ANY)
+    vmem = pl.BlockSpec(memory_space=pltpu.VMEM)
+    part = pltpu.VMEM((nt, tokens // nt, width), LOW)
+    first = pltpu.VMEM((nt - 1, tokens // nt, width), LOW)
+    dma = pltpu.SemaphoreType.DMA
+    return pl.pallas_call(
+        functools.partial(forward_kernel, sizes),
+        grid=(layers,),
+        out_shape=[
+            jax.ShapeDtypeStruct(h0.shape, f32),
+            jax.ShapeDtypeStruct((layers, blocks, nf, 2, half, local), LOW),
+            *(shape for shape, _ in saves),
+        ],
+        in_specs=[vmem, vmem, anywhere],
+        out_specs=[vmem, anywhere, *(spec for _, spec in saves)],
+        scratch_shapes=[
+            pltpu.VMEM((layers, blocks, nf, 2, half, local), LOW),
+            pltpu.VMEM((layers, nc, count, rows, 2 * local), LOW),
+            pltpu.VMEM((count, rows, width), f32),
+            part, first, part, part, first, part,
+            dma((2, layers, max(nf - 1, 1))),
+            dma((2, layers, max(nf - 1, 1))),
+            dma((2, layers)),
+            dma((2, layers, nc - 1)),
+            dma((2, 2, nt - 1)),
+            dma((2, 2, nt - 1)),
+        ],
+        compiler_params=pltpu.CompilerParams(
+            collective_id=1, has_side_effects=True, vmem_limit_bytes=56 * 2**20
+        ),
+        cost_estimate=pl.CostEstimate(
+            flops=2 * tokens * width * blocks * local * layers,
+            bytes_accessed=layers * blocks * width * local * 4,
+            transcendentals=0,
+        ),
+        name="forward_layers",
+    )(h0, mods, low)
 
 
 def layer_backward(kept, mods, weights, grad_out):
@@ -188,6 +448,7 @@
 
 
 def per_device(
+    mesh,
     latents,
     noise,
     var_target,
@@ -258,14 +519,12 @@
         jnp.einsum("gsp,dp->gsd", noisy, patch_full, preferred_element_type=jnp.float32)
         + positions(first, rows, width)[None]
     )
-    kept = []
-    weights = []
-    for layer in range(layers):
-        weights.append(
-            gather_layer(attend_weight[layer], hidden_weight[layer], output_weight[layer])
-        )
-        h, saved = layer_forward(h, mods[:, 6 * layer : 6 * layer + 6], weights[layer])
-        kept.append(saved)
+    low = jnp.concatenate(
+        [jnp.swapaxes(w, 1, 2).astype(LOW) for w in (attend_weight, hidden_weight, output_weight)], 1
+    ).reshape(layers, -1, 2, shard // 2, attend_weight.shape[3])
+    spread_mods = jnp.swapaxes(mods, 0, 1)[:, :, None]
+    h, full, *saved = forward(mesh, h, spread_mods, low)
+    full = full.reshape(layers, low.shape[1], width, -1)
     final_in = modln(h, mods[:, 6 * layers, None], mods[:, 6 * layers + 1, None]).astype(LOW)
     pred = jnp.einsum("gsd,dp->gsp", final_in, head_full, preferred_element_type=jnp.float32)
     diff = pred - jnp.concatenate([noise, var_target], -1)
@@ -278,9 +537,35 @@
     mod_grads = [None] * layers
     layer_shards = [None] * layers
     for layer in reversed(range(layers)):
-        d_h, mod_grads[layer], grads = layer_backward(
-            kept[layer], mods[:, 6 * layer : 6 * layer + 6], weights[layer], d_h
+        weights = tuple(
+            jnp.swapaxes(full[layer, lo:hi], 0, 1) for lo, hi in ((0, 3), (3, 7), (7, 12))
         )
+        keep_h, keep_mid, keep_a, keep_m, keep_q, keep_kv, keep_p, keep_att, keep_pre = (
+            k[layer] for k in saved
+        )
+        m = mods[:, 6 * layer : 6 * layer + 6]
+        heads = keep_q.shape[-1] // HEAD_DIM
+        both = jnp.swapaxes(keep_kv, 0, 1).reshape(count, -1, 2, heads, HEAD_DIM)
+        probs = keep_p.reshape(count, heads, rows, -1)
+        pre = jnp.swapaxes(keep_pre, 0, 1).reshape(count, rows, -1)
+        kept = (
+            keep_h,
+            modln(keep_h, m[:, 0, None], m[:, 1, None]).astype(LOW),
+            keep_q.reshape(count, rows, heads, HEAD_DIM),
+            both[:, :, 0],
+            both[:, :, 1],
+            probs,
+            probs.astype(LOW),
+            keep_att.reshape(count, rows, -1),
+            keep_a.astype(jnp.float32),
+            keep_mid,
+            modln(keep_mid, m[:, 3, None], m[:, 4, None]).astype(LOW),
+            pre,
+            gelu_tanh(pre).astype(LOW),
+            weights[2][:, 1:].reshape(width, -1),
+            keep_m.astype(jnp.float32),
+        )
+        d_h, mod_grads[layer], grads = layer_backward(kept, m, weights, d_h)
         layer_shards[layer] = reduce_layer(grads)
 
     d_mods = jnp.concatenate(mod_grads + [d_shift_f, d_scale_f], 1).reshape(count, -1)
@@ -358,7 +643,7 @@
     cond = P("fsdp", "tp")
     weights = (layer,) * 9 + (rows,) * 12 + (cond,) * 3 + (rows,) * 3
     return jax.shard_map(
-        per_device,
+        functools.partial(per_device, mesh),
         mesh=mesh,
         in_specs=(image, image, image, P("fsdp"), P("fsdp")) + weights,
         out_specs=(P(), P()) + weights,

time: 2230 us -> 1720 us (0.77)
  waiting for transfers between devices: 1520 us -> 880 us
  Pallas kernels: 0 us -> 193 us
  matrix products: 154 us -> 114 us
  blocking collectives: 119 us -> 92.2 us
    all_gather x12 -> x0, waiting for transfers between devices: 330 us -> none  [the longest x4 132 us: gather_layer(): lax.all_gather(hidden.astype(LOW), 'fsdp', axis=0, tiled=True)]
    psum x16 -> x8, waiting for transfers between devices: 510 us -> 205 us  [tp_total(): return lax.psum(part.astype(LOW), 'tp').astype(jnp.float32)]
    pallas_call x0 -> x1, Pallas kernels: none -> 193 us  [forward(): pl.pallas_call(functools.partial(forward_kernel, sizes), grid=(layers,),...]
    dot_general x20 -> x0, matrix products: 35 us -> none  [the longest x4 8.99 us: layer_forward(): jnp.einsum('gsd,dkc->gskc', w_in, hidden, preferred_element_type=jnp.floa...]
    all_gather x4 -> x0, blocking collectives: 28.8 us -> none  [layer_forward(): both = lax.all_gather(qkv[:, :, 1:], 'ctx', axis=1, tiled=True)]
    transpose x0 -> x11, local copies, waits for them, and re-layouts: none -> 22.3 us  [the longest x5 8.05 us: per_device(): pre = jnp.swapaxes(keep_pre, 0, 1).reshape(count, rows, -1)]
    slice x31 -> x15, local copies, waits for them, and re-layouts: 45.8 us -> 36.8 us  [the longest x8 22.9 us: per_device(): weights[2][:, 1:].reshape(width, -1)]
    unnamed x557 -> x421, local copies, waits for them, and re-layouts: 76.6 us -> 69.7 us
  transfers between devices with their start and end apart: 49 -> 29, of which waited for: 44 -> 24; matrix products, arithmetic and copies ran while one was open for 8% -> 10% of each run, Pallas kernels for 0% -> 0%
where the time goes in v2:
time: 1720 us; the launch traced here: 1710 us
  waiting for transfers between devices  880 us (51%)
  other arithmetic  230 us (13%)
  Pallas kernels  193 us (11%)
  local copies, waits for them, and re-layouts  164 us (10%)
  matrix products  114 us (7%)
  blocking collectives  92.2 us (5%)
  between operations  31.2 us (2%)
    reduce_scatter x12, waiting for transfers between devices, reduce_layer(): lax.psum_scatter(g.astype(LOW), 'fsdp', scatter_dimension=0, tiled=True)  343 us
    psum x1, waiting for transfers between devices, reduce_layer(): return [lax.psum(s, 'ctx').astype(jnp.float32) for s in shards]  226 us
    psum x8, waiting for transfers between devices, tp_total(): return lax.psum(part.astype(LOW), 'tp').astype(jnp.float32)  205 us
    pallas_call x1, Pallas kernels, forward(): pl.pallas_call(functools.partial(forward_kernel, sizes), grid=(layers,),...  193 us
    sub x9, other arithmetic, adamw(): weight - RATE * (fixed_mean / (jnp.sqrt(fixed_square) + EPSILON) + DECAY...  104 us
    reduce_scatter x4, waiting for transfers between devices, layer_backward(): lax.psum_scatter(jnp.stack([d_keys.reshape(count, -1, local), d_values.re...  74 us
    unnamed x421, local copies, waits for them, and re-layouts  69.7 us
  transfers between devices with their start and end apart: 29, of which 24 were waited for; matrix products, arithmetic and copies ran while one was open for 10% of the time, Pallas kernels for 0%

profile of v2, /device:TPU:0, one launch (start us, length us, event | category | flops | bytes accessed | tf_op | source)
XLA Modules:
  0.0 1706.1 jit_solution(5626166232178285344)
XLA Ops:
  75.6 192.8 %forward_layers.1 = (f32[2,64,1024]{2,1,0:T(8,128)}, bf16[4,12,2,2,256,256]{5,4,3,2,1,0:T(8,128)(2,1)}, f32[4,2,64,1024]{3,2,1,0:T(8,128)}, f32[4,2,64,1024]{3,2...) custom-call(f32[2,64,1024]{2,1,0:T(8,128)} %convolution_add_fusion.h, ...), custom_call_target="tpu_custom_call" | custom-call | flops 3221225472 | bytes 50331648 | tf_op jit(solution)/shard_map/forward_layers/pallas_call | solution.py:362
  309.6 22.3 %all-reduce.17.cloned.1.call-done = bf16[2,64,1024]{2,1,0:T(8,128)(2,1)} async-done(((bf16[2,64,1024]{2,1,0:T(8,128)(2,1)}), bf16[2,64,1024]{2,1,0:T(8,128)(2,1)}) %all-reduce.17.cloned.1.call-update) | async-done | bytes 262160 | tf_op jit(solution)/shard_map/psum | solution.py:83
  349.1 19.2 %reduce-scatter.21.cloned.1.call-done = bf16[2,64,2,256]{3,1,2,0:T(8,128)(2,1)} async-done(((bf16[2,256,2,256]{3,1,2,0:T(8,128)(2,1)}), bf16[2,64,2,256]{3,1,2,0:T(8,128)(2,1)}) %reduce-scatter.21.cloned.1.call-update) | async-done | bytes 131088 | tf_op jit(solution)/shard_map/reduce_scatter | solution.py:430
  385.6 21.1 %all-reduce.19.cloned.1.call-done = bf16[2,64,1024]{2,1,0:T(8,128)(2,1)} async-done(((bf16[2,64,1024]{2,1,0:T(8,128)(2,1)}), bf16[2,64,1024]{2,1,0:T(8,128)(2,1)}) %all-reduce.19.cloned.1.call-update) | async-done | bytes 262160 | tf_op jit(solution)/shard_map/psum | solution.py:83
  422.0 31.1 %all-reduce.21.cloned.1.call-done = bf16[2,64,1024]{2,1,0:T(8,128)(2,1)} async-done(((bf16[2,64,1024]{2,1,0:T(8,128)(2,1)}), bf16[2,64,1024]{2,1,0:T(8,128)(2,1)}) %all-reduce.21.cloned.1.call-update) | async-done | bytes 262160 | tf_op jit(solution)/shard_map/psum | solution.py:83
  545.5 29.9 %all-reduce.25.cloned.1.call-done = bf16[2,64,1024]{2,1,0:T(8,128)(2,1)} async-done(((bf16[2,64,1024]{2,1,0:T(8,128)(2,1)}), bf16[2,64,1024]{2,1,0:T(8,128)(2,1)}) %all-reduce.25.cloned.1.call-update) | async-done | bytes 262160 | tf_op jit(solution)/shard_map/psum | solution.py:83
  670.4 29.9 %all-reduce.29.cloned.1.call-done = bf16[2,64,1024]{2,1,0:T(8,128)(2,1)} async-done(((bf16[2,64,1024]{2,1,0:T(8,128)(2,1)}), bf16[2,64,1024]{2,1,0:T(8,128)(2,1)}) %all-reduce.29.cloned.1.call-update) | async-done | bytes 262160 | tf_op jit(solution)/shard_map/psum | solution.py:83
  745.3 32.9 %all-reduce.31.cloned.1.call-done = bf16[2,64,1024]{2,1,0:T(8,128)(2,1)} async-done(((bf16[2,64,1024]{2,1,0:T(8,128)(2,1)}), bf16[2,64,1024]{2,1,0:T(8,128)(2,1)}) %all-reduce.31.cloned.1.call-update) | async-done | bytes 262160 | tf_op jit(solution)/shard_map/psum | solution.py:83
  868.5 31.4 %reduce-scatter.51.cloned.1.call-done = bf16[512,5,256]{2,0,1:T(8,128)(2,1)} async-done(((bf16[1024,5,256]{2,0,1:T(8,128)(2,1)}), bf16[512,5,256]{2,0,1:T(8,128)(2,1)}) %reduce-scatter.51.cloned.1.call-update) | async-done | bytes 1310736 | tf_op jit(solution)/shard_map/reduce_scatter | solution.py:96
  899.9 34.6 %reduce-scatter.43.cloned.1.call-done = bf16[512,4,256]{2,0,1:T(8,128)(2,1)} async-done(((bf16[1024,4,256]{2,0,1:T(8,128)(2,1)}), bf16[512,4,256]{2,0,1:T(8,128)(2,1)}) %reduce-scatter.43.cloned.1.call-update) | async-done | bytes 1048592 | tf_op jit(solution)/shard_map/reduce_scatter | solution.py:96
  934.6 28.9 %reduce-scatter.41.cloned.1.call-done = bf16[512,3,256]{2,0,1:T(8,128)(2,1)} async-done(((bf16[1024,3,256]{2,0,1:T(8,128)(2,1)}), bf16[512,3,256]{2,0,1:T(8,128)(2,1)}) %reduce-scatter.41.cloned.1.call-update) | async-done | bytes 786448 | tf_op jit(solution)/shard_map/reduce_scatter | solution.py:96
  963.5 40.4 %reduce-scatter.45.cloned.1.call-done = bf16[512,5,256]{2,0,1:T(8,128)(2,1)} async-done(((bf16[1024,5,256]{2,0,1:T(8,128)(2,1)}), bf16[512,5,256]{2,0,1:T(8,128)(2,1)}) %reduce-scatter.45.cloned.1.call-update) | async-done | bytes 1310736 | tf_op jit(solution)/shard_map/reduce_scatter | solution.py:96
  1003.9 34.7 %reduce-scatter.37.cloned.1.call-done = bf16[512,4,256]{2,0,1:T(8,128)(2,1)} async-done(((bf16[1024,4,256]{2,0,1:T(8,128)(2,1)}), bf16[512,4,256]{2,0,1:T(8,128)(2,1)}) %reduce-scatter.37.cloned.1.call-update) | async-done | bytes 1048592 | tf_op jit(solution)/shard_map/reduce_scatter | solution.py:96
  1038.6 29.0 %reduce-scatter.35.cloned.1.call-done = bf16[512,3,256]{2,0,1:T(8,128)(2,1)} async-done(((bf16[1024,3,256]{2,0,1:T(8,128)(2,1)}), bf16[512,3,256]{2,0,1:T(8,128)(2,1)}) %reduce-scatter.35.cloned.1.call-update) | async-done | bytes 786448 | tf_op jit(solution)/shard_map/reduce_scatter | solution.py:96
  1067.6 40.4 %reduce-scatter.39.cloned.1.call-done = bf16[512,5,256]{2,0,1:T(8,128)(2,1)} async-done(((bf16[1024,5,256]{2,0,1:T(8,128)(2,1)}), bf16[512,5,256]{2,0,1:T(8,128)(2,1)}) %reduce-scatter.39.cloned.1.call-update) | async-done | bytes 1310736 | tf_op jit(solution)/shard_map/reduce_scatter | solution.py:96
  1108.0 34.6 %reduce-scatter.31.cloned.1.call-done = bf16[512,4,256]{2,0,1:T(8,128)(2,1)} async-done(((bf16[1024,4,256]{2,0,1:T(8,128)(2,1)}), bf16[512,4,256]{2,0,1:T(8,128)(2,1)}) %reduce-scatter.31.cloned.1.call-update) | async-done | bytes 1048592 | tf_op jit(solution)/shard_map/reduce_scatter | solution.py:96
  1142.6 28.9 %reduce-scatter.29.cloned.1.call-done = bf16[512,3,256]{2,0,1:T(8,128)(2,1)} async-done(((bf16[1024,3,256]{2,0,1:T(8,128)(2,1)}), bf16[512,3,256]{2,0,1:T(8,128)(2,1)}) %reduce-scatter.29.cloned.1.call-update) | async-done | bytes 786448 | tf_op jit(solution)/shard_map/reduce_scatter | solution.py:96
  1171.6 40.4 %reduce-scatter.33.cloned.1.call-done = bf16[512,5,256]{2,0,1:T(8,128)(2,1)} async-done(((bf16[1024,5,256]{2,0,1:T(8,128)(2,1)}), bf16[512,5,256]{2,0,1:T(8,128)(2,1)}) %reduce-scatter.33.cloned.1.call-update) | async-done | bytes 1310736 | tf_op jit(solution)/shard_map/reduce_scatter | solution.py:96
  1233.4 29.6 %all-reduce.33.cloned.1.call-done = f32[512,48]{0,1:T(8,128)} async-done(((f32[512,48]{0,1:T(8,128)}), f32[512,48]{0,1:T(8,128)}) %all-reduce.33.cloned.1.call-update) | async-done | bytes 98320 | tf_op jit(solution)/shard_map/psum | solution.py:588
  1265.2 226.3 %all-reduce.37.cloned.1.call-done = (bf16[512,3,256]{2,0,1:T(8,128)(2,1)}, bf16[512,4,256]{2,0,1:T(8,128)(2,1)}, bf16[512,5,256]{2,0,1:T(8,128)(2,1)}, bf16[512,...) async-done(((bf16[512,3,256]{2,0,1:T(8,128)(2,1)}, ...) | async-done | bytes 12582928 | tf_op jit(solution)/shard_map/psum | solution.py:98
  1534.1 21.9 %psum.199 = f32[]{:T(128)} all-reduce(f32[]{:T(128)S(6)} %add.744), channel_id=1, replica_groups=mesh['fsdp'=2,'ctx'=4,'tp'=4] {'fsdp','tp'}, use_global_device_ids=true, to_apply=%region_127.128 | all-reduce | flops 1 | bytes 8 | tf_op jit(solution)/shard_map/psum | solution.py:608
  1556.8 22.0 %multiply_subtract_fusion.2 = (f32[4,512,4,256]{3,1,2,0:T(8,128)}, f32[4,512,4,256]{3,1,2,0:T(8,128)}, f32[4,512,4,256]{3,1,2,0:T(8,128)}) fusion(f32[4,512,4,256]{3,2,1,0:T(4,128)} %param.40, f32[]{:T(128)S(6)} %min.3, f32[1,512,4,256]{3,1,2,0:T(8,128)} %convert_bitcast_fusion.6, f32[1,512,4,256]{3,1,2,0:T(8,128)} %convert_bitcast_fusion.7, ...), kind=kLoop, calls=%fused_computation.19 | loop fusion | flops 37748736 | bytes 58720260 | tf_op jit(solution)/shard_map/sub | solution.py:65
  1633.9 20.8 %multiply_subtract_fusion.1 = (f32[4,512,5,256]{3,1,2,0:T(8,128)}, f32[4,512,5,256]{3,1,2,0:T(8,128)}, f32[4,512,5,256]{3,1,2,0:T(8,128)}) fusion(f32[4,512,5,256]{3,1,2,0:T(8,128)S(1)} %bitcast.808, f32[]{:T(128)S(6)} %min.3, f32[1,512,5,256]{3,1,2,0:T(8,128)S(1)} %copy-done.5, f32[1,512,5,256]{3,1,2,0:T(8,128)} %convert_bitcast_fusion.2, ...), kind=kLoop, calls=%fused_computation.12 | loop fusion | flops 47185920 | bytes 73400320 | tf_op jit(solution)/shard_map/sub | solution.py:65
  1670.1 26.8 %multiply_subtract_fusion = (f32[512,6656]{1,0:T(8,128)}, f32[512,6656]{1,0:T(8,128)}, f32[512,6656]{1,0:T(8,128)}) fusion(f32[512,6656]{1,0:T(8,128)S(1)} %bitcast.805, f32[]{:T(128)S(6)} %min.3, f32[6656]{0:T(1024)S(1)} %get-tuple-element.227, f32[512]{0:T(512)S(1)} %bitcast.902, f32[6656]{0:T(1024)S(1)} %get-tuple-element.228, f32[512]{0:T(512)S(1)} %bitcast.901, ...), kind=kLoop, calls=%fused_computation.5 | loop fusion | flops 74973184 | bytes 81903616 | tf_op jit(solution)/shard_map/sub | solution.py:65
  (782 shorter events, 604.8 us)
Async XLA Ops:
  32.0 299.9 %all-reduce.17.cloned.1.call-start = ((), (), s32[]{:S(2)}) async-start(), calls=%async_computation.18 | async-start | bytes 524288 | tf_op jit(solution)/shard_map/psum | solution.py:83
  296.6 71.7 %reduce-scatter.21.cloned.1.call-start = ((), (), s32[]{:S(2)}) async-start(), calls=%async_computation.19 | async-start | bytes 655360 | tf_op jit(solution)/shard_map/reduce_scatter | solution.py:430
  371.1 82.0 %all-reduce.21.cloned.1.call-start = ((), (), s32[]{:S(2)}) async-start(), calls=%async_computation.21 | async-start | bytes 524288 | tf_op jit(solution)/shard_map/psum | solution.py:83
  417.9 72.7 %reduce-scatter.23.cloned.1.call-start = ((), (), s32[]{:S(2)}) async-start(), calls=%async_computation.22 | async-start | bytes 655360 | tf_op jit(solution)/shard_map/reduce_scatter | solution.py:430
  493.4 82.0 %all-reduce.25.cloned.1.call-start = ((), (), s32[]{:S(2)}) async-start(), calls=%async_computation.24 | async-start | bytes 524288 | tf_op jit(solution)/shard_map/psum | solution.py:83
  540.2 73.5 %reduce-scatter.25.cloned.1.call-start = ((), (), s32[]{:S(2)}) async-start(), calls=%async_computation.25 | async-start | bytes 655360 | tf_op jit(solution)/shard_map/reduce_scatter | solution.py:430
  616.5 83.8 %all-reduce.29.cloned.1.call-start = ((), (), s32[]{:S(2)}) async-start(), calls=%async_computation.27 | async-start | bytes 524288 | tf_op jit(solution)/shard_map/psum | solution.py:83
  665.1 74.8 %reduce-scatter.27.cloned.1.call-start = ((), (), s32[]{:S(2)}) async-start(), calls=%async_computation.28 | async-start | bytes 655360 | tf_op jit(solution)/shard_map/reduce_scatter | solution.py:430
  742.8 125.0 %reduce-scatter.53.cloned.1.call-start = ((), (), s32[]{:S(2)}) async-start(), calls=%async_computation.42 | async-start | bytes 294912 | tf_op jit(solution)/shard_map/reduce_scatter | solution.py:589
  784.3 84.2 %reduce-scatter.49.cloned.1.call-start = ((), (), s32[]{:S(2)}) async-start(), calls=%async_computation.39 | async-start | bytes 3145728 | tf_op jit(solution)/shard_map/reduce_scatter | solution.py:96
  787.2 81.3 %reduce-scatter.47.cloned.1.call-start = ((), (), s32[]{:S(2)}) async-start(), calls=%async_computation.38 | async-start | bytes 2359296 | tf_op jit(solution)/shard_map/reduce_scatter | solution.py:96
  790.2 109.7 %reduce-scatter.51.cloned.1.call-start = ((), (), s32[]{:S(2)}) async-start(), calls=%async_computation.40 | async-start | bytes 3932160 | tf_op jit(solution)/shard_map/reduce_scatter | solution.py:96
  797.3 137.3 %reduce-scatter.43.cloned.1.call-start = ((), (), s32[]{:S(2)}) async-start(), calls=%async_computation.36 | async-start | bytes 3145728 | tf_op jit(solution)/shard_map/reduce_scatter | solution.py:96
  800.3 163.2 %reduce-scatter.41.cloned.1.call-start = ((), (), s32[]{:S(2)}) async-start(), calls=%async_computation.35 | async-start | bytes 2359296 | tf_op jit(solution)/shard_map/reduce_scatter | solution.py:96
  803.4 200.5 %reduce-scatter.45.cloned.1.call-start = ((), (), s32[]{:S(2)}) async-start(), calls=%async_computation.37 | async-start | bytes 3932160 | tf_op jit(solution)/shard_map/reduce_scatter | solution.py:96
  807.7 230.8 %reduce-scatter.37.cloned.1.call-start = ((), (), s32[]{:S(2)}) async-start(), calls=%async_computation.33 | async-start | bytes 3145728 | tf_op jit(solution)/shard_map/reduce_scatter | solution.py:96
  810.8 256.8 %reduce-scatter.35.cloned.1.call-start = ((), (), s32[]{:S(2)}) async-start(), calls=%async_computation.32 | async-start | bytes 2359296 | tf_op jit(solution)/shard_map/reduce_scatter | solution.py:96
  813.8 294.2 %reduce-scatter.39.cloned.1.call-start = ((), (), s32[]{:S(2)}) async-start(), calls=%async_computation.34 | async-start | bytes 3932160 | tf_op jit(solution)/shard_map/reduce_scatter | solution.py:96
  818.1 324.6 %reduce-scatter.31.cloned.1.call-start = ((), (), s32[]{:S(2)}) async-start(), calls=%async_computation.30 | async-start | bytes 3145728 | tf_op jit(solution)/shard_map/reduce_scatter | solution.py:96
  821.1 350.5 %reduce-scatter.29.cloned.1.call-start = ((), (), s32[]{:S(2)}) async-start(), calls=%async_computation.29 | async-start | bytes 2359296 | tf_op jit(solution)/shard_map/reduce_scatter | solution.py:96
  824.2 387.7 %reduce-scatter.33.cloned.1.call-start = ((), (), s32[]{:S(2)}) async-start(), calls=%async_computation.31 | async-start | bytes 3932160 | tf_op jit(solution)/shard_map/reduce_scatter | solution.py:96
  827.5 401.9 %reduce-scatter.55.cloned.1.call-start = ((), (), s32[]{:S(2)}) async-start(), calls=%async_computation.44 | async-start | bytes 786432
  867.7 395.3 %all-reduce.33.cloned.1.call-start = ((), (), s32[]{:S(2)}) async-start(), calls=%async_computation.43 | async-start | bytes 196608 | tf_op jit(solution)/shard_map/psum | solution.py:588
  868.4 623.1 %all-reduce.37.cloned.1.call-start = ((), (), s32[]{:S(2)}) async-start(), calls=%async_computation.46 | async-start | bytes 25165824 | tf_op jit(solution)/shard_map/psum | solution.py:98
  (205 other events, 3153.9 us)
Sparse Core Ops, SparseCore 0:
  32.2 22.8 all-reduce.34
  296.8 35.1 all-reduce.16
  371.3 35.3 all-reduce.18
  418.0 35.0 all-reduce.20
  493.6 35.3 all-reduce.22
  540.3 35.0 all-reduce.24
  592.2 21.3 reduce-scatter.24
  616.7 35.2 all-reduce.26
  665.2 35.0 all-reduce.28
  742.9 35.2 all-reduce.30
  797.8 31.8 reduce-scatter.48
  832.4 27.2 reduce-scatter.46
  862.3 37.5 reduce-scatter.50
  902.7 31.8 reduce-scatter.42
  937.4 26.0 reduce-scatter.40
  966.2 37.5 reduce-scatter.44
  1006.7 31.8 reduce-scatter.36
  1041.5 26.0 reduce-scatter.34
  1070.4 37.5 reduce-scatter.38
  1110.8 31.8 reduce-scatter.30
  1145.5 26.0 reduce-scatter.28
  1174.3 37.5 reduce-scatter.32
  1231.7 31.2 all-reduce.32
  1266.8 224.6 all-reduce.36
  (5 shorter events, 89.1 us)

commit v3 on v2

--- a/solution.py
+++ b/solution.py
@@ -77,25 +77,6 @@
     one = jnp.einsum("nd,md->nm", left, left, precision=HIGH)
     two = jnp.einsum("nd,md->nm", right, right, precision=HIGH)
     return jnp.sum(one * two)
-
-
-def tp_total(part):
-    return lax.psum(part.astype(LOW), "tp").astype(jnp.float32)
-
-
-def gather_layer(attend, hidden, output):
-    return (
-        lax.all_gather(attend.astype(LOW), "fsdp", axis=0, tiled=True),
-        lax.all_gather(hidden.astype(LOW), "fsdp", axis=0, tiled=True),
-        lax.all_gather(output.astype(LOW), "fsdp", axis=0, tiled=True),
-    )
-
-
-def reduce_layer(grads):
-    shards = [
-        lax.psum_scatter(g.astype(LOW), "fsdp", scatter_dimension=0, tiled=True) for g in grads
-    ]
-    return [lax.psum(s, "ctx").astype(jnp.float32) for s in shards]
 
 
 MESH = pl.DeviceIdType.MESH
@@ -393,58 +374,335 @@
     )(h0, mods, low)
 
 
-def layer_backward(kept, mods, weights, grad_out):
-    attend, hidden, output = weights
-    (h, u_in, query, keys, values, probs, probs_low, attended, branch_a, h_mid, w_in, pre) = kept[:12]
-    act, out_mlp, branch_m = kept[12:]
-    count, rows, width = h.shape
-    local = attend.shape[2]
+CHUNKS = 4
+
+
+def backward_kernel(
+    sizes, dh0_ref, mods_ref, w_ref, keep_h, keep_mid, keep_a, keep_m, keep_q, keep_kv, keep_p, keep_att, keep_pre,
+    dh_out, dmods_ref, grads_ref, square_ref,
+    dh_ref, dmid_ref, act_ref, dpre_ref, dba_ref, dqkv_ref,
+    send_w, first_w, full_w, send_u, first_u, full_u, kv_send, kv_got,
+    grads, pair_got, x_send, x_got, y_send, y_got, done,
+    w_sems, u_sems, kv_sems, pair_sems, x_sems, y_sems, end_sems, own_sems,
+):
+    nf, nc, nt = sizes["fsdp"], sizes["ctx"], sizes["tp"]
+    chips = nc // 2
+    layers, blocks, _, half, local = grads_ref.shape
+    each = blocks // CHUNKS
+    step = pl.program_id(0)
+    new = lax.rem(step, 2)
+    old = 1 - new
+    f, c = lax.axis_index("fsdp"), lax.axis_index("ctx")
+    core = lax.rem(c, 2)
+    sibling = c + 1 - 2 * core
+    count, rows, width = dh_ref.shape
+    tokens = count * rows
+    heads = local // HEAD_DIM
     scale = 1.0 / math.sqrt(HEAD_DIM)
-    d_gate_m = jnp.sum(grad_out * branch_m, 1)
-    d_branch = (mods[:, 5, None] * grad_out).astype(LOW)
-    d_act = jnp.einsum("gsd,dk->gsk", d_branch, out_mlp, preferred_element_type=jnp.float32)
-    d_out_mlp = jnp.einsum("gsd,gsk->dk", d_branch, act, preferred_element_type=jnp.float32)
-    _, gelu_back = jax.vjp(gelu_tanh, pre)
-    d_pre = gelu_back(d_act)[0].astype(LOW).reshape(count, rows, 4, local)
-    d_hidden = jnp.einsum("gsd,gskc->dkc", w_in, d_pre, preferred_element_type=jnp.float32)
-    d_w = tp_total(jnp.einsum("gskc,dkc->gsd", d_pre, hidden, preferred_element_type=jnp.float32))
-    _, norm_back = jax.vjp(modln, h_mid, mods[:, 3, None], mods[:, 4, None])
-    d_mid, d_shift_m, d_scale_m = norm_back(d_w)
-    d_mid = d_mid + grad_out
-    d_gate_a = jnp.sum(d_mid * branch_a, 1)
-    d_branch_a = (mods[:, 2, None] * d_mid).astype(LOW)
-    d_att = jnp.einsum(
-        "gsd,dc->gsc", d_branch_a, output[:, 0], preferred_element_type=jnp.float32
-    ).astype(LOW)
-    d_out_att = jnp.einsum("gsd,gsc->dc", d_branch_a, attended, preferred_element_type=jnp.float32)
-    d_att = d_att.reshape(count, rows, -1, HEAD_DIM)
-    d_probs = jnp.einsum("gqhe,gkhe->ghqk", d_att, values, preferred_element_type=jnp.float32)
-    d_values = jnp.einsum("ghqk,gqhe->gkhe", probs_low, d_att, preferred_element_type=jnp.float32)
-    d_scores = (probs * (d_probs - jnp.sum(d_probs * probs, -1, keepdims=True))).astype(LOW)
-    d_query = (
-        jnp.einsum("ghqk,gkhe->gqhe", d_scores, keys, preferred_element_type=jnp.float32) * scale
-    ).astype(LOW)
-    d_keys = (
-        jnp.einsum("ghqk,gqhe->gkhe", d_scores, query, preferred_element_type=jnp.float32) * scale
-    )
-    d_both = lax.psum_scatter(
-        jnp.stack(
-            [d_keys.reshape(count, -1, local), d_values.reshape(count, -1, local)], 2
-        ).astype(LOW),
-        "ctx",
-        scatter_dimension=1,
-        tiled=True,
-    )
-    d_qkv = jnp.concatenate([d_query.reshape(count, rows, 1, local), d_both], 2)
-    d_attend = jnp.einsum("gsd,gske->dke", u_in, d_qkv, preferred_element_type=jnp.float32)
-    d_u = tp_total(jnp.einsum("gske,dke->gsd", d_qkv, attend, preferred_element_type=jnp.float32))
-    _, norm_back = jax.vjp(modln, h, mods[:, 0, None], mods[:, 1, None])
-    d_h, d_shift_a, d_scale_a = norm_back(d_u)
-    d_mods = jnp.stack(
-        [d_shift_a[:, 0], d_scale_a[:, 0], d_gate_a, d_shift_m[:, 0], d_scale_m[:, 0], d_gate_m], 1
-    )
-    d_output = jnp.concatenate([d_out_att[:, None], d_out_mlp.reshape(width, 4, local)], 1)
-    return (d_h + d_mid, d_mods, (d_attend, d_hidden, d_output))
+    piece = min(64, half)
+    f32 = jnp.float32
+
+    def chunk(q):
+        return pl.ds(q * each, each)
+
+    def pieces(body):
+        def one(j, carry):
+            b, r = j // (half // piece), lax.rem(j, half // piece)
+            body(b, pl.ds(pl.multiple_of(r * piece, piece), piece))
+            return carry
+
+        return lambda q: lax.fori_loop(q * each * (half // piece), (q + 1) * each * (half // piece), one, 0)
+
+    def each_chunk(body):
+        def one(q, carry):
+            body(q)
+            return carry
+
+        lax.fori_loop(0, CHUNKS, one, 0)
+
+    def pair_copy(q):
+        return remote(
+            grads.at[old, chunk(q), :, 1 - core], pair_got.at[old, chunk(q)], pair_sems, (old, q), ctx=sibling
+        )
+
+    def x_copy(q, ahead):
+        peer = lax.rem(f + ahead, nf)
+        return remote(
+            x_send.at[ahead - 1, chunk(q)], x_got.at[old, ahead - 1, chunk(q)], x_sems, (old, q, ahead - 1), fsdp=peer
+        )
+
+    def y_copy(q, ahead, parity):
+        peer = lax.rem(c // 2 + ahead, chips) * 2 + core
+        return remote(
+            y_send.at[chunk(q)], y_got.at[parity, ahead - 1, chunk(q)], y_sems, (parity, q, ahead - 1), ctx=peer
+        )
+
+    def end_copy(q, layer, parity, to):
+        return remote(
+            done.at[chunk(q)], grads_ref.at[layer, chunk(q), to], end_sems, (parity, q), ctx=sibling
+        )
+
+    def own_copy(q, layer):
+        return pltpu.make_async_copy(done.at[chunk(q)], grads_ref.at[layer, chunk(q), core], own_sems.at[q])
+
+    def start_pair():
+        each_chunk(lambda q: pair_copy(q).start())
+
+    def start_x():
+        def one(q):
+            pair_copy(q).wait()
+            for ahead in range(1, nf):
+                peer = lax.rem(f + ahead, nf)
+
+                def add(b, r):
+                    total = grads[old, b, peer, core, r].astype(f32) + pair_got[old, b, peer, r].astype(f32)
+                    x_send[ahead - 1, b, r] = total.astype(LOW)
+
+                pieces(add)(q)
+                x_copy(q, ahead).start()
+
+        each_chunk(one)
+
+    def start_y():
+        def one(q):
+            for ahead in range(1, nf):
+                x_copy(q, ahead).wait()
+
+            def add(b, r):
+                total = grads[old, b, f, core, r].astype(f32) + pair_got[old, b, f, r].astype(f32)
+                for ahead in range(1, nf):
+                    total = total + x_got[old, ahead - 1, b, r].astype(f32)
+                y_send[b, r] = total.astype(LOW)
+
+            pieces(add)(q)
+            for ahead in range(1, chips):
+                y_copy(q, ahead, old).start()
+
+        each_chunk(one)
+
+    def wait_end(layer, parity):
+        def one(q):
+            own_copy(q, layer).wait()
+            end_copy(q, layer, parity, core).wait_send()
+            end_copy(q, layer, parity, 1 - core).wait_recv()
+
+        each_chunk(one)
+
+    def start_end():
+        layer = layers + 1 - step
+
+        @pl.when(step >= 3)
+        def _():
+            wait_end(layer + 1, old)
+
+        def one(q):
+            for ahead in range(1, chips):
+                y_copy(q, ahead, new).wait()
+
+            def add(b, r):
+                total = y_send[b, r].astype(f32)
+                for ahead in range(1, chips):
+                    total = total + y_got[new, ahead - 1, b, r].astype(f32)
+                low = total.astype(LOW)
+                done[b, r] = low
+                total = low.astype(f32)
+                square_ref[...] += jnp.sum((total * total).reshape(piece // 8, 8, local), 0)
+
+            pieces(add)(q)
+            own_copy(q, layer).start()
+            end_copy(q, layer, new, core).start()
+
+        each_chunk(one)
+
+    def matrix(k):
+        return w_ref[0, k].reshape(width, local)
+
+    def mod(k):
+        return mods_ref[6 * (layers - 1 - step) + k]
+
+    def keep_grad(k, value):
+        grads[new, k] = value.astype(LOW).reshape(nf, 2, half, local)
+
+    @pl.when(step == 0)
+    def _():
+        meet(sizes)
+        dh_ref[...] = dh0_ref[...]
+        square_ref[...] = jnp.zeros_like(square_ref)
+
+    @pl.when((step >= 1) & (step <= layers))
+    def _():
+        start_pair()
+
+    @pl.when(step < layers)
+    def _():
+        grad = dh_ref[...]
+        dmods_ref[0, 5] = jnp.sum(grad * keep_m[0].astype(f32), 1)
+        branch = (mod(5) * grad).astype(LOW).reshape(tokens, width)
+        part = jnp.zeros((tokens, width), f32)
+        for k in range(4):
+            value, slope = gelu_parts(keep_pre[0, k])
+            act_ref[k] = value.astype(LOW)
+            d_pre = (dot(branch, matrix(8 + k)) * slope).astype(LOW)
+            dpre_ref[k] = d_pre
+            part = part + dot_nt(d_pre, matrix(3 + k))
+        tp_send(part, nt, send_w, first_w, w_sems)
+        for k in range(4):
+            keep_grad(8 + k, dot_tn(branch, act_ref[k]))
+        normed, _ = norm_parts(keep_mid[0])
+        w_in = (normed * (1.0 + mod(4)) + mod(3)).astype(LOW).reshape(tokens, width)
+        for k in range(4):
+            keep_grad(3 + k, dot_tn(w_in, dpre_ref[k]))
+
+    @pl.when((step >= 1) & (step <= layers))
+    def _():
+        start_x()
+
+    @pl.when(step < layers)
+    def _():
+        tp_finish(nt, send_w, first_w, full_w, w_sems)
+        normed, inv = norm_parts(keep_mid[0])
+        d_mid, d_shift, d_scale = norm_back(
+            full_w[...].reshape(count, rows, width).astype(f32), normed, inv, mod(4)
+        )
+        d_mid = d_mid + dh_ref[...]
+        dmid_ref[...] = d_mid
+        dmods_ref[0, 3] = d_shift
+        dmods_ref[0, 4] = d_scale
+        dmods_ref[0, 2] = jnp.sum(d_mid * keep_a[0].astype(f32), 1)
+        branch = (mod(2) * d_mid).astype(LOW).reshape(tokens, width)
+        dba_ref[...] = branch
+        d_att = dot(branch, matrix(7)).astype(LOW)
+        for g in range(count):
+            keys = keep_kv[0, :, g, :, :local].reshape(nc * rows, local)
+            values = keep_kv[0, :, g, :, local:].reshape(nc * rows, local)
+            grad = spread(d_att[g * rows : (g + 1) * rows], heads)
+            query = spread(keep_q[0, g], heads)
+            probs = keep_p[0, g]
+            d_probs = dot_nt(grad, values)
+            d_scores = (probs * (d_probs - jnp.sum(d_probs * probs, -1, keepdims=True))).astype(LOW)
+            d_values = dot_tn(probs.astype(LOW), grad)
+            d_keys = dot_tn(d_scores, query) * scale
+            kv_send[:, g, :, :local] = d_keys.astype(LOW).reshape(nc, rows, local)
+            kv_send[:, g, :, local:] = d_values.astype(LOW).reshape(nc, rows, local)
+            d_query = pick(dot(d_scores, keys), heads) * scale
+            dqkv_ref[0, g * rows : (g + 1) * rows] = d_query.astype(LOW)
+        for ahead in range(1, nc):
+            peer = lax.rem(c + ahead, nc)
+            remote(kv_send.at[peer], kv_got.at[new, ahead - 1], kv_sems, (new, ahead - 1), ctx=peer).start()
+        keep_grad(7, dot_tn(dba_ref[...], keep_att[0]))
+        both = kv_send[c].astype(f32)
+        for ahead in range(1, nc):
+            peer = lax.rem(c + ahead, nc)
+            remote(kv_send.at[peer], kv_got.at[new, ahead - 1], kv_sems, (new, ahead - 1), ctx=peer).wait()
+            both = both + kv_got[new, ahead - 1].astype(f32)
+        both = both.reshape(tokens, 2 * local).astype(LOW)
+        dqkv_ref[1] = both[:, :local]
+        dqkv_ref[2] = both[:, local:]
+        part = dot_nt(dqkv_ref[0], matrix(0))
+        part = part + dot_nt(dqkv_ref[1], matrix(1))
+        part = part + dot_nt(dqkv_ref[2], matrix(2))
+        tp_send(part, nt, send_u, first_u, u_sems)
+        normed, _ = norm_parts(keep_h[0])
+        u_in = (normed * (1.0 + mod(1)) + mod(0)).astype(LOW).reshape(tokens, width)
+        for k in range(3):
+            keep_grad(k, dot_tn(u_in, dqkv_ref[k]))
+
+    @pl.when(step >= 2)
+    def _():
+        start_end()
+
+    @pl.when(step < layers)
+    def _():
+        tp_finish(nt, send_u, first_u, full_u, u_sems)
+        normed, inv = norm_parts(keep_h[0])
+        d_h, d_shift, d_scale = norm_back(
+            full_u[...].reshape(count, rows, width).astype(f32), normed, inv, mod(1)
+        )
+        dmods_ref[0, 0] = d_shift
+        dmods_ref[0, 1] = d_scale
+        dh_ref[...] = d_h + dmid_ref[...]
+
+    @pl.when(step == layers - 1)
+    def _():
+        dh_out[...] = dh_ref[...]
+
+    @pl.when((step >= 1) & (step <= layers))
+    def _():
+        start_y()
+
+    @pl.when(step == layers + 1)
+    def _():
+        wait_end(0, new)
+
+
+def backward(mesh, dh0, mods, full, saved):
+    sizes = dict(mesh.shape)
+    nf, nc, nt = sizes["fsdp"], sizes["ctx"], sizes["tp"]
+    chips = nc // 2
+    count, rows, width = dh0.shape
+    layers, blocks, _, _, half, local = full.shape
+    tokens = count * rows
+    f32 = jnp.float32
+
+    def per_layer(array):
+        shape = array.shape[1:]
+        return pl.BlockSpec(
+            (1, *shape), lambda i: (jnp.maximum(layers - 1 - i, 0),) + (0,) * len(shape)
+        )
+
+    anywhere = pl.BlockSpec(memory_space=pl.ANY)
+    vmem = pl.BlockSpec(memory_space=pltpu.VMEM)
+    part = pltpu.VMEM((nt, tokens // nt, width), LOW)
+    first = pltpu.VMEM((nt - 1, tokens // nt, width), LOW)
+    dma = pltpu.SemaphoreType.DMA
+    dmods = jax.ShapeDtypeStruct((layers, 6, count, width), f32)
+    return pl.pallas_call(
+        functools.partial(backward_kernel, sizes),
+        grid=(layers + 2,),
+        out_shape=[
+            jax.ShapeDtypeStruct(dh0.shape, f32),
+            dmods,
+            jax.ShapeDtypeStruct((layers, blocks, 2, half, local), LOW),
+            jax.ShapeDtypeStruct((8, local), f32),
+        ],
+        in_specs=[vmem, vmem, per_layer(full), *(per_layer(s) for s in saved)],
+        out_specs=[vmem, per_layer(dmods), anywhere, vmem],
+        scratch_shapes=[
+            pltpu.VMEM((count, rows, width), f32),
+            pltpu.VMEM((count, rows, width), f32),
+            pltpu.VMEM((4, tokens, local), LOW),
+            pltpu.VMEM((4, tokens, local), LOW),
+            pltpu.VMEM((tokens, width), LOW),
+            pltpu.VMEM((3, tokens, local), LOW),
+            part, first, part, part, first, part,
+            pltpu.VMEM((nc, count, rows, 2 * local), LOW),
+            pltpu.VMEM((2, nc - 1, count, rows, 2 * local), LOW),
+            pltpu.VMEM((2, blocks, nf, 2, half, local), LOW),
+            pltpu.VMEM((2, blocks, nf, half, local), LOW),
+            pltpu.VMEM((max(nf - 1, 1), blocks, half, local), LOW),
+            pltpu.VMEM((2, max(nf - 1, 1), blocks, half, local), LOW),
+            pltpu.VMEM((blocks, half, local), LOW),
+            pltpu.VMEM((2, max(chips - 1, 1), blocks, half, local), LOW),
+            pltpu.VMEM((blocks, half, local), LOW),
+            dma((2, 2, nt - 1)),
+            dma((2, 2, nt - 1)),
+            dma((2, 2, nc - 1)),
+            dma((2, 2, CHUNKS)),
+            dma((2, 2, CHUNKS, max(nf - 1, 1))),
+            dma((2, 2, CHUNKS, max(chips - 1, 1))),
+            dma((2, 2, CHUNKS)),
+            dma((CHUNKS,)),
+        ],
+        compiler_params=pltpu.CompilerParams(
+            collective_id=2, has_side_effects=True, vmem_limit_bytes=60 * 2**20
+        ),
+        cost_estimate=pl.CostEstimate(
+            flops=4 * tokens * width * blocks * local * layers,
+            bytes_accessed=layers * blocks * width * local * 4,
+            transcendentals=0,
+        ),
+        name="backward_layers",
+    )(dh0, mods, full, *saved)
 
 
 def per_device(
@@ -524,7 +782,6 @@
     ).reshape(layers, -1, 2, shard // 2, attend_weight.shape[3])
     spread_mods = jnp.swapaxes(mods, 0, 1)[:, :, None]
     h, full, *saved = forward(mesh, h, spread_mods, low)
-    full = full.reshape(layers, low.shape[1], width, -1)
     final_in = modln(h, mods[:, 6 * layers, None], mods[:, 6 * layers + 1, None]).astype(LOW)
     pred = jnp.einsum("gsd,dp->gsp", final_in, head_full, preferred_element_type=jnp.float32)
     diff = pred - jnp.concatenate([noise, var_target], -1)
@@ -534,41 +791,12 @@
     d_final = jnp.einsum("gsp,dp->gsd", d_pred, head_full, preferred_element_type=jnp.float32)
     _, norm_back = jax.vjp(modln, h, mods[:, 6 * layers, None], mods[:, 6 * layers + 1, None])
     d_h, d_shift_f, d_scale_f = norm_back(d_final)
-    mod_grads = [None] * layers
-    layer_shards = [None] * layers
-    for layer in reversed(range(layers)):
-        weights = tuple(
-            jnp.swapaxes(full[layer, lo:hi], 0, 1) for lo, hi in ((0, 3), (3, 7), (7, 12))
-        )
-        keep_h, keep_mid, keep_a, keep_m, keep_q, keep_kv, keep_p, keep_att, keep_pre = (
-            k[layer] for k in saved
-        )
-        m = mods[:, 6 * layer : 6 * layer + 6]
-        heads = keep_q.shape[-1] // HEAD_DIM
-        both = jnp.swapaxes(keep_kv, 0, 1).reshape(count, -1, 2, heads, HEAD_DIM)
-        probs = keep_p.reshape(count, heads, rows, -1)
-        pre = jnp.swapaxes(keep_pre, 0, 1).reshape(count, rows, -1)
-        kept = (
-            keep_h,
-            modln(keep_h, m[:, 0, None], m[:, 1, None]).astype(LOW),
-            keep_q.reshape(count, rows, heads, HEAD_DIM),
-            both[:, :, 0],
-            both[:, :, 1],
-            probs,
-            probs.astype(LOW),
-            keep_att.reshape(count, rows, -1),
-            keep_a.astype(jnp.float32),
-            keep_mid,
-            modln(keep_mid, m[:, 3, None], m[:, 4, None]).astype(LOW),
-            pre,
-            gelu_tanh(pre).astype(LOW),
-            weights[2][:, 1:].reshape(width, -1),
-            keep_m.astype(jnp.float32),
-        )
-        d_h, mod_grads[layer], grads = layer_backward(kept, m, weights, d_h)
-        layer_shards[layer] = reduce_layer(grads)
-
-    d_mods = jnp.concatenate(mod_grads + [d_shift_f, d_scale_f], 1).reshape(count, -1)
+    d_h, layer_mods, grads, squares = backward(mesh, d_h, spread_mods, full, saved)
+    layer_mods = jnp.moveaxis(layer_mods, 2, 0).reshape(count, 6 * layers, width)
+    d_mods = jnp.concatenate([layer_mods, d_shift_f, d_scale_f], 1).reshape(count, -1)
+    grads = jnp.swapaxes(
+        grads.reshape(layers, low.shape[1], shard, -1).astype(jnp.float32), 1, 2
+    )
     d_cols = lax.dynamic_slice_in_dim(d_mods, lax.axis_index("tp") * columns, columns, 1)
     d_cols = lax.all_gather(lax.psum(d_cols, "ctx"), "fsdp", axis=0, tiled=True)
     d_silu = lax.psum(
@@ -599,9 +827,8 @@
         "cond": d_cols,
     }
 
-    split_sq = sum(jnp.sum(g * g) for parts in layer_shards for g in parts) + rank_square(
-        lefts["cond"], rights["cond"]
-    )
+    chips = lax.axis_size("ctx") // 2
+    split_sq = lax.psum(jnp.sum(squares), "ctx") / chips + rank_square(lefts["cond"], rights["cond"])
     copied_sq = jnp.sum(d_small * d_small) + sum(
         rank_square(lefts[k], rights[k]) for k in ("freq", "time", "label")
     )
@@ -609,9 +836,9 @@
     grad_norm = jnp.sqrt(total_sq)
     clip = jnp.minimum(1.0, CLIP / (grad_norm + 1e-06))
     grads_all = (
-        jnp.stack([s[0] for s in layer_shards]),
-        jnp.stack([s[1] for s in layer_shards]),
-        jnp.stack([s[2] for s in layer_shards]),
+        grads[:, :, 0:3],
+        grads[:, :, 3:7],
+        grads[:, :, 7:12],
         d_small[:, :patch_in],
         rank_sum(lefts["freq"], rights["freq"]),
         rank_sum(lefts["time"], rights["time"]),

time: 1720 us -> 842 us (0.49)
  waiting for transfers between devices: 880 us -> 36.8 us
  Pallas kernels: 193 us -> 464 us
  local copies, waits for them, and re-layouts: 164 us -> 48 us
  other arithmetic: 230 us -> 141 us
  matrix products: 114 us -> 30.9 us
    psum x9 -> x0, waiting for transfers between devices: 432 us -> none  [the longest x1 226 us: reduce_layer(): return [lax.psum(s, 'ctx').astype(jnp.float32) for s in shards]]
    reduce_scatter x16 -> x0, waiting for transfers between devices: 417 us -> none  [the longest x12 343 us: reduce_layer(): lax.psum_scatter(g.astype(LOW), 'fsdp', scatter_dimension=0, tiled=True)]
    pallas_call x0 -> x1, Pallas kernels: none -> 271 us  [backward(): pl.pallas_call(functools.partial(backward_kernel, sizes), grid=(layers +...]
    dot_general x48 -> x0, matrix products: 81.2 us -> none  [the longest x4 12.7 us: layer_backward(): jnp.einsum('gskc,dkc->gsd', d_pre, hidden, preferred_element_type=jnp.flo...]
    slice x15 -> x0, local copies, waits for them, and re-layouts: 36.8 us -> none  [the longest x8 22.9 us: per_device(): weights[2][:, 1:].reshape(width, -1)]
    another operation x19 -> x3, other arithmetic: 26.9 us -> 0.12 us  [the longest x4 7.48 us: layer_backward(): jnp.stack([d_keys.reshape(count, -1, local), d_values.reshape(count, -1,...]
    unnamed x421 -> x72, local copies, waits for them, and re-layouts: 69.7 us -> 46.8 us
    reduce_sum x16 -> x1, other arithmetic: 24.2 us -> 1.3 us  [per_device(): jnp.sum(squares)]
  transfers between devices with their start and end apart: 29 -> 4, of which waited for: 24 -> 2; matrix products, arithmetic and copies ran while one was open for 10% -> 5% of each run, Pallas kernels for 0% -> 0%
where the time goes in v3:
time: 842 us; the launch traced here: 836 us
  Pallas kernels  464 us (55%)
  other arithmetic  141 us (17%)
  blocking collectives  93.5 us (11%)
  local copies, waits for them, and re-layouts  48 us (6%)
  waiting for transfers between devices  36.8 us (4%)
  matrix products  30.9 us (4%)
  between operations  21.9 us (3%)
    pallas_call x1, Pallas kernels, backward(): pl.pallas_call(functools.partial(backward_kernel, sizes), grid=(layers +...  271 us
    pallas_call x1, Pallas kernels, forward(): pl.pallas_call(functools.partial(forward_kernel, sizes), grid=(layers,),...  192 us
    sub x9, other arithmetic, adamw(): weight - RATE * (fixed_mean / (jnp.sqrt(fixed_square) + EPSILON) + DECAY...  102 us
    unnamed x72, local copies, waits for them, and re-layouts  46.8 us
    psum x1, waiting for transfers between devices, per_device(): lax.psum(lax.psum_scatter(jnp.concatenate([d_patch, d_head], 1), 'fsdp',...  30.9 us
    psum x1, blocking collectives, per_device(): lax.psum(split_sq + copied_sq / lax.axis_size('tp'), ('fsdp', 'tp'))  21.9 us
  transfers between devices with their start and end apart: 4, of which 2 were waited for; matrix products, arithmetic and copies ran while one was open for 5% of the time, Pallas kernels for 0%

profile of v3, /device:TPU:0, one launch (start us, length us, event | category | flops | bytes accessed | tf_op | source)
XLA Modules:
  0.0 836.2 jit_solution(9031452111818127951)
XLA Ops:
  11.0 5.2 all-reduce.3
  25.8 6.5 fusion.7
  49.3 8.3 pad_maximum_fusion
  59.2 14.7 %all_gather.22 = f32[2,26624]{1,0:T(2,128)S(1)} all-gather(f32[2,6656]{1,0:T(2,128)S(1)} %constant_dynamic-slice_fusion), channel_id=1, replica_groups=mesh['fsdp'=2,'ctx'=4,'tp'=4] {'tp'}, dimensions={1}, use_global_device_ids=true | all-gather | bytes 266240 | tf_op jit(solution)/shard_map/all_gather | solution.py:771
  74.8 192.5 %forward_layers.1 = (f32[2,64,1024]{2,1,0:T(8,128)}, bf16[4,12,2,2,256,256]{5,4,3,2,1,0:T(8,128)(2,1)}, f32[4,2,64,1024]{3,2,1,0:T(8,128)}, f32[4,2,64,1024]{3,2...) custom-call(f32[2,64,1024]{2,1,0:T(8,128)} %convolution_add_fusion.h, ...), custom_call_target="tpu_custom_call" | custom-call | flops 3221225472 | bytes 50331648 | tf_op jit(solution)/shard_map/forward_layers/pallas_call | solution.py:343
  276.5 271.1 %backward_layers.1 = (f32[2,64,1024]{2,1,0:T(8,128)}, f32[4,6,2,1024]{3,2,1,0:T(2,128)}, bf16[4,12,2,256,256]{4,3,2,1,0:T(8,128)(2,1)}, f32[8,256]{1,0:T(8,128)}) custom-call(f32[2,64,1024]{2,1,0:T(8,128)} %broadcast_add_fusion.dh0_ref, f32[26,2,1,1024]{3,2,1,0:T(1,128)} %broadcast_in_dim.6.mods_ref, ...), custom_call_target="tpu_custom_call" | custom-call | flops 6442450944 | bytes 50331648 | tf_op jit(solution)/shard_map/backward_layers/pallas_call | solution.py:659
  550.2 12.1 %all-reduce.4 = (f32[]{:T(128)}, f32[2,6656]{1,0:T(2,128)S(1)}) all-reduce(f32[]{:T(128)} %reduce_sum.138, f32[2,6656]{1,0:T(2,128)S(1)} %constant_dynamic-slice_fusion.1), channel_id=1, replica_groups=mesh['fsdp'=2,'ctx'=4,'tp'=4] {'ctx'}, use_global_device_ids=true, to_apply=%region_8.9 | all-reduce | flops 13313 | bytes 106504 | tf_op jit(solution)/shard_map/psum | solution.py:831
  562.3 5.2 all-gather
  567.6 8.6 %fusion.5 = f32[4,512]{1,0:T(4,128)S(1)} fusion(f32[4,6656]{1,0:T(4,128)S(1)} %reshape.182, f32[512,6656]{1,0:T(8,128)} %param.58), kind=kOutput, calls=%fused_computation.27 | convolution fusion | flops 166985728 | bytes 13746176 | tf_op jit(solution)/shard_map/dot_general | solution.py:803
  576.1 12.7 %psum.46 = f32[4,512]{1,0:T(4,128)S(1)} all-reduce(f32[4,512]{1,0:T(4,128)S(1)} %fusion.5), channel_id=1, replica_groups=mesh['fsdp'=2,'ctx'=4,'tp'=4] {'tp'}, use_global_device_ids=true, to_apply=%region_16.17 | all-reduce | flops 2048 | bytes 16384 | tf_op jit(solution)/shard_map/psum | solution.py:802
  593.6 14.1 %convert_bitcast_fusion = f32[4,512,12,256]{3,1,2,0:T(8,128)} fusion(bf16[4,12,2,256,256]{4,3,2,1,0:T(8,128)(2,1)} %get-tuple-element.58), kind=kLoop, calls=%fused_computation | loop fusion | flops 6291456 | bytes 37748736 | tf_op jit(solution)/shard_map/transpose | solution.py:797
  609.2 12.4 %psum.42 = f32[]{:T(128)} all-reduce(f32[]{:T(128)} %get-tuple-element.198), channel_id=1, replica_groups=mesh['fsdp'=2,'ctx'=4,'tp'=4] {'fsdp','ctx'}, use_global_device_ids=true, to_apply=%region_4.5 | all-reduce | flops 1 | bytes 8 | tf_op jit(solution)/shard_map/psum | solution.py:788
  624.2 5.8 reduce-scatter.5.cloned.1.call-done
  632.7 30.9 %all-reduce.8.cloned.1.call-done = f32[512,48]{0,1:T(8,128)} async-done(((f32[512,48]{0,1:T(8,128)}), f32[512,48]{0,1:T(8,128)}) %all-reduce.8.cloned.1.call-update) | async-done | bytes 98320 | tf_op jit(solution)/shard_map/psum | solution.py:816
  665.8 21.9 %psum.47 = f32[]{:T(128)} all-reduce(f32[]{:T(128)S(6)} %add.310), channel_id=1, replica_groups=mesh['fsdp'=2,'ctx'=4,'tp'=4] {'fsdp','tp'}, use_global_device_ids=true, to_apply=%region_21.22 | all-reduce | flops 1 | bytes 8 | tf_op jit(solution)/shard_map/psum | solution.py:835
  688.5 21.4 %multiply_subtract_fusion.2 = (f32[4,512,4,256]{3,1,2,0:T(8,128)}, f32[4,512,4,256]{3,1,2,0:T(8,128)}, f32[4,512,4,256]{3,1,2,0:T(8,128)}) fusion(f32[4,512,4,256]{3,2,1,0:T(4,128)} %param.40, f32[]{:T(128)S(6)} %min.3, f32[4,512,12,256]{3,1,2,0:T(8,128)} %convert_bitcast_fusion, f32[4,512,4,256]{3,2,1,0:T(4,128)} %param.41, f32[4,512,4,256]{3,2,1,0:T(4,128)} %param.42), kind=kLoop, calls=%fused_computation.20 | loop fusion | flops 31457280 | bytes 58720260 | tf_op jit(solution)/shard_map/sub | solution.py:65
  709.9 12.2 %copy.74 = f32[4,512,4,256]{3,2,1,0:T(4,128)} copy(f32[4,512,4,256]{3,1,2,0:T(8,128)} %get-tuple-element.150) | data formatting | bytes 16777216
  722.1 12.2 %copy.75 = f32[4,512,4,256]{3,2,1,0:T(4,128)} copy(f32[4,512,4,256]{3,1,2,0:T(8,128)} %get-tuple-element.151) | data formatting | bytes 16777216
  734.2 12.5 %copy.76 = f32[4,512,4,256]{3,2,1,0:T(4,128)} copy(f32[4,512,4,256]{3,1,2,0:T(8,128)} %get-tuple-element.152) | data formatting | bytes 16777216
  746.8 17.2 %multiply_subtract_fusion.3 = (f32[4,512,3,256]{3,1,2,0:T(8,128)}, f32[4,512,3,256]{3,1,2,0:T(8,128)}, f32[4,512,3,256]{3,1,2,0:T(8,128)}) fusion(f32[4,512,3,256]{3,1,2,0:T(8,128)} %param.37, f32[]{:T(128)S(6)} %min.3, f32[4,512,12,256]{3,1,2,0:T(8,128)} %convert_bitcast_fusion, f32[4,512,3,256]{3,1,2,0:T(8,128)} %param.38, f32[4,512,3,256]{3,1,2,0:T(8,128)} %param.39), kind=kLoop, calls=%fused_computation.24 | loop fusion | flops 23592960 | bytes 44040196 | tf_op jit(solution)/shard_map/sub | solution.py:65
  764.1 22.1 %multiply_subtract_fusion.1 = (f32[4,512,5,256]{3,1,2,0:T(8,128)}, f32[4,512,5,256]{3,1,2,0:T(8,128)}, f32[4,512,5,256]{3,1,2,0:T(8,128)}) fusion(f32[4,512,5,256]{3,1,2,0:T(8,128)S(1)} %bitcast.92, f32[]{:T(128)S(6)} %min.3, f32[4,512,12,256]{3,1,2,0:T(8,128)} %convert_bitcast_fusion, f32[4,512,5,256]{3,1,2,0:T(8,128)} %param.44, f32[4,512,5,256]{3,1,2,0:T(8,128)} %param.45), kind=kLoop, calls=%fused_computation.13 | loop fusion | flops 39321600 | bytes 73400320 | tf_op jit(solution)/shard_map/sub | solution.py:65
  786.2 5.1 multiply_subtract_fusion.4
  791.4 6.8 multiply_subtract_fusion.5
  800.0 26.7 %multiply_subtract_fusion = (f32[512,6656]{1,0:T(8,128)}, f32[512,6656]{1,0:T(8,128)}, f32[512,6656]{1,0:T(8,128)}) fusion(f32[512,6656]{1,0:T(8,128)S(1)} %bitcast.89, f32[]{:T(128)S(6)} %min.3, f32[6656]{0:T(1024)S(1)} %get-tuple-element.122, f32[512]{0:T(512)S(1)} %bitcast.123, f32[6656]{0:T(1024)S(1)} %get-tuple-element.123, f32[512]{0:T(512)S(1)} %bitcast.122, ...), kind=kLoop, calls=%fused_computation.6 | loop fusion | flops 74973184 | bytes 81903616 | tf_op jit(solution)/shard_map/sub | solution.py:65
  (143 shorter events, 56.1 us)
Async XLA Ops:
  7.2 51.1 %all-reduce.10.cloned.1.call-start = ((), (), s32[]{:S(2)}) async-start(), calls=%async_computation.5 | async-start | bytes 212992
  32.3 590.6 %reduce-scatter.7.cloned.1.call-start = ((), (), s32[]{:S(2)}) async-start(), calls=%async_computation.4 | async-start | bytes 786432
  32.6 14.6 %slice-start.7 = ((s8[6291456]{0:T(1024)(128)(4,1)}), s8[2097152]{0:T(1024)(128)(4,1)S(1)}, s32[]{:S(2)}) async-start(s8[6291456]{0:T(1024)(128)(4,1)} %bitcast.93), calls=%async_computation.13 | async-start | bytes 4194304
  37.7 9.5 %slice-start.8 = ((s8[6291456]{0:T(1024)(128)(4,1)}), s8[4194304]{0:T(1024)(128)(4,1)S(1)}, s32[]{:S(2)}) async-start(s8[6291456]{0:T(1024)(128)(4,1)} %bitcast.93), calls=%async_computation.14 | async-start | bytes 8388608
  74.8 194.9 %copy-start.19 = (f32[2,64,16]{1,2,0:T(8,128)S(1)}, f32[2,64,16]{1,2,0:T(8,128)}, u32[]{:S(2)}) copy-start(f32[2,64,16]{1,2,0:T(8,128)} %param.34) | copy-start | bytes 24580
  276.5 273.4 %copy-start = (f32[2,64,1024]{2,1,0:T(8,128)S(1)}, f32[2,64,1024]{2,1,0:T(8,128)}, u32[]{:S(2)}) copy-start(f32[2,64,1024]{2,1,0:T(8,128)} %get-tuple-element.44) | copy-start | bytes 1572868
  567.6 21.3 %copy-start.1 = (f32[512,1024]{1,0:T(8,128)S(1)}, f32[512,1024]{1,0:T(8,128)}, u32[]{:S(2)}) copy-start(f32[512,1024]{1,0:T(8,128)} %param.52) | copy-start | bytes 6291460
  567.6 24.9 %copy-start.7 = (f32[2,64,1024]{2,1,0:T(8,128)S(1)}, f32[2,64,1024]{2,1,0:T(8,128)}, u32[]{:S(2)}) copy-start(f32[2,64,1024]{2,1,0:T(8,128)} %get-tuple-element.57) | copy-start | bytes 1572868
  592.8 37.2 %reduce-scatter.5.cloned.1.call-start = ((), (), s32[]{:S(2)}) async-start(), calls=%async_computation.2 | async-start | bytes 294912 | tf_op jit(solution)/shard_map/reduce_scatter | solution.py:817
  622.9 40.7 %all-reduce.8.cloned.1.call-start = ((), (), s32[]{:S(2)}) async-start(), calls=%async_computation.3 | async-start | bytes 196608 | tf_op jit(solution)/shard_map/psum | solution.py:816
  734.2 29.8 %slice-start.4 = ((s8[10485760]{0:T(1024)(128)(4,1)}), s8[2097152]{0:T(1024)(128)(4,1)S(1)}, s32[]{:S(2)}) async-start(s8[10485760]{0:T(1024)(128)(4,1)} %bitcast.91), calls=%async_computation.10 | async-start | bytes 4194304
  746.8 17.2 %slice-start.5 = ((s8[10485760]{0:T(1024)(128)(4,1)}), s8[4194304]{0:T(1024)(128)(4,1)S(1)}, s32[]{:S(2)}) async-start(s8[10485760]{0:T(1024)(128)(4,1)} %bitcast.91), calls=%async_computation.11 | async-start | bytes 8388608
  746.8 17.2 %slice-start.6 = ((s8[10485760]{0:T(1024)(128)(4,1)}), s8[4194304]{0:T(1024)(128)(4,1)S(1)}, s32[]{:S(2)}) async-start(s8[10485760]{0:T(1024)(128)(4,1)} %bitcast.91), calls=%async_computation.12 | async-start | bytes 8388608
  764.0 22.1 %copy-start.4 = (f32[512,1024]{1,0:T(8,128)S(1)}, f32[512,1024]{1,0:T(8,128)}, u32[]{:S(2)}) copy-start(f32[512,1024]{1,0:T(8,128)} %param.53) | copy-start | bytes 6291460
  764.0 22.1 %copy-start.5 = (f32[512,1024]{1,0:T(8,128)S(1)}, f32[512,1024]{1,0:T(8,128)}, u32[]{:S(2)}) copy-start(f32[512,1024]{1,0:T(8,128)} %param.54) | copy-start | bytes 6291460
  786.2 13.7 %slice-start = ((s8[13631488]{0:T(1024)(128)(4,1)}), s8[4194304]{0:T(1024)(128)(4,1)S(1)}, s32[]{:S(2)}) async-start(s8[13631488]{0:T(1024)(128)(4,1)} %bitcast.88), calls=%async_computation.6 | async-start | bytes 8388608
  786.2 13.7 %slice-start.1 = ((s8[13631488]{0:T(1024)(128)(4,1)}), s8[4194304]{0:T(1024)(128)(4,1)S(1)}, s32[]{:S(2)}) async-start(s8[13631488]{0:T(1024)(128)(4,1)} %bitcast.88), calls=%async_computation.7 | async-start | bytes 8388608
  791.3 8.6 %slice-start.2 = ((s8[13631488]{0:T(1024)(128)(4,1)}), s8[4194304]{0:T(1024)(128)(4,1)S(1)}, s32[]{:S(2)}) async-start(s8[13631488]{0:T(1024)(128)(4,1)} %bitcast.88), calls=%async_computation.8 | async-start | bytes 8388608
  791.3 8.6 %slice-start.3 = ((s8[13631488]{0:T(1024)(128)(4,1)}), s8[1048576]{0:T(1024)(128)(4,1)S(1)}, s32[]{:S(2)}) async-start(s8[13631488]{0:T(1024)(128)(4,1)} %bitcast.88), calls=%async_computation.9 | async-start | bytes 2097152
  799.9 26.8 %copy-start.10 = (f32[512,48]{0,1:T(8,128)S(1)}, f32[512,48]{0,1:T(8,128)}, u32[]{:S(2)}) copy-start(f32[512,48]{0,1:T(8,128)} %all-reduce.8.cloned.1.call-done) | copy-start | bytes 294916
  799.9 26.8 %copy-start.15 = (f32[512,16]{0,1:T(8,128)S(1)}, f32[512,16]{0,1:T(8,128)}, u32[]{:S(2)}) copy-start(f32[512,16]{0,1:T(8,128)} %param.47) | copy-start | bytes 98308
  800.0 26.8 %copy-start.16 = (f32[512,16]{0,1:T(8,128)S(1)}, f32[512,16]{0,1:T(8,128)}, u32[]{:S(2)}) copy-start(f32[512,16]{0,1:T(8,128)} %param.48) | copy-start | bytes 98308
  800.0 27.4 %copy-start.13 = (f32[512,32]{0,1:T(8,128)S(1)}, f32[512,32]{0,1:T(8,128)}, u32[]{:S(2)}) copy-start(f32[512,32]{0,1:T(8,128)} %param.62) | copy-start | bytes 196612
  800.0 27.4 %copy-start.14 = (f32[512,32]{0,1:T(8,128)S(1)}, f32[512,32]{0,1:T(8,128)}, u32[]{:S(2)}) copy-start(f32[512,32]{0,1:T(8,128)} %param.63) | copy-start | bytes 196612
  (10 other events, 53.2 us)
Sparse Core Ops, SparseCore 0:
  32.5 22.8 all-reduce.9
  592.9 11.0 reduce-scatter.6
  623.0 6.9 reduce-scatter.4
  632.3 31.2 all-reduce.7

commit v4 on v1

v4 whole, which is shorter than its diff:
```python
import functools
import math

import jax
import jax.numpy as jnp
from jax import lax
from jax.experimental import pallas as pl
from jax.experimental.pallas import tpu as pltpu
from jax.sharding import PartitionSpec as P

HEAD_DIM = 64
FREQ = 256
GRID = 16
STEP = 5


HIGH = lax.Precision.HIGHEST
RATE = 0.05
DECAY = 0.1
BETA = 0.5
EPSILON = 1e-08
CLIP = 1.0
LOW = jnp.bfloat16


def modln(h, shift, scale):
    mean = jnp.mean(h, -1, keepdims=True)
    cent = h - mean
    var = jnp.mean(cent * cent, -1, keepdims=True)
    return cent * lax.rsqrt(var + 1e-06) * (1.0 + scale) + shift


def gelu_tanh(v):
    return jax.nn.gelu(v, approximate=True)


def noise_level(steps):
    phase = (steps.astype(jnp.float32) / 1000.0 + 0.008) / 1.008 * (0.5 * math.pi)
    return jnp.cos(phase) ** 2


def time_freqs(steps):
    half = FREQ // 2
    rates = jnp.exp(-math.log(10000.0) * jnp.arange(half, dtype=jnp.float32) / half)
    angles = steps.astype(jnp.float32)[:, None] * rates[None, :]
    return jnp.concatenate([jnp.cos(angles), jnp.sin(angles)], -1)


def positions(first, count, width):
    index = first + jnp.arange(count, dtype=jnp.int32)
    row = (index // GRID).astype(jnp.float32)
    column = (index % GRID).astype(jnp.float32)
    quarter = width // 4
    rates = jnp.power(10000.0, -jnp.arange(quarter, dtype=jnp.float32) / quarter)
    across = column[:, None] * rates[None, :]
    down = row[:, None] * rates[None, :]
    return jnp.concatenate([jnp.sin(across), jnp.cos(across), jnp.sin(down), jnp.cos(down)], -1)


def adamw(weight, mean, square, grad):
    mean_next = BETA * mean + (1.0 - BETA) * grad
    square_next = BETA * square + (1.0 - BETA) * grad * grad
    fixed_mean = mean_next / (1.0 - BETA**STEP)
    fixed_square = square_next / (1.0 - BETA**STEP)
    weight_next = weight - RATE * (fixed_mean / (jnp.sqrt(fixed_square) + EPSILON) + DECAY * weight)
    return [weight_next, mean_next, square_next]


def rank_sum(left, right):
    total = left[0][:, None] * right[0][None, :]
    for k in range(1, left.shape[0]):
        total = total + left[k][:, None] * right[k][None, :]
    return total


MESH = pl.DeviceIdType.MESH
GROUPS = ((4, 4), (0, 4), (8, 4))
QUERY, KEY, VALUE, OUT, HIDDEN, MLP = 4, 5, 6, 7, 0, 8
LANES = 128


def dot(left, right):
    return jnp.dot(left, right, preferred_element_type=jnp.float32)


def dot_nt(left, right):
    return lax.dot_general(left, right, (((1,), (1,)), ((), ())), preferred_element_type=jnp.float32)


def dot_tn(left, right):
    return lax.dot_general(left, right, (((0,), (0,)), ((), ())), preferred_element_type=jnp.float32)


def remote(src, dst, sems, where, **device):
    send, recv = (sems.at[(0, *where)], sems.at[(1, *where)])
    return pltpu.make_async_remote_copy(
        src_ref=src, dst_ref=dst, send_sem=send, recv_sem=recv, device_id=device, device_id_type=MESH
    )


def meet(sizes):
    barrier = pltpu.get_barrier_semaphore()
    count = 0
    for axis, size in sizes.items():
        for step in range(1, size):
            peer = lax.rem(lax.axis_index(axis) + step, size)
            pl.semaphore_signal(barrier, inc=1, device_id={axis: peer}, device_id_type=MESH)
            count += 1
    pl.semaphore_wait(barrier, count)


def norm_parts(h):
    mean = jnp.mean(h, -1, keepdims=True)
    cent = h - mean
    var = jnp.mean(cent * cent, -1, keepdims=True)
    inv = lax.rsqrt(var + 1e-06)
    return cent * inv, inv


def norm_back(grad, normed, inv, scale):
    grad_shift = jnp.sum(grad, 0, keepdims=True)
    grad_scale = jnp.sum(grad * normed, 0, keepdims=True)
    inner = grad * (1.0 + scale)
    mean = jnp.mean(inner, -1, keepdims=True)
    along = jnp.mean(inner * normed, -1, keepdims=True)
    return inv * (inner - mean - normed * along), grad_shift, grad_scale


class Total:
    def __init__(self, size, g, send, first, full, sems):
        self.size, self.g, self.sems = size, g, sems
        self.send, self.first, self.full = send.at[g], first.at[g], full.at[g]
        self.me = lax.axis_index("tp")

    def peer(self, ahead):
        return lax.rem(self.me + ahead, self.size)

    def one(self, ahead):
        peer = self.peer(ahead)
        return remote(
            self.send.at[peer], self.first.at[ahead - 1], self.sems, (0, self.g, ahead - 1), tp=peer
        )

    def two(self, block, ahead):
        block = self.full.at[block]
        return remote(block, block, self.sems, (1, self.g, ahead - 1), tp=self.peer(ahead))

    def scatter(self, part):
        self.send[...] = part.astype(LOW).reshape(self.send.shape)
        for ahead in range(1, self.size):
            self.one(ahead).start()

    def share(self):
        total = self.send[self.me].astype(jnp.float32)
        for ahead in range(1, self.size):
            self.one(ahead).wait()
            total = total + self.first[ahead - 1].astype(jnp.float32)
        self.full[self.me] = total.astype(LOW)
        for ahead in range(1, self.size):
            self.two(self.me, ahead).start()

    def get(self):
        for ahead in range(1, self.size):
            self.two(self.me, ahead).wait_send()
            self.two(lax.rem(self.me + self.size - ahead, self.size), ahead).wait_recv()
        size, rows, width = self.full.shape
        return self.full[...].reshape(size * rows, width)


def spread(block, heads):
    lane = lax.broadcasted_iota(jnp.int32, block.shape, 1) // HEAD_DIM
    zero = jnp.zeros_like(block)
    return jnp.concatenate([jnp.where(lane == k, block, zero) for k in range(heads)], 0)


def pick(stacked, heads):
    rows = stacked.shape[0] // heads
    lane = lax.broadcasted_iota(jnp.int32, (rows, stacked.shape[1]), 1) // HEAD_DIM
    total = jnp.zeros((rows, stacked.shape[1]), stacked.dtype)
    for k in range(heads):
        total = jnp.where(lane == k, stacked[k * rows : (k + 1) * rows], total)
    return total


ROOT_2_PI = math.sqrt(2.0 / math.pi)


def gelu_parts(v):
    inside = jnp.tanh(ROOT_2_PI * (v + 0.044715 * (v * v * v)))
    value = v * (0.5 * (1.0 + inside))
    slope = 0.5 * (1.0 + inside) + 0.5 * v * (1.0 - inside * inside) * ROOT_2_PI * (
        1.0 + 3 * 0.044715 * v * v
    )
    return value, slope


def row(ref, g, index, width):
    return ref[g : g + 1, pl.ds(pl.multiple_of(index * width, LANES), width)]


def put_row(ref, g, index, width, value):
    ref[g : g + 1, pl.ds(pl.multiple_of(index * width, LANES), width)] = value


def interleave(blocks, tiles, back=False):
    size = blocks * tiles * 16
    to = lax.broadcasted_iota(jnp.int32, (size, size), 1 if back else 0)
    source = lax.broadcasted_iota(jnp.int32, (size, size), 0 if back else 1)
    block, tile, at = to % blocks, (to // blocks) % tiles, to // (blocks * tiles)
    return jnp.where(source == (block * tiles + tile) * 16 + at, 1.0, 0.0).astype(LOW)


def forward_kernel(
    sizes, h0_ref, part_ref, hidden_ref, attend_ref, output_ref, h_out, mods_out, full_ref,
    keep_h, keep_mid, keep_a, keep_m, keep_q, keep_kv, keep_p, keep_att, keep_pre,
    weights, stage_h, stage_a, stage_o, kv, h_ref, q_ref, mods_ref, mods_got, send_a, first_a, full_a, send_m, first_m, full_m,
    x_sems, y_sems, pair_sems, own_sems, kv_sems, a_sems, m_sems, mods_x_sems, mods_t_sems,
):
    nf, nc, nt = sizes["fsdp"], sizes["ctx"], sizes["tp"]
    chips = nc // 2
    step = pl.program_id(0)
    layers = attend_ref.shape[0]
    f, c, t = lax.axis_index("fsdp"), lax.axis_index("ctx"), lax.axis_index("tp")
    core, chip = lax.rem(c, 2), c // 2
    sibling = c + 1 - 2 * core
    count, rows, width = h_ref.shape
    local = weights.shape[-1]
    heads = local // HEAD_DIM
    scale = 1.0 / math.sqrt(HEAD_DIM)
    columns = part_ref.shape[-1]

    def blocks(k):
        return pl.ds(*GROUPS[k])

    def x_copy(layer, k, ahead):
        return remote(
            weights.at[layer, blocks(k), f, chip, core],
            weights.at[layer, blocks(k), f, chip, core],
            x_sems,
            (layer, k, ahead - 1),
            fsdp=lax.rem(f + ahead, nf),
        )

    def x_arrived(layer, k, ahead):
        source = lax.rem(f + nf - ahead, nf)
        block = weights.at[layer, blocks(k), source, chip, core]
        remote(block, block, x_sems, (layer, k, ahead - 1), fsdp=source).wait_recv()

    def y_copy(layer, k, ahead, over, at):
        source = lax.rem(f + nf - ahead, nf)
        block = weights.at[layer, blocks(k), source, at, core]
        peer = lax.rem(chip + over, chips) * 2 + core
        return remote(block, block, y_sems, (layer, k, ahead - 1, over - 1), ctx=peer)

    def pair_copy(layer, k, ahead, half):
        source = lax.rem(f + nf - ahead, nf)
        block = weights.at[layer, blocks(k), source, :, half]
        return remote(block, block, pair_sems, (layer, k, ahead - 1), ctx=sibling)

    def pass_y(layer, k):
        for ahead in range(1, nf):
            x_arrived(layer, k, ahead)
            for over in range(1, chips):
                y_copy(layer, k, ahead, over, chip).start()

    def pass_pair(layer, k):
        for ahead in range(1, nf):
            for over in range(1, chips):
                y_copy(layer, k, ahead, over, lax.rem(chip + chips - over, chips)).wait_recv()
            pair_copy(layer, k, ahead, core).start()

    def arrived(layer, k):
        for ahead in range(1, nf):
            pair_copy(layer, k, ahead, 1 - core).wait_recv()

    def stage_copies(layer):
        return [
            pltpu.make_async_copy(source.at[layer], stage, own_sems.at[1 + k])
            for k, (source, stage) in enumerate(
                ((attend_ref, stage_a), (hidden_ref, stage_h), (output_ref, stage_o))
            )
        ]

    def quarters(value):
        return value.astype(LOW).reshape(chips, 2, -1, local)

    def send_x(layer, k):
        for ahead in range(1, nf):
            x_copy(layer, k, ahead).start()

    def lower(layer):
        copies = stage_copies(layer)
        copies[0].wait()
        copies[2].wait()
        for k in range(3):
            weights[layer, QUERY + k, f] = quarters(stage_a[k])
        weights[layer, OUT, f] = quarters(stage_o[0])
        send_x(layer, 0)
        copies[1].wait()
        tiles = local // LANES
        size = 4 * tiles * 16
        order = interleave(4, tiles, back=True)
        quarter = weights.shape[-2]

        def split(r, carry):
            rows_in = pl.ds(pl.multiple_of(r * size, size), size)
            value = dot(order, stage_h[rows_in].astype(LOW)).astype(LOW)
            part = (r * 16) // quarter
            at = pl.ds(pl.multiple_of(lax.rem(r * 16, quarter), 16), 16)
            for k in range(4):
                for n in range(tiles):
                    first = (k * tiles + n) * 16
                    weights[
                        layer, HIDDEN + k, f, part // 2, lax.rem(part, 2), at, n * LANES : (n + 1) * LANES
                    ] = value[first : first + 16]
            return carry

        lax.fori_loop(0, stage_h.shape[0] // size, split, 0, unroll=2)
        send_x(layer, 1)
        for k in range(4):
            weights[layer, MLP + k, f] = quarters(stage_o[1 + k])
        send_x(layer, 2)

    def store_copy(layer):
        return pltpu.make_async_copy(weights.at[layer], full_ref.at[layer], own_sems.at[4 + layer])

    def share_mods():
        for ahead in range(1, nf):
            peer = lax.rem(f + ahead, nf)
            remote(part_ref.at[peer], mods_got.at[ahead - 1], mods_x_sems, (ahead - 1,), fsdp=peer).start()

    def finish_mods():
        total = part_ref[f]
        for ahead in range(1, nf):
            peer = lax.rem(f + ahead, nf)
            remote(part_ref.at[peer], mods_got.at[ahead - 1], mods_x_sems, (ahead - 1,), fsdp=peer).wait()
            total = total + mods_got[ahead - 1]

        def at(k):
            return mods_ref.at[:, pl.ds(pl.multiple_of(k * columns, LANES), columns)]

        mods_ref[:, pl.ds(pl.multiple_of(t * columns, LANES), columns)] = total
        for ahead in range(1, nt):
            remote(at(t), at(t), mods_t_sems, (ahead - 1,), tp=lax.rem(t + ahead, nt)).start()
        for ahead in range(1, nt):
            source = lax.rem(t + nt - ahead, nt)
            remote(at(t), at(t), mods_t_sems, (ahead - 1,), tp=source).wait_send()
            remote(at(source), at(source), mods_t_sems, (ahead - 1,), tp=source).wait_recv()

    def mod(k, g, layer):
        return row(mods_ref, g, 6 * layer + k, width)

    def total_a(g):
        return Total(nt, g, send_a, first_a, full_a, a_sems)

    def total_m(g):
        return Total(nt, g, send_m, first_m, full_m, m_sems)

    def kv_copy(layer, g, ahead, at):
        block = kv.at[layer, g, at]
        return remote(block, block, kv_sems, (layer, g, ahead - 1), ctx=lax.rem(c + ahead, nc))

    @pl.when(step == 0)
    def _():
        for copy in stage_copies(0):
            copy.start()
        meet(sizes)
        share_mods()
        lower(0)
        for copy in stage_copies(1):
            copy.start()
        h_ref[...] = h0_ref[...]
        finish_mods()
        pass_y(0, 0)
        pass_pair(0, 0)
        pass_y(0, 1)

    def matrix(k):
        return weights[step, k].reshape(width, local)

    def begin(g):
        h = h_ref[g]
        keep_h[0, g] = h
        normed, _ = norm_parts(h)
        u_in = (normed * (1.0 + mod(1, g, step)) + mod(0, g, step)).astype(LOW)
        kv[step, g, c, :, :local] = dot(u_in, matrix(KEY)).astype(LOW)
        kv[step, g, c, :, local:] = dot(u_in, matrix(VALUE)).astype(LOW)
        for ahead in range(1, nc):
            kv_copy(step, g, ahead, c).start()
        q_ref[g] = dot(u_in, matrix(QUERY)).astype(LOW)

    def last_branch(g):
        branch = total_m(g).get()
        keep_m[0, g] = branch
        h_ref[g] = h_ref[g] + mod(5, g, step - 1) * branch.astype(jnp.float32)

    @pl.when(step < layers)
    def _():
        arrived(step, 0)

    for g in range(count):

        @pl.when(step >= 1)
        def _():
            last_branch(g)

        @pl.when(step < layers)
        def _():
            begin(g)

    @pl.when(step + 1 < layers)
    def _():
        lower(step + 1)

    @pl.when(step + 2 < layers)
    def _():
        for copy in stage_copies(step + 2):
            copy.start()

    @pl.when(step < layers)
    def _():
        pass_y(step, 2)
        pass_pair(step, 1)
        for g in range(count):
            for ahead in range(1, nc):
                kv_copy(step, g, ahead, c).wait_send()
                kv_copy(step, g, ahead, lax.rem(c + nc - ahead, nc)).wait_recv()
            keep_q[0, g] = q_ref[g]
            keep_kv[0, g] = kv[step, g]
            keys = kv[step, g, :, :, :local].reshape(nc * rows, local)
            values = kv[step, g, :, :, local:].reshape(nc * rows, local)
            scores = dot_nt(spread(q_ref[g], heads), keys) * scale
            expo = jnp.exp(scores - jnp.max(scores, -1, keepdims=True))
            probs = expo / jnp.sum(expo, -1, keepdims=True)
            keep_p[0, g] = probs
            attended = pick(dot(probs.astype(LOW), values), heads).astype(LOW)
            keep_att[0, g] = attended
            total_a(g).scatter(dot_nt(attended, matrix(OUT)))
        pass_pair(step, 2)
        for g in range(count):
            total_a(g).share()
        arrived(step, 1)

    @pl.when(step + 1 < layers)
    def _():
        pass_y(step + 1, 0)

    @pl.when(step < layers)
    def _():
        for g in range(count):
            branch = total_a(g).get()
            keep_a[0, g] = branch
            h_mid = h_ref[g] + mod(2, g, step) * branch.astype(jnp.float32)
            keep_mid[0, g] = h_mid
            h_ref[g] = h_mid
            normed, _ = norm_parts(h_mid)
            w_in = (normed * (1.0 + mod(4, g, step)) + mod(3, g, step)).astype(LOW)
            if g == 0:
                arrived(step, 2)
                store_copy(step).start()
            part = jnp.zeros((rows, width), jnp.float32)
            for k in range(4):
                pre = dot(w_in, matrix(HIDDEN + k))
                keep_pre[0, g, k] = pre
                part = part + dot_nt(gelu_parts(pre)[0].astype(LOW), matrix(MLP + k))
            total_m(g).scatter(part)

    @pl.when(step + 1 < layers)
    def _():
        pass_pair(step + 1, 0)
        pass_y(step + 1, 1)

    @pl.when(step < layers)
    def _():
        for g in range(count):
            total_m(g).share()

    @pl.when(step == layers)
    def _():
        h_out[...] = h_ref[...]
        mods_out[...] = mods_ref[...]

        def drain(layer, carry):
            store_copy(layer).wait()
            for k in range(len(GROUPS)):
                for ahead in range(1, nf):
                    x_copy(layer, k, ahead).wait_send()
                    for over in range(1, chips):
                        y_copy(layer, k, ahead, over, chip).wait_send()
                    pair_copy(layer, k, ahead, core).wait_send()
            return carry

        lax.fori_loop(0, layers, drain, 0)


def forward(mesh, h0, part, hidden, attend, output):
    sizes = dict(mesh.shape)
    nf, nc, nt = sizes["fsdp"], sizes["ctx"], sizes["tp"]
    chips = nc // 2
    count, rows, width = h0.shape
    layers, _, shard, local = attend.shape
    blocks, quarter = 4 + attend.shape[1] + output.shape[1], shard // nc
    heads = local // HEAD_DIM
    tokens = count * rows
    others, overs = max(nf - 1, 1), max(chips - 1, 1)
    f32 = jnp.float32

    def kept(shape, dtype, late=0):
        spec = pl.BlockSpec(
            (1, *shape), lambda i: (jnp.clip(i - late, 0, layers - 1),) + (0,) * len(shape)
        )
        return jax.ShapeDtypeStruct((layers, *shape), dtype), spec

    saves = [
        kept((count, rows, width), f32),
        kept((count, rows, width), f32),
        kept((count, rows, width), LOW),
        kept((count, rows, width), LOW, 1),
        kept((count, rows, local), LOW),
        kept((count, nc, rows, 2 * local), LOW),
        kept((count, heads * rows, nc * rows), f32),
        kept((count, rows, local), LOW),
        kept((count, 4, rows, local), f32),
    ]
    anywhere = pl.BlockSpec(memory_space=pl.ANY)
    vmem = pl.BlockSpec(memory_space=pltpu.VMEM)
    whole = pltpu.VMEM((count, nt, rows // nt, width), LOW)
    first = pltpu.VMEM((count, nt - 1, rows // nt, width), LOW)
    dma = pltpu.SemaphoreType.DMA
    return pl.pallas_call(
        functools.partial(forward_kernel, sizes),
        grid=(layers + 1,),
        out_shape=[
            jax.ShapeDtypeStruct(h0.shape, f32),
            jax.ShapeDtypeStruct((count, nt * part.shape[-1]), f32),
            jax.ShapeDtypeStruct((layers, blocks, nf, chips, 2, quarter, local), LOW),
            *(shape for shape, _ in saves),
        ],
        in_specs=[vmem, vmem, anywhere, anywhere, anywhere],
        out_specs=[vmem, vmem, anywhere, *(spec for _, spec in saves)],
        scratch_shapes=[
            pltpu.VMEM((layers, blocks, nf, chips, 2, quarter, local), LOW),
            *(pltpu.VMEM(w.shape[1:], f32) for w in (hidden, attend, output)),
            pltpu.VMEM((layers, count, nc, rows, 2 * local), LOW),
            pltpu.VMEM((count, rows, width), f32),
            pltpu.VMEM((count, rows, local), LOW),
            pltpu.VMEM((count, nt * part.shape[-1]), f32),
            pltpu.VMEM((others, count, part.shape[-1]), f32),
            whole, first, whole, whole, first, whole,
            dma((2, layers, 3, others)),
            dma((2, layers, 3, others, overs)),
            dma((2, layers, 3, others)),
            dma((4 + layers,)),
            dma((2, layers, count, nc - 1)),
            dma((2, 2, count, nt - 1)),
            dma((2, 2, count, nt - 1)),
            dma((2, others)),
            dma((2, nt - 1)),
        ],
        compiler_params=pltpu.CompilerParams(
            collective_id=1, has_side_effects=True, vmem_limit_bytes=56 * 2**20
        ),
        cost_estimate=pl.CostEstimate(
            flops=2 * tokens * width * blocks * local * layers,
            bytes_accessed=layers * blocks * width * local * 4,
            transcendentals=0,
        ),
        name="forward_layers",
    )(h0, part, hidden, attend, output)


def halves(value):
    high = value.astype(LOW).astype(jnp.float32)
    return high, value - high


def backward_kernel(
    sizes, images, dh0_ref, mods_ref, dmods_end_ref, loss_ref, noisy_ref, dpred_ref, final_ref,
    slope_c_ref, slope_a_ref, gram_c_ref, gram_t_ref, gram_f_ref, time_ref, cond_ref,
    w_ref, keep_h, keep_mid, keep_a, keep_m, keep_q, keep_kv, keep_p, keep_att, keep_pre,
    grads_ref, small_ref, dcols_out, dcvec_ref, dact_ref, stat_ref,
    dh_ref, dmid_ref, h_ref, act_ref, dpre_ref, branch_ref, dba_ref, dqkv_ref, dm_ref,
    send_w, first_w, full_w, send_u, first_u, full_u, kv_send, kv_got,
    grads, pair_got, x_send, x_got, y_send, y_got, done, square,
    s_grads, s_pair, s_send, s_x, s_y_send, s_y, s_done,
    c_got, dcols_ref, cond_buf, product, gram, silu_got, swish_got, stat_got,
    w_sems, u_sems, kv_sems, pair_sems, x_sems, y_sems, end_sems, own_sems,
    s_sems, s_x_sems, s_y_sems, s_own_sems, c_sems, f_sems, cond_sems, t_sems, a_sems, n_sems,
):
    nf, nc, nt = sizes["fsdp"], sizes["ctx"], sizes["tp"]
    chips = nc // 2
    layers, _, _, half, local = grads_ref.shape
    step = pl.program_id(0)
    new = lax.rem(step, 2)
    old = 1 - new
    f, c, t = lax.axis_index("fsdp"), lax.axis_index("ctx"), lax.axis_index("tp")
    core, chip = lax.rem(c, 2), c // 2
    sibling = c + 1 - 2 * core
    count, rows, width = dh_ref.shape
    heads = local // HEAD_DIM
    scale = 1.0 / math.sqrt(HEAD_DIM)
    piece = min(64, half)
    columns = cond_ref.shape[1]
    f32 = jnp.float32
    A, H, M = 0, 1, 2
    layer = layers - 1 - step

    def blocks(k):
        return pl.ds(*GROUPS[k])

    def pieces(k, body):
        parts = half // piece

        def one(j, carry):
            body(j // parts, pl.ds(pl.multiple_of(lax.rem(j, parts) * piece, piece), piece))
            return carry

        low, size = GROUPS[k]
        lax.fori_loop(low * parts, (low + size) * parts, one, 0)

    def pair_copy(k, at):
        return remote(
            grads.at[blocks(k), :, 1 - core], pair_got.at[at, blocks(k)], pair_sems, (at, k), ctx=sibling
        )

    def x_copy(k, at, ahead):
        return remote(
            x_send.at[ahead - 1, blocks(k)], x_got.at[at, ahead - 1, blocks(k)],
            x_sems, (at, k, ahead - 1), fsdp=lax.rem(f + ahead, nf),
        )

    def y_copy(k, at, ahead):
        return remote(
            y_send.at[blocks(k)], y_got.at[at, ahead - 1, blocks(k)],
            y_sems, (at, k, ahead - 1), ctx=lax.rem(chip + ahead, chips) * 2 + core,
        )

    def end_copy(k, at, layer, to):
        return remote(done.at[blocks(k)], grads_ref.at[layer, blocks(k), to], end_sems, (at, k), ctx=sibling)

    def own_copy(k, layer):
        return pltpu.make_async_copy(done.at[blocks(k)], grads_ref.at[layer, blocks(k), core], own_sems.at[k])

    def stage_2(k, at):
        pair_copy(k, at).wait()
        for ahead in range(1, nf):
            peer = lax.rem(f + ahead, nf)

            def add(b, r):
                total = grads[b, peer, core, r].astype(f32) + pair_got[at, b, peer, r].astype(f32)
                x_send[ahead - 1, b, r] = total.astype(LOW)

            pieces(k, add)
            x_copy(k, at, ahead).start()

    def stage_3(k, at):
        for ahead in range(1, nf):
            x_copy(k, at, ahead).wait()

        def add(b, r):
            total = grads[b, f, core, r].astype(f32) + pair_got[at, b, f, r].astype(f32)
            for ahead in range(1, nf):
                total = total + x_got[at, ahead - 1, b, r].astype(f32)
            y_send[b, r] = total.astype(LOW)

        pieces(k, add)
        for ahead in range(1, chips):
            y_copy(k, at, ahead).start()

    def end_wait(k, at, layer):
        own_copy(k, layer).wait()
        end_copy(k, at, layer, core).wait_send()
        end_copy(k, at, layer, 1 - core).wait_recv()

    def stage_4(k, at, layer):
        for ahead in range(1, chips):
            y_copy(k, at, ahead).wait()

        def add(b, r):
            total = y_send[b, r].astype(f32)
            for ahead in range(1, chips):
                total = total + y_got[at, ahead - 1, b, r].astype(f32)
            low = total.astype(LOW)
            done[b, r] = low
            total = low.astype(f32)
            square[...] += jnp.sum((total * total).reshape(piece // 8, 8, local), 0)

        pieces(k, add)
        own_copy(k, layer).start()
        end_copy(k, at, layer, core).start()

    def when(low, high, body):
        pl.when((step >= low) & (step <= high))(body)

    def matrix(k):
        return w_ref[0, k].reshape(width, local)

    def mod(k, g, layer):
        return row(mods_ref, g, 6 * layer + k, width)

    def put_dmod(k, g, layer, value):
        put_row(dm_ref, g, 6 * layer + k, width, value)

    def keep_grad(k, value):
        grads[k] = value.astype(LOW).reshape(nf, 2, half, local)

    def total_w(g):
        return Total(nt, g, send_w, first_w, full_w, w_sems)

    def total_u(g):
        return Total(nt, g, send_u, first_u, full_u, u_sems)

    def both(ref):
        value = ref[...]
        return value.reshape(count * rows, value.shape[-1])

    @pl.when(step == 0)
    def _():
        meet(sizes)
        dh_ref[...] = dh0_ref[...]
        square[...] = jnp.zeros_like(square)
        for g in range(count):
            put_row(dm_ref, g, 3 * layers, 2 * width, dmods_end_ref[g : g + 1])

    def finish_input(g):
        normed, inv = norm_parts(h_ref[g])
        d_h, d_shift, d_scale = norm_back(
            total_u(g).get().astype(f32), normed, inv, mod(1, g, layer + 1)
        )
        put_dmod(0, g, layer + 1, d_shift)
        put_dmod(1, g, layer + 1, d_scale)
        dh_ref[g] = d_h + dmid_ref[g]

    def mlp_back(g):
        grad = dh_ref[g]
        put_dmod(5, g, layer, jnp.sum(grad * keep_m[0, g].astype(f32), 0, keepdims=True))
        branch = (mod(5, g, layer) * grad).astype(LOW)
        branch_ref[g] = branch
        part = jnp.zeros((rows, width), f32)
        for k in range(4):
            value, slope = gelu_parts(keep_pre[0, g, k])
            act_ref[k, g] = value.astype(LOW)
            d_pre = (dot(branch, matrix(MLP + k)) * slope).astype(LOW)
            dpre_ref[k, g] = d_pre
            part = part + dot_nt(d_pre, matrix(HIDDEN + k))
        total_w(g).scatter(part)

    for g in range(count):
        when(1, layers, lambda: finish_input(g))
        when(0, layers - 1, lambda: mlp_back(g))

    def share(own, slots, sems, axis, size, where=()):
        me = lax.axis_index(axis)
        for ahead in range(1, size):
            remote(own, slots.at[me], sems, (*where, ahead - 1), **{axis: lax.rem(me + ahead, size)}).start()

    def shared(own, slots, sems, axis, size, where=()):
        me = lax.axis_index(axis)
        for ahead in range(1, size):
            remote(own, slots.at[me], sems, (*where, ahead - 1), **{axis: lax.rem(me + ahead, size)}).wait_send()
            source = lax.rem(me + size - ahead, size)
            remote(slots.at[source], slots.at[source], sems, (*where, ahead - 1), **{axis: source}).wait_recv()

    def slot_sum(slots, size):
        total = slots[0]
        for k in range(1, size):
            total = total + slots[k]
        return total

    chunk = cond_buf.shape[-1]

    def cond_copy(j):
        return pltpu.make_async_copy(
            cond_ref.at[:, pl.ds(pl.multiple_of(j * chunk, LANES), chunk)],
            cond_buf.at[lax.rem(j, 2)],
            cond_sems.at[lax.rem(j, 2)],
        )

    def small_pair():
        return remote(s_grads.at[:, 1 - core], s_pair, s_sems, (0,), ctx=sibling)

    def small_x(ahead):
        return remote(
            s_send.at[ahead - 1], s_x.at[ahead - 1], s_x_sems, (ahead - 1,), fsdp=lax.rem(f + ahead, nf)
        )

    def small_y(ahead):
        return remote(
            s_y_send, s_y.at[ahead - 1], s_y_sems, (ahead - 1,), ctx=lax.rem(chip + ahead, chips) * 2 + core
        )

    def small_end(to):
        return remote(s_done, small_ref.at[to], s_sems, (1,), ctx=sibling)

    @pl.when(step == layers)
    def _():
        cond_copy(0).start()
        c_got[c] = dm_ref[:, pl.ds(pl.multiple_of(t * columns, LANES), columns)]
        share(c_got.at[c], c_got, c_sems, "ctx", nc)
        high, low = halves(both(dh_ref))
        noisy = noisy_ref[...]
        small = dot_tn(high.astype(LOW), noisy) + dot_tn(low.astype(LOW), noisy)
        small = small + dot_tn(final_ref[...], dpred_ref[...])
        s_grads[...] = small.reshape(s_grads.shape)
        small_pair().start()

    when(1, layers, lambda: stage_2(A, old))
    when(2, layers, lambda: (pl.when(step >= 3)(lambda: end_wait(A, old, layer + 3)), stage_4(A, new, layer + 2))[1])
    when(1, layers, lambda: stage_3(M, old))

    @pl.when(step == layers)
    def _():
        small_pair().wait()
        for ahead in range(1, nf):
            peer = lax.rem(f + ahead, nf)
            s_send[ahead - 1] = s_grads[peer, core] + s_pair[peer]
            small_x(ahead).start()
        shared(c_got.at[c], c_got, c_sems, "ctx", nc)
        dcols_ref[f] = slot_sum(c_got, nc)
        share(dcols_ref.at[f], dcols_ref, f_sems, "fsdp", nf)

    def stacked_input(ref, first):
        normed, _ = norm_parts(ref[0])
        parts = [
            normed[g] * (1.0 + mod(first + 1, g, layer)) + mod(first, g, layer) for g in range(count)
        ]
        return jnp.concatenate(parts, 0).astype(LOW)

    def mlp_grads():
        w_in = stacked_input(keep_mid, 3)
        for k in range(4):
            keep_grad(HIDDEN + k, dot_tn(w_in, dpre_ref[k].reshape(count * rows, local)))
        pair_copy(H, new).start()
        branch = both(branch_ref)
        for k in range(4):
            keep_grad(MLP + k, dot_tn(branch, act_ref[k].reshape(count * rows, local)))
        pair_copy(M, new).start()
        for g in range(count):
            total_w(g).share()
        stage_2(H, new)
        stage_2(M, new)

    when(0, layers - 1, mlp_grads)
    when(1, layers, lambda: (pl.when(step >= 2)(lambda: end_wait(H, new, layer + 2)), stage_4(H, old, layer + 1))[1])

    def attention_back(g):
        normed, inv = norm_parts(keep_mid[0, g])
        d_mid, d_shift, d_scale = norm_back(total_w(g).get().astype(f32), normed, inv, mod(4, g, layer))
        d_mid = d_mid + dh_ref[g]
        dmid_ref[g] = d_mid
        put_dmod(3, g, layer, d_shift)
        put_dmod(4, g, layer, d_scale)
        put_dmod(2, g, layer, jnp.sum(d_mid * keep_a[0, g].astype(f32), 0, keepdims=True))
        branch = (mod(2, g, layer) * d_mid).astype(LOW)
        dba_ref[g] = branch
        grad = spread(dot(branch, matrix(OUT)).astype(LOW), heads)
        query = spread(keep_q[0, g], heads)
        keys = keep_kv[0, g, :, :, :local].reshape(nc * rows, local)
        values = keep_kv[0, g, :, :, local:].reshape(nc * rows, local)
        probs = keep_p[0, g]
        d_probs = dot_nt(grad, values)
        d_scores = (probs * (d_probs - jnp.sum(d_probs * probs, -1, keepdims=True))).astype(LOW)
        d_values = dot_tn(probs.astype(LOW), grad)
        d_keys = dot_tn(d_scores, query) * scale
        kv_send[g, :, :, :local] = d_keys.astype(LOW).reshape(nc, rows, local)
        kv_send[g, :, :, local:] = d_values.astype(LOW).reshape(nc, rows, local)
        for ahead in range(1, nc):
            kv_copy(g, ahead).start()
        d_query = pick(dot(d_scores, keys), heads) * scale
        dqkv_ref[0, g] = d_query.astype(LOW)

    def kv_copy(g, ahead):
        peer = lax.rem(c + ahead, nc)
        return remote(kv_send.at[g, peer], kv_got.at[new, g, ahead - 1], kv_sems, (new, g, ahead - 1), ctx=peer)

    @pl.when(step < layers)
    def _():
        for g in range(count):
            attention_back(g)

    when(1, layers, lambda: stage_3(A, old))

    @pl.when(step < layers)
    def _():
        for g in range(count):
            total = kv_send[g, c].astype(f32)
            for ahead in range(1, nc):
                kv_copy(g, ahead).wait()
                total = total + kv_got[new, g, ahead - 1].astype(f32)
            dqkv_ref[1, g] = total[:, :local].astype(LOW)
            dqkv_ref[2, g] = total[:, local:].astype(LOW)
            part = dot_nt(dqkv_ref[0, g], matrix(QUERY))
            part = part + dot_nt(dqkv_ref[1, g], matrix(KEY))
            part = part + dot_nt(dqkv_ref[2, g], matrix(VALUE))
            total_u(g).scatter(part)
        h_ref[...] = keep_h[0]
        u_in = stacked_input(keep_h, 0)
        for k in range(3):
            keep_grad(QUERY + k, dot_tn(u_in, dqkv_ref[k].reshape(count * rows, local)))
        keep_grad(OUT, dot_tn(both(dba_ref), keep_att[0].reshape(count * rows, local)))
        pair_copy(A, new).start()
        for g in range(count):
            total_u(g).share()
        stage_3(H, new)

    images_row = max(8, images)

    @pl.when(step == layers)
    def _():
        shared(dcols_ref.at[f], dcols_ref, f_sems, "fsdp", nf)
        dcols_out[...] = dcols_ref[...]
        product[...] = jnp.zeros_like(product)
        gram[...] = jnp.zeros_like(gram)
        index = lax.broadcasted_iota(jnp.int32, (LANES, chunk), 0)

        def multiply(j, carry):
            @pl.when(j + 1 < columns // chunk)
            def _():
                cond_copy(j + 1).start()

            pair = jnp.zeros((LANES, chunk), f32)
            for n in range(images):
                source = dcols_ref[
                    n // count, n % count : n % count + 1, pl.ds(pl.multiple_of(j * chunk, LANES), chunk)
                ]
                high, low = halves(source)
                pair = jnp.where(index == n, high, pair)
                pair = jnp.where(index == images + n, low, pair)
            pair = pair.astype(LOW)
            gram[...] += dot_nt(pair, pair)
            cond_copy(j).wait()
            product[...] += dot_nt(cond_buf[lax.rem(j, 2)].astype(LOW), pair)
            return carry

        lax.fori_loop(0, columns // chunk, multiply, 0)
        total = product[...]
        total = jnp.transpose(total + pltpu.roll(total, LANES - images, 1))[:images_row]
        silu_got[t] = total
        share(silu_got.at[t], silu_got, t_sems, "tp", nt)
        for ahead in range(1, nf):
            small_x(ahead).wait()
        total = s_grads[f, core] + s_pair[f]
        for ahead in range(1, nf):
            total = total + s_x[ahead - 1]
        s_y_send[...] = total
        for ahead in range(1, chips):
            small_y(ahead).start()
        shared(silu_got.at[t], silu_got, t_sems, "tp", nt)
        d_cvec = slot_sum(silu_got, nt) * slope_c_ref[...]
        dcvec_ref[...] = d_cvec
        high, low = halves(d_cvec)
        pair = jnp.concatenate([high, low], 0).astype(LOW)
        time_label = jnp.sum(dot_nt(pair, pair) * gram_t_ref[...])
        total = dot(pair, time_ref[...])
        swish_got[f] = total[:images_row] + total[images_row:]
        share(swish_got.at[f], swish_got, a_sems, "fsdp", nf)
        shared(swish_got.at[f], swish_got, a_sems, "fsdp", nf)
        d_act = slot_sum(swish_got, nf) * slope_a_ref[...]
        dact_ref[...] = d_act
        high, low = halves(d_act)
        pair = jnp.concatenate([high, low], 0).astype(LOW)
        freq = jnp.sum(dot_nt(pair, pair) * gram_f_ref[...])
        cond = jnp.sum(gram[...] * gram_c_ref[...])
        stat_ref[...] = jnp.full(
            stat_ref.shape, cond / nc + time_label / (nt * nc) + freq / (nf * nt * nc), f32
        )

    when(1, layers, lambda: (pl.when(step >= 2)(lambda: end_wait(M, new, layer + 2)), stage_4(M, old, layer + 1))[1])

    @pl.when(step == layers)
    def _():
        end_wait(A, new, 1)
        stage_4(A, old, 0)
        total = s_y_send[...]
        for ahead in range(1, chips):
            small_y(ahead).wait()
            total = total + s_y[ahead - 1]
        s_done[...] = total
        own = pltpu.make_async_copy(s_done, small_ref.at[core], s_own_sems.at[0])
        own.start()
        small_end(core).start()
        part = jnp.sum(square[...]) / chips + jnp.sum(total * total) / (nt * chips)
        index = lax.broadcasted_iota(jnp.int32, stat_ref.shape, 0)
        stat_ref[...] = jnp.where(index < 8, stat_ref[...] + part, loss_ref[0:1] / nt)
        for k, (axis, size) in enumerate((("ctx", nc), ("fsdp", nf), ("tp", nt))):
            me = lax.axis_index(axis)
            slots = stat_got.at[k]
            slots[me] = stat_ref[...]
            share(slots.at[me], slots, n_sems, axis, size, (k,))
            shared(slots.at[me], slots, n_sems, axis, size, (k,))
            stat_ref[...] = slot_sum(slots, size)
        for k in range(3):
            end_wait(k, old, 0)
        own.wait()
        small_end(core).wait_send()
        small_end(1 - core).wait_recv()


def backward(mesh, images, dh0, mods, dmods_end, loss, noisy, dpred, final_in, slopes, grams, time_low, cond, full, saved):
    sizes = dict(mesh.shape)
    nf, nc, nt = sizes["fsdp"], sizes["ctx"], sizes["tp"]
    chips = nc // 2
    others, overs = max(nf - 1, 1), max(chips - 1, 1)
    count, rows, width = dh0.shape
    layers, blocks, _, local = full.shape
    shard, columns = cond.shape
    half = shard // 2
    tokens = count * rows
    padded = max(8, images)
    f32 = jnp.float32

    def per_layer(array):
        shape = array.shape[1:]
        return pl.BlockSpec(
            (1, *shape), lambda i: (jnp.maximum(layers - 1 - i, 0),) + (0,) * len(shape)
        )

    anywhere = pl.BlockSpec(memory_space=pl.ANY)
    vmem = pl.BlockSpec(memory_space=pltpu.VMEM)
    whole = pltpu.VMEM((count, nt, rows // nt, width), LOW)
    first = pltpu.VMEM((count, nt - 1, rows // nt, width), LOW)
    image = pltpu.VMEM((count, rows, width), f32)
    image_low = pltpu.VMEM((count, rows, width), LOW)
    mlp = pltpu.VMEM((4, count, rows, local), LOW)
    small = (half, LANES)
    dma = pltpu.SemaphoreType.DMA
    return pl.pallas_call(
        functools.partial(backward_kernel, sizes, images),
        grid=(layers + 1,),
        out_shape=[
            jax.ShapeDtypeStruct((layers, blocks, 2, half, local), LOW),
            jax.ShapeDtypeStruct((2, half, LANES), f32),
            jax.ShapeDtypeStruct((nf, count, columns), f32),
            jax.ShapeDtypeStruct((padded, shard), f32),
            jax.ShapeDtypeStruct((padded, width), f32),
            jax.ShapeDtypeStruct((16, LANES), f32),
        ],
        in_specs=[vmem] * 13 + [anywhere, per_layer(full), *(per_layer(s) for s in saved)],
        out_specs=[anywhere, anywhere, vmem, vmem, vmem, vmem],
        scratch_shapes=[
            image, image, image, mlp, mlp, image_low, image_low,
            pltpu.VMEM((3, count, rows, local), LOW),
            pltpu.VMEM(mods.shape, f32),
            whole, first, whole, whole, first, whole,
            pltpu.VMEM((count, nc, rows, 2 * local), LOW),
            pltpu.VMEM((2, count, nc - 1, rows, 2 * local), LOW),
            pltpu.VMEM((blocks, nf, 2, half, local), LOW),
            pltpu.VMEM((2, blocks, nf, half, local), LOW),
            pltpu.VMEM((others, blocks, half, local), LOW),
            pltpu.VMEM((2, others, blocks, half, local), LOW),
            pltpu.VMEM((blocks, half, local), LOW),
            pltpu.VMEM((2, overs, blocks, half, local), LOW),
            pltpu.VMEM((blocks, half, local), LOW),
            pltpu.VMEM((8, local), f32),
            pltpu.VMEM((nf, 2, *small), f32),
            pltpu.VMEM((nf, *small), f32),
            pltpu.VMEM((others, *small), f32),
            pltpu.VMEM((others, *small), f32),
            pltpu.VMEM(small, f32),
            pltpu.VMEM((overs, *small), f32),
            pltpu.VMEM(small, f32),
            pltpu.VMEM((nc, count, columns), f32),
            pltpu.VMEM((nf, count, columns), f32),
            pltpu.VMEM((2, shard, 512), f32),
            pltpu.VMEM((shard, LANES), f32),
            pltpu.VMEM((LANES, LANES), f32),
            pltpu.VMEM((nt, padded, shard), f32),
            pltpu.VMEM((nf, padded, width), f32),
            pltpu.VMEM((3, max(sizes.values()), 16, LANES), f32),
            dma((2, 2, count, nt - 1)),
            dma((2, 2, count, nt - 1)),
            dma((2, 2, count, nc - 1)),
            dma((2, 2, 3)),
            dma((2, 2, 3, others)),
            dma((2, 2, 3, overs)),
            dma((2, 2, 3)),
            dma((3,)),
            dma((2, 2)),
            dma((2, others)),
            dma((2, overs)),
            dma((1,)),
            dma((2, nc - 1)),
            dma((2, others)),
            dma((2,)),
            dma((2, nt - 1)),
            dma((2, others)),
            dma((2, 3, max(sizes.values()))),
        ],
        compiler_params=pltpu.CompilerParams(
            collective_id=2, has_side_effects=True, vmem_limit_bytes=60 * 2**20
        ),
        cost_estimate=pl.CostEstimate(
            flops=4 * tokens * width * blocks * local * layers,
            bytes_accessed=layers * blocks * width * local * 4,
            transcendentals=0,
        ),
        name="backward_layers",
    )(dh0, mods, dmods_end, loss, noisy, dpred, final_in, *slopes, *grams, time_low, cond, full, *saved)


FIX = 1.0 / (1.0 - BETA**STEP)


def update_block(weight, mean, square, grad, outs, where):
    mean_next = BETA * mean[where] + (1.0 - BETA) * grad
    square_next = BETA * square[where] + (1.0 - BETA) * (grad * grad)
    moved = (mean_next * FIX) / (jnp.sqrt(square_next * FIX) + EPSILON)
    outs[0][where] = weight[where] - RATE * (moved + DECAY * weight[where])
    outs[1][where] = mean_next
    outs[2][where] = square_next


def update_plain_kernel(clip_ref, grad_ref, weight, mean, square, *outs):
    clip = clip_ref[0, 0]
    rows = weight.shape[-2]
    piece = min(64, rows)
    for r in range(0, rows, piece):
        where = (0, 0, pl.ds(r, piece))
        update_block(weight, mean, square, grad_ref[where].astype(jnp.float32) * clip, outs, where)


def update_mixed_kernel(clip_ref, grad_ref, weight, mean, square, *outs):
    clip = clip_ref[0, 0]
    _, blocks, rows, columns = grad_ref.shape
    tiles = columns // LANES
    size = blocks * tiles * 16
    order = interleave(blocks, tiles)
    for r in range(rows // 16):
        parts = [
            grad_ref[0, k, 16 * r : 16 * r + 16, n * LANES : (n + 1) * LANES]
            for k in range(blocks)
            for n in range(tiles)
        ]
        grad = dot(order, jnp.concatenate(parts, 0)) * clip
        update_block(weight, mean, square, grad, outs, (0, pl.ds(r * size, size)))


def update_rank_kernel(clip_ref, left_ref, right_ref, weight, mean, square, *outs):
    clip = clip_ref[0, 0]
    rows = weight.shape[0]
    piece = min(64, rows)
    for r in range(0, rows, piece):
        where = (pl.ds(r, piece),)
        grad = dot_tn(left_ref[:, r : r + piece], right_ref[...]) * clip
        update_block(weight, mean, square, grad, outs, where)


def update(kernel, clip, factors, factor_specs, trio, spec, grid, name):
    shape = jax.ShapeDtypeStruct(trio[0].shape, jnp.float32)
    size = trio[0].size
    return pl.pallas_call(
        kernel,
        grid=grid,
        out_shape=[shape] * 3,
        in_specs=[pl.BlockSpec(memory_space=pltpu.SMEM), *factor_specs, spec, spec, spec],
        out_specs=[spec] * 3,
        compiler_params=pltpu.CompilerParams(vmem_limit_bytes=48 * 2**20),
        cost_estimate=pl.CostEstimate(flops=20 * size, bytes_accessed=26 * size, transcendentals=2 * size),
        name=name,
    )(clip, *factors, *trio)


def update_plain(clip, grads, trio, first):
    trio = [jnp.swapaxes(a, 1, 2) for a in trio]
    layers, blocks, rows, columns = trio[0].shape
    block = (1, 1, rows, columns)
    spec = pl.BlockSpec(block, lambda i, j: (i, j, 0, 0))
    grad_spec = pl.BlockSpec(block, lambda i, j: (i, first + j, 0, 0))
    outs = update(
        update_plain_kernel, clip, [grads], [grad_spec], trio, spec, (layers, blocks), "update_plain"
    )
    return [jnp.swapaxes(a, 1, 2) for a in outs]


def mixed(a):
    layers, rows, blocks, columns = a.shape
    a = a.reshape(layers, rows, blocks, columns // LANES, LANES)
    return jnp.swapaxes(a, 2, 3).reshape(layers, -1, LANES)


def update_mixed(clip, grads, trio):
    layers, rows, blocks, columns = trio[0].shape
    tiles = columns // LANES

    def back(a):
        a = a.reshape(layers, rows, tiles, blocks, LANES)
        return jnp.swapaxes(a, 2, 3).reshape(layers, rows, blocks, columns)

    step = min(rows, 128)
    spec = pl.BlockSpec((1, step * blocks * tiles, LANES), lambda i, j: (i, j, 0))
    grad_spec = pl.BlockSpec((1, blocks, step, columns), lambda i, j: (i, 0, j, 0))
    outs = update(
        update_mixed_kernel,
        clip,
        [grads],
        [grad_spec],
        [mixed(a) for a in trio],
        spec,
        (layers, rows // step),
        "update_mixed",
    )
    return [back(a) for a in outs]


def update_rank(clip, left, right, trio):
    rows, columns = trio[0].shape
    step = 512 if columns % 512 == 0 else columns
    spec = pl.BlockSpec((rows, step), lambda i: (0, i))
    left_spec = pl.BlockSpec(left.shape, lambda i: (0, 0))
    right_spec = pl.BlockSpec((right.shape[0], step), lambda i: (0, i))
    return update(
        update_rank_kernel,
        clip,
        [left, right],
        [left_spec, right_spec],
        trio,
        spec,
        (columns // step,),
        "update_rank",
    )


def split_rows(value, other):
    rounded = lax.reduce_precision(value, 8, 7)
    high, low = rounded.astype(LOW), (value - rounded).astype(LOW)
    pad = -2 * value.shape[0] % 16
    return (
        jnp.pad(jnp.concatenate([high, low]), ((0, pad), (0, 0))),
        jnp.pad(jnp.concatenate([other, other]).astype(LOW), ((0, pad), (0, 0))),
    )


def per_device(
    mesh,
    latents,
    noise,
    var_target,
    timesteps,
    labels,
    attend_weight,
    attend_mean,
    attend_square,
    hidden_weight,
    hidden_mean,
    hidden_square,
    output_weight,
    output_mean,
    output_square,
    patch_weight,
    patch_mean,
    patch_square,
    freq_weight,
    freq_mean,
    freq_square,
    time_weight,
    time_mean,
    time_square,
    label_table,
    label_mean,
    label_square,
    cond_weight,
    cond_mean,
    cond_square,
    head_weight,
    head_mean,
    head_square,
):
    count, rows, patch_in = latents.shape
    layers, shard = attend_weight.shape[:2]
    columns = cond_weight.shape[1]

    steps_all = lax.all_gather(timesteps, "fsdp", axis=0, tiled=True)
    labels_all = lax.all_gather(labels, "fsdp", axis=0, tiled=True)
    freqs = time_freqs(steps_all).astype(LOW)
    act = jnp.dot(freqs, freq_weight.astype(LOW).T, preferred_element_type=jnp.float32)
    act = lax.all_gather(act, "fsdp", axis=1, tiled=True)
    swish = jax.nn.silu(act).astype(LOW)
    time_low = time_weight.astype(LOW)
    temb = jnp.dot(swish, time_low.T, preferred_element_type=jnp.float32)
    onehot = (labels_all[:, None] == jnp.arange(label_table.shape[1], dtype=jnp.int32)[None]).astype(
        LOW
    )
    cvec = temb + jnp.dot(onehot, label_table.astype(LOW).T, preferred_element_type=jnp.float32)
    cond_in = jax.nn.silu(cvec).astype(LOW)
    cond_low = cond_weight.astype(LOW)
    mods_part = jnp.dot(cond_in, cond_low, preferred_element_type=jnp.float32)
    patch_head = lax.all_gather(
        jnp.concatenate([patch_weight, head_weight], 1).astype(LOW), "fsdp", axis=0, tiled=True
    )
    patch_full, head_full = patch_head[:, :patch_in], patch_head[:, patch_in:]
    width = patch_full.shape[0]

    level = noise_level(timesteps)[:, None, None]
    noisy = (jnp.sqrt(level) * latents + jnp.sqrt(1.0 - level) * noise).astype(LOW)
    first = lax.axis_index("ctx") * rows
    h = (
        jnp.einsum("gsp,dp->gsd", noisy, patch_full, preferred_element_type=jnp.float32)
        + positions(first, rows, width)[None]
    )
    h, flat_mods, full, *saved = forward(
        mesh,
        h,
        mods_part.reshape(-1, count, columns),
        mixed(hidden_weight),
        jnp.swapaxes(attend_weight, 1, 2),
        jnp.swapaxes(output_weight, 1, 2),
    )
    blocks = full.shape[1]
    full = full.reshape(layers, blocks, width, -1)
    mods = flat_mods.reshape(count, -1, width)
    final_in = modln(h, mods[:, 6 * layers, None], mods[:, 6 * layers + 1, None]).astype(LOW)
    pred = jnp.einsum("gsd,dp->gsp", final_in, head_full, preferred_element_type=jnp.float32)
    diff = pred - jnp.concatenate([noise, var_target], -1)
    loss_part = jnp.full((8, LANES), jnp.sum(diff * diff))
    d_pred = (2.0 * diff).astype(LOW)
    d_final = jnp.einsum("gsp,dp->gsd", d_pred, head_full, preferred_element_type=jnp.float32)
    _, norm_back = jax.vjp(modln, h, mods[:, 6 * layers, None], mods[:, 6 * layers + 1, None])
    d_h, d_shift_f, d_scale_f = norm_back(d_final)
    images = freqs.shape[0]
    padded = max(8, images) - images
    tokens = count * rows

    def slope(value):
        _, back = jax.vjp(jax.nn.silu, value)
        return jnp.pad(back(jnp.ones_like(value))[0], ((0, padded), (0, 0)))

    def gram(value):
        value = value.astype(jnp.float32)
        return jnp.einsum("nd,md->nm", value, value, precision=HIGH)

    def doubled(value):
        return jnp.tile(jnp.pad(value, ((0, padded), (0, padded))), (2, 2))

    beyond = LANES - 2 * images
    grams = (
        jnp.pad(jnp.tile(gram(cond_in), (2, 2)), ((0, beyond), (0, beyond))),
        doubled(gram(swish) + gram(onehot)),
        doubled(gram(freqs)),
    )
    patch_out = d_pred.shape[-1]
    grads, d_small, d_cols, d_cvec, d_act, stat = backward(
        mesh,
        images,
        d_h,
        flat_mods,
        jnp.concatenate([d_shift_f, d_scale_f], 2).reshape(count, -1),
        loss_part,
        jnp.pad(noisy.reshape(tokens, -1), ((0, 0), (0, LANES - patch_in))),
        jnp.pad(d_pred.reshape(tokens, -1), ((0, 0), (patch_in, LANES - patch_in - patch_out))),
        final_in.reshape(tokens, -1),
        (slope(cvec), slope(act)),
        grams,
        time_low,
        cond_weight,
        full,
        saved,
    )
    grads = grads.reshape(layers, blocks, shard, -1)
    d_small = d_small.reshape(shard, -1)
    d_cols = d_cols.reshape(images, columns)
    d_cvec = d_cvec[:images]
    d_act = lax.dynamic_slice_in_dim(
        d_act[:images], lax.axis_index("fsdp") * shard, shard, 1
    )
    total_sq, loss = stat[0, 0], stat[8, 0]
    grad_norm = jnp.sqrt(total_sq)
    clip = jnp.minimum(1.0, CLIP / (grad_norm + 1e-06))
    factor = clip.reshape(1, 1)
    cols_parts, cond_parts = split_rows(d_cols, cond_in)
    cvec_parts, swish_parts = split_rows(d_cvec, swish)
    act_parts, freq_parts = split_rows(d_act, freqs)
    updated = [
        *update_plain(factor, grads, (attend_weight, attend_mean, attend_square), QUERY),
        *update_mixed(factor, grads, (hidden_weight, hidden_mean, hidden_square)),
        *update_plain(factor, grads, (output_weight, output_mean, output_square), OUT),
        *adamw(patch_weight, patch_mean, patch_square, d_small[:, :patch_in] * clip),
        *update_rank(factor, act_parts, freq_parts, (freq_weight, freq_mean, freq_square)),
        *update_rank(factor, cvec_parts, swish_parts, (time_weight, time_mean, time_square)),
        *adamw(
            label_table,
            label_mean,
            label_square,
            rank_sum(d_cvec, onehot.astype(jnp.float32)) * clip,
        ),
        *update_rank(factor, cond_parts, cols_parts, (cond_weight, cond_mean, cond_square)),
        *adamw(
            head_weight, head_mean, head_square, d_small[:, patch_in : patch_in + patch_out] * clip
        ),
    ]
    return (loss, grad_norm, *updated)


def solution(mesh):
    image = P("fsdp", "ctx", None)
    layer = P(None, "fsdp", None, "tp")
    rows = P("fsdp", None)
    cond = P("fsdp", "tp")
    weights = (layer,) * 9 + (rows,) * 12 + (cond,) * 3 + (rows,) * 3
    return jax.shard_map(
        functools.partial(per_device, mesh),
        mesh=mesh,
        in_specs=(image, image, image, P("fsdp"), P("fsdp")) + weights,
        out_specs=(P(), P()) + weights,
        check_vma=False,
    )
```

time: 2230 us -> 546 us (0.24)
  waiting for transfers between devices: 1520 us -> 0 us
  Pallas kernels: 0 us -> 474 us
  other arithmetic: 227 us -> 19.3 us
  matrix products: 154 us -> 10.5 us
  local copies, waits for them, and re-layouts: 160 us -> 21.4 us
  blocking collectives: 119 us -> 14.3 us
  between operations: 32.7 us -> 3.49 us
    psum x18 -> x0, waiting for transfers between devices: 766 us -> none  [the longest x16 510 us: tp_total(): return lax.psum(part.astype(LOW), 'tp').astype(jnp.float32)]
    pallas_call x0 -> x8, Pallas kernels: none -> 474 us  [the longest x1 204 us: backward(): pl.pallas_call(functools.partial(backward_kernel, sizes, images), grid=(l...]
    reduce_scatter x17 -> x0, waiting for transfers between devices: 420 us -> none  [the longest x12 348 us: reduce_layer(): lax.psum_scatter(g.astype(LOW), 'fsdp', scatter_dimension=0, tiled=True)]
    all_gather x12 -> x0, waiting for transfers between devices: 330 us -> none  [the longest x4 132 us: gather_layer(): lax.all_gather(hidden.astype(LOW), 'fsdp', axis=0, tiled=True)]
    dot_general x79 -> x5, matrix products: 138 us -> 6.41 us  [the longest x1 5.86 us: per_device(): mods_part = jnp.dot(cond_in, cond_low, preferred_element_type=jnp.float32)]
    sub x9 -> x3, other arithmetic: 104 us -> 8.65 us  [adamw(): weight - RATE * (fixed_mean / (jnp.sqrt(fixed_square) + EPSILON) + DECAY...]
    unnamed x557 -> x37, local copies, waits for them, and re-layouts: 76.6 us -> 7.71 us
    psum x4 -> x0, blocking collectives: 56 us -> none  [the longest x1 21.9 us: per_device(): lax.psum(split_sq + copied_sq / lax.axis_size('tp'), ('fsdp', 'tp'))]
  transfers between devices with their start and end apart: 49 -> 0, of which waited for: 44 -> 0; matrix products, arithmetic and copies ran while one was open for 8% -> 0% of each run, Pallas kernels for 0% -> 0%
where the time goes in v4:
time: 546 us; the launch traced here: 543 us
  Pallas kernels  474 us (87%)
  local copies, waits for them, and re-layouts  21.4 us (4%)
  other arithmetic  19.3 us (4%)
  blocking collectives  14.3 us (3%)
  matrix products  10.5 us (2%)
    pallas_call x1, Pallas kernels, backward(): pl.pallas_call(functools.partial(backward_kernel, sizes, images), grid=(l...  204 us
    pallas_call x1, Pallas kernels, forward(): pl.pallas_call(functools.partial(forward_kernel, sizes), grid=(layers + 1...  152 us
    pallas_call x6, Pallas kernels, update(): pl.pallas_call(kernel, grid=grid, out_shape=[shape] * 3, in_specs=[pl.Blo...  118 us

profile of v4, /device:TPU:0, one launch (start us, length us, event | category | flops | bytes accessed | tf_op | source)
XLA Modules:
  0.0 543.0 jit_solution(10855089135283978991)
XLA Ops:
  0.7 1.4 dynamic-slice
  4.4 5.2 all-reduce.15
  11.5 1.2 fusion.6
  12.7 4.4 all_gather.14
  21.8 4.8 all_gather.12
  28.8 1.4 copy-done.7
  32.0 5.9 %fusion = f32[4,6656]{1,0:T(4,128)S(1)} fusion(bf16[4,512]{1,0:T(4,128)(2,1)S(1)} %get-tuple-element.139, f32[512,6656]{1,0:T(8,128)} %weight.5), kind=kOutput, calls=%fused_computation | convolution fusion | flops 30670848 | bytes 13742080 | tf_op jit(solution)/shard_map/dot_general | solution.py:1286
  38.5 151.7 %forward_layers.1 = (f32[2,64,1024]{2,1,0:T(8,128)}, f32[2,26624]{1,0:T(2,128)}, bf16[4,12,2,2,2,128,256]{6,5,4,3,2,1,0:T(8,128)(2,1)}, f32[4,2,64,1024]{3,2,1,0...) custom-call(f32[2,64,1024]{2,1,0:T(8,128)} %convolution_add_fusion.h, ...), custom_call_target="tpu_custom_call" | custom-call | flops 3221225472 | bytes 50331648 | tf_op jit(solution)/shard_map/forward_layers/pallas_call | solution.py:530
  190.3 1.2 reduce_sum.62
  191.5 1.2 multiply_reduce_fusion.2
  192.8 1.1 reshape.223
  194.0 1.2 add_convert_fusion
  196.0 1.2 broadcast_in_dim.8.loss_ref
  200.4 204.2 %backward_layers.1 = (bf16[4,12,2,256,256]{4,3,2,1,0:T(8,128)(2,1)}, f32[2,256,128]{2,1,0:T(8,128)}, f32[2,2,6656]{2,1,0:T(2,128)}, f32[8,512]{1,0:T(8,128)}, f32[8,1024]{1,0:T(8,128)}, /*index=5*/f32[16,128]{1,0:T(8,128)}) custom-call(f32[2,64,1024]{2,1,0:T(8,128)} %broadcast_add_fusion.dh0_ref, f32[2,26624]{1,0:T(2,128)} %get-tuple-element.66.mods_ref, ...), custom_call_target="tpu_custom_call" | custom-call | flops 6442450944 | bytes 50331648 | tf_op jit(solution)/shard_map/backward_layers/pallas_call | solution.py:1027
  404.6 1.3 fusion.58
  411.9 1.8 slice.86
  414.7 1.6 multiply_subtract_fusion.1
  417.4 1.7 update_rank.3
  419.1 6.4 %multiply_subtract_fusion = (f32[512,1001]{0,1:T(8,128)}, f32[512,1001]{0,1:T(8,128)}, f32[512,1001]{0,1:T(8,128)}) fusion(f32[512,1001]{0,1:T(8,128)} %param.55, f32[]{:T(128)} %min.3, f32[1001]{0:T(1024)S(1)} %bitcast.121, f32[512]{0:T(512)S(1)} %bitcast.125, f32[1001]{0:T(1024)S(1)} %bitcast.122, f32[512]{0:T(512)S(1)} %bitcast.126, ...), kind=kLoop, calls=%fused_computation.5 | loop fusion | flops 11275264 | bytes 12324500 | tf_op jit(solution)/shard_map/sub | solution.py:65
  425.5 5.3 update_rank.4
  430.9 18.9 %update_plain.2 = (f32[4,3,512,256]{3,2,1,0:T(8,128)}, f32[4,3,512,256]{3,2,1,0:T(8,128)}, f32[4,3,512,256]{3,2,1,0:T(8,128)}) custom-call(f32[1,1]{1,0:T(1,128)} %bitcast.17.clip_ref, bf16[4,12,512,256]{3,2,1,0:T(8,128)(2,1)} %bitcast.92, f32[4,3,512,256]{3,2,1,0:T(8,128)} %bitcast.101, f32[4,3,512,256]{3,2,1,0:T(8,128)} %bitcast.106, ...), custom_call_target="tpu_custom_call" | custom-call | flops 31457280 | bytes 40894464 | tf_op jit(solution)/shard_map/update_plain/pallas_call | solution.py:1151
  449.8 25.6 %update_mixed.1 = (f32[4,4096,128]{2,1,0:T(8,128)}, f32[4,4096,128]{2,1,0:T(8,128)}, f32[4,4096,128]{2,1,0:T(8,128)}) custom-call(f32[1,1]{1,0:T(1,128)} %bitcast.17.clip_ref, bf16[4,12,512,256]{3,2,1,0:T(8,128)(2,1)} %bitcast.93, f32[4,4096,128]{2,1,0:T(8,128)} %bitcast.98, f32[4,4096,128]{2,1,0:T(8,128)} %bitcast.104, f32[4,4096,128]{2,1,0:T(8,128)} %bitcast.105), custom_call_target="tpu_custom_call" | custom-call | flops 41943040 | bytes 54525952 | tf_op jit(solution)/shard_map/update_mixed/pallas_call | solution.py:1151
  475.4 31.1 %update_plain.3 = (f32[4,5,512,256]{3,2,1,0:T(8,128)}, f32[4,5,512,256]{3,2,1,0:T(8,128)}, f32[4,5,512,256]{3,2,1,0:T(8,128)}) custom-call(f32[1,1]{1,0:T(1,128)} %bitcast.17.clip_ref, bf16[4,12,512,256]{3,2,1,0:T(8,128)(2,1)} %bitcast.94, f32[4,5,512,256]{3,2,1,0:T(8,128)} %bitcast.96, f32[4,5,512,256]{3,2,1,0:T(8,128)} %bitcast.102, ...), custom_call_target="tpu_custom_call" | custom-call | flops 52428800 | bytes 68157440 | tf_op jit(solution)/shard_map/update_plain/pallas_call | solution.py:1151
  506.5 35.3 %update_rank.5 = (f32[512,6656]{1,0:T(8,128)}, f32[512,6656]{1,0:T(8,128)}, f32[512,6656]{1,0:T(8,128)}) custom-call(f32[1,1]{1,0:T(1,128)} %bitcast.17.clip_ref, bf16[16,512]{1,0:T(8,128)(2,1)S(1)} %fusion.27.left_ref, bf16[16,6656]{1,0:T(8,128)(2,1)S(1)} %fusion.8.right_ref, f32[512,6656]{1,0:T(8,128)} %weight.5, f32[512,6656]{1,0:T(8,128)} %mean.5, ...), custom_call_target="tpu_custom_call" | custom-call | flops 68157440 | bytes 88604672 | tf_op jit(solution)/shard_map/update_rank/pallas_call | solution.py:1151
  (97 shorter events, 24.2 us)
Async XLA Ops:
  0.7 27.6 %copy-start = (f32[512,1024]{1,0:T(8,128)S(1)}, f32[512,1024]{1,0:T(8,128)}, u32[]{:S(2)}) copy-start(f32[512,1024]{1,0:T(8,128)} %weight.4) | copy-start | bytes 6291460
  28.2 2.0 copy-start.7
  28.4 9.4 %copy-start.6 = (bf16[512,1024]{1,0:T(8,128)(2,1)}, bf16[512,1024]{1,0:T(8,128)(2,1)S(1)}, u32[]{:S(2)}) copy-start(bf16[512,1024]{1,0:T(8,128)(2,1)S(1)} %convert_element_type.107.time_ref) | copy-start | bytes 3145732
  190.3 4.9 copy-start.10
  190.3 4.9 copy-start.13
  190.3 7.8 %copy-start.5 = (f32[2,64,1024]{2,1,0:T(8,128)S(1)}, f32[2,64,1024]{2,1,0:T(8,128)}, u32[]{:S(2)}) copy-start(f32[2,64,1024]{2,1,0:T(8,128)} %get-tuple-element.65) | copy-start | bytes 1572868
  195.2 5.3 copy-start.8
  200.4 209.7 %copy-start.9 = (f32[512,16]{0,1:T(8,128)S(1)}, f32[512,16]{0,1:T(8,128)}, u32[]{:S(2)}) copy-start(f32[512,16]{0,1:T(8,128)} %param.46) | copy-start | bytes 98308
  200.4 209.7 %copy-start.11 = (f32[512,16]{0,1:T(8,128)S(1)}, f32[512,16]{0,1:T(8,128)}, u32[]{:S(2)}) copy-start(f32[512,16]{0,1:T(8,128)} %param.47) | copy-start | bytes 98308
  200.4 209.7 %copy-start.12 = (f32[512,16]{0,1:T(8,128)S(1)}, f32[512,16]{0,1:T(8,128)}, u32[]{:S(2)}) copy-start(f32[512,16]{0,1:T(8,128)} %param.48) | copy-start | bytes 98308
  404.6 11.7 %copy-start.2 = (f32[512,256]{1,0:T(8,128)S(1)}, f32[512,256]{1,0:T(8,128)}, u32[]{:S(2)}) copy-start(f32[512,256]{1,0:T(8,128)} %weight.3) | copy-start | bytes 1572868
  404.6 11.7 %copy-start.3 = (f32[512,256]{1,0:T(8,128)S(1)}, f32[512,256]{1,0:T(8,128)}, u32[]{:S(2)}) copy-start(f32[512,256]{1,0:T(8,128)} %mean.3) | copy-start | bytes 1572868
  416.3 1.0 copy-start.4
  419.1 6.4 %copy-start.1 = (f32[512,1024]{1,0:T(8,128)S(1)}, f32[512,1024]{1,0:T(8,128)}, u32[]{:S(2)}) copy-start(f32[512,1024]{1,0:T(8,128)} %mean.4) | copy-start | bytes 6291460

commit v5 on v4

--- a/solution.py
+++ b/solution.py
@@ -21,17 +21,6 @@
 EPSILON = 1e-08
 CLIP = 1.0
 LOW = jnp.bfloat16
-
-
-def modln(h, shift, scale):
-    mean = jnp.mean(h, -1, keepdims=True)
-    cent = h - mean
-    var = jnp.mean(cent * cent, -1, keepdims=True)
-    return cent * lax.rsqrt(var + 1e-06) * (1.0 + scale) + shift
-
-
-def gelu_tanh(v):
-    return jax.nn.gelu(v, approximate=True)
 
 
 def noise_level(steps):
@@ -57,22 +46,6 @@
     return jnp.concatenate([jnp.sin(across), jnp.cos(across), jnp.sin(down), jnp.cos(down)], -1)
 
 
-def adamw(weight, mean, square, grad):
-    mean_next = BETA * mean + (1.0 - BETA) * grad
-    square_next = BETA * square + (1.0 - BETA) * grad * grad
-    fixed_mean = mean_next / (1.0 - BETA**STEP)
-    fixed_square = square_next / (1.0 - BETA**STEP)
-    weight_next = weight - RATE * (fixed_mean / (jnp.sqrt(fixed_square) + EPSILON) + DECAY * weight)
-    return [weight_next, mean_next, square_next]
-
-
-def rank_sum(left, right):
-    total = left[0][:, None] * right[0][None, :]
-    for k in range(1, left.shape[0]):
-        total = total + left[k][:, None] * right[k][None, :]
-    return total
-
-
 MESH = pl.DeviceIdType.MESH
 GROUPS = ((4, 4), (0, 4), (8, 4))
 QUERY, KEY, VALUE, OUT, HIDDEN, MLP = 4, 5, 6, 7, 0, 8
@@ -211,10 +184,11 @@
 
 
 def forward_kernel(
-    sizes, h0_ref, part_ref, hidden_ref, attend_ref, output_ref, h_out, mods_out, full_ref,
+    sizes, images, target_first, target_count, cond_in_ref, cond_ref, ends_ref, noisy_ref, pos_ref, target_ref, hidden_ref, attend_ref, output_ref,
+    dh_out, mods_out, dmods_out, loss_out, dpred_out, final_out, full_ref,
     keep_h, keep_mid, keep_a, keep_m, keep_q, keep_kv, keep_p, keep_att, keep_pre,
-    weights, stage_h, stage_a, stage_o, kv, h_ref, q_ref, mods_ref, mods_got, send_a, first_a, full_a, send_m, first_m, full_m,
-    x_sems, y_sems, pair_sems, own_sems, kv_sems, a_sems, m_sems, mods_x_sems, mods_t_sems,
+    weights, stage_h, stage_a, stage_o, part_ref, cond_buf, ends, kv, h_ref, q_ref, mods_ref, mods_got, send_a, first_a, full_a, send_m, first_m, full_m,
+    x_sems, y_sems, pair_sems, own_sems, kv_sems, a_sems, m_sems, mods_x_sems, mods_t_sems, cond_sems, ends_sems,
 ):
     nf, nc, nt = sizes["fsdp"], sizes["ctx"], sizes["tp"]
     chips = nc // 2
@@ -288,7 +262,7 @@
         for ahead in range(1, nf):
             x_copy(layer, k, ahead).start()
 
-    def lower(layer):
+    def lower_attend(layer):
         copies = stage_copies(layer)
         copies[0].wait()
         copies[2].wait()
@@ -296,7 +270,9 @@
             weights[layer, QUERY + k, f] = quarters(stage_a[k])
         weights[layer, OUT, f] = quarters(stage_o[0])
         send_x(layer, 0)
-        copies[1].wait()
+
+    def lower_rest(layer):
+        stage_copies(layer)[1].wait()
         tiles = local // LANES
         size = 4 * tiles * 16
         order = interleave(4, tiles, back=True)
@@ -321,6 +297,34 @@
             weights[layer, MLP + k, f] = quarters(stage_o[1 + k])
         send_x(layer, 2)
 
+    chunk = cond_buf.shape[-1]
+
+    def cond_copy(j):
+        return pltpu.make_async_copy(
+            cond_ref.at[:, pl.ds(pl.multiple_of(j * chunk, LANES), chunk)],
+            cond_buf.at[lax.rem(j, 2)],
+            cond_sems.at[lax.rem(j, 2)],
+        )
+
+    def multiply(j, carry):
+        @pl.when(j + 1 < columns // chunk)
+        def _():
+            cond_copy(j + 1).start()
+
+        cond_copy(j).wait()
+        product = dot(cond_in_ref[...], cond_buf[lax.rem(j, 2)].astype(LOW))
+        for n in range(images):
+            part_ref[
+                n // count, n % count : n % count + 1, pl.ds(pl.multiple_of(j * chunk, LANES), chunk)
+            ] = product[n : n + 1]
+        return carry
+
+    def ends_copy(ahead, at):
+        return remote(ends.at[at], ends.at[at], ends_sems, (ahead - 1,), fsdp=lax.rem(f + ahead, nf))
+
+    def both_ends():
+        return ends[...].reshape(width, LANES)
+
     def store_copy(layer):
         return pltpu.make_async_copy(weights.at[layer], full_ref.at[layer], own_sems.at[4 + layer])
 
@@ -364,15 +368,25 @@
     def _():
         for copy in stage_copies(0):
             copy.start()
+        cond_copy(0).start()
+        ends[f] = ends_ref[...]
         meet(sizes)
+        for ahead in range(1, nf):
+            ends_copy(ahead, f).start()
+        lower_attend(0)
+        lax.fori_loop(0, columns // chunk, multiply, 0)
         share_mods()
-        lower(0)
+        pass_y(0, 0)
+        lower_rest(0)
         for copy in stage_copies(1):
             copy.start()
-        h_ref[...] = h0_ref[...]
+        pass_pair(0, 0)
+        for ahead in range(1, nf):
+            ends_copy(ahead, f).wait_send()
+            ends_copy(ahead, lax.rem(f + nf - ahead, nf)).wait_recv()
+        for g in range(count):
+            h_ref[g] = dot_nt(noisy_ref[g], both_ends()) + pos_ref[...]
         finish_mods()
-        pass_y(0, 0)
-        pass_pair(0, 0)
         pass_y(0, 1)
 
     def matrix(k):
@@ -398,19 +412,41 @@
     def _():
         arrived(step, 0)
 
+    def finish(g):
+        normed, inv = norm_parts(h_ref[g])
+        shift, scale_row = (row(mods_ref, g, 6 * layers + k, width) for k in range(2))
+        final_in = (normed * (1.0 + scale_row) + shift).astype(LOW)
+        final_out[g] = final_in
+        lane = lax.broadcasted_iota(jnp.int32, (rows, LANES), 1)
+        inside = (lane >= target_first) & (lane < target_first + target_count)
+        diff = jnp.where(inside, dot(final_in, both_ends()) - target_ref[g], 0.0)
+        squares = jnp.sum((diff * diff).reshape(rows // 8, 8, LANES), 0)
+        loss_out[...] = squares if g == 0 else loss_out[...] + squares
+        d_pred = (2.0 * diff).astype(LOW)
+        dpred_out[g] = d_pred
+        d_h, d_shift, d_scale = norm_back(dot_nt(d_pred, both_ends()), normed, inv, scale_row)
+        dh_out[g] = d_h
+        put_row(dmods_out, g, 0, width, d_shift)
+        put_row(dmods_out, g, 1, width, d_scale)
+
     for g in range(count):
 
         @pl.when(step >= 1)
         def _():
             last_branch(g)
 
+        @pl.when(step == layers)
+        def _():
+            finish(g)
+
         @pl.when(step < layers)
         def _():
             begin(g)
 
     @pl.when(step + 1 < layers)
     def _():
-        lower(step + 1)
+        lower_attend(step + 1)
+        lower_rest(step + 1)
 
     @pl.when(step + 2 < layers)
     def _():
@@ -477,7 +513,6 @@
 
     @pl.when(step == layers)
     def _():
-        h_out[...] = h_ref[...]
         mods_out[...] = mods_ref[...]
 
         def drain(layer, carry):
@@ -493,11 +528,12 @@
         lax.fori_loop(0, layers, drain, 0)
 
 
-def forward(mesh, h0, part, hidden, attend, output):
+def forward(mesh, images, target_at, cond_in, cond, ends, noisy, pos, target, hidden, attend, output):
     sizes = dict(mesh.shape)
     nf, nc, nt = sizes["fsdp"], sizes["ctx"], sizes["tp"]
     chips = nc // 2
-    count, rows, width = h0.shape
+    count, rows, _ = noisy.shape
+    width, columns = pos.shape[1], cond.shape[1]
     layers, _, shard, local = attend.shape
     blocks, quarter = 4 + attend.shape[1] + output.shape[1], shard // nc
     heads = local // HEAD_DIM
@@ -528,24 +564,31 @@
     first = pltpu.VMEM((count, nt - 1, rows // nt, width), LOW)
     dma = pltpu.SemaphoreType.DMA
     return pl.pallas_call(
-        functools.partial(forward_kernel, sizes),
+        functools.partial(forward_kernel, sizes, images, *target_at),
         grid=(layers + 1,),
         out_shape=[
-            jax.ShapeDtypeStruct(h0.shape, f32),
-            jax.ShapeDtypeStruct((count, nt * part.shape[-1]), f32),
+            jax.ShapeDtypeStruct((count, rows, width), f32),
+            jax.ShapeDtypeStruct((count, nt * columns), f32),
+            jax.ShapeDtypeStruct((count, 2 * width), f32),
+            jax.ShapeDtypeStruct((8, LANES), f32),
+            jax.ShapeDtypeStruct((count, rows, LANES), LOW),
+            jax.ShapeDtypeStruct((count, rows, width), LOW),
             jax.ShapeDtypeStruct((layers, blocks, nf, chips, 2, quarter, local), LOW),
             *(shape for shape, _ in saves),
         ],
-        in_specs=[vmem, vmem, anywhere, anywhere, anywhere],
-        out_specs=[vmem, vmem, anywhere, *(spec for _, spec in saves)],
+        in_specs=[vmem, anywhere, *[vmem] * 4, anywhere, anywhere, anywhere],
+        out_specs=[*[vmem] * 6, anywhere, *(spec for _, spec in saves)],
         scratch_shapes=[
             pltpu.VMEM((layers, blocks, nf, chips, 2, quarter, local), LOW),
             *(pltpu.VMEM(w.shape[1:], f32) for w in (hidden, attend, output)),
+            pltpu.VMEM((nf, count, columns), f32),
+            pltpu.VMEM((2, shard, 512), f32),
+            pltpu.VMEM((nf, shard, LANES), LOW),
             pltpu.VMEM((layers, count, nc, rows, 2 * local), LOW),
             pltpu.VMEM((count, rows, width), f32),
             pltpu.VMEM((count, rows, local), LOW),
-            pltpu.VMEM((count, nt * part.shape[-1]), f32),
-            pltpu.VMEM((others, count, part.shape[-1]), f32),
+            pltpu.VMEM((count, nt * columns), f32),
+            pltpu.VMEM((others, count, columns), f32),
             whole, first, whole, whole, first, whole,
             dma((2, layers, 3, others)),
             dma((2, layers, 3, others, overs)),
@@ -556,6 +599,8 @@
             dma((2, 2, count, nt - 1)),
             dma((2, others)),
             dma((2, nt - 1)),
+            dma((2,)),
+            dma((2, others)),
         ],
         compiler_params=pltpu.CompilerParams(
             collective_id=1, has_side_effects=True, vmem_limit_bytes=56 * 2**20
@@ -566,7 +611,7 @@
             transcendentals=0,
         ),
         name="forward_layers",
-    )(h0, part, hidden, attend, output)
+    )(cond_in, cond, ends, noisy, pos, target, hidden, attend, output)
 
 
 def halves(value):
@@ -806,7 +851,7 @@
 
     when(1, layers, lambda: stage_2(A, old))
     when(2, layers, lambda: (pl.when(step >= 3)(lambda: end_wait(A, old, layer + 3)), stage_4(A, new, layer + 2))[1])
-    when(1, layers, lambda: stage_3(M, old))
+    when(2, layers, lambda: stage_3(M, old))
 
     @pl.when(step == layers)
     def _():
@@ -879,6 +924,7 @@
             attention_back(g)
 
     when(1, layers, lambda: stage_3(A, old))
+    when(0, 0, lambda: stage_3(H, new))
 
     @pl.when(step < layers)
     def _():
@@ -901,14 +947,15 @@
         pair_copy(A, new).start()
         for g in range(count):
             total_u(g).share()
-        stage_3(H, new)
+
+    when(1, layers - 1, lambda: stage_3(H, new))
+    when(0, 0, lambda: stage_3(M, new))
 
     images_row = max(8, images)
 
     @pl.when(step == layers)
     def _():
         shared(dcols_ref.at[f], dcols_ref, f_sems, "fsdp", nf)
-        dcols_out[...] = dcols_ref[...]
         product[...] = jnp.zeros_like(product)
         gram[...] = jnp.zeros_like(gram)
         index = lax.broadcasted_iota(jnp.int32, (LANES, chunk), 0)
@@ -927,6 +974,7 @@
                 pair = jnp.where(index == n, high, pair)
                 pair = jnp.where(index == images + n, low, pair)
             pair = pair.astype(LOW)
+            dcols_out[:, pl.ds(pl.multiple_of(j * chunk, LANES), chunk)] = pair[: dcols_out.shape[0]]
             gram[...] += dot_nt(pair, pair)
             cond_copy(j).wait()
             product[...] += dot_nt(cond_buf[lax.rem(j, 2)].astype(LOW), pair)
@@ -947,18 +995,18 @@
             small_y(ahead).start()
         shared(silu_got.at[t], silu_got, t_sems, "tp", nt)
         d_cvec = slot_sum(silu_got, nt) * slope_c_ref[...]
-        dcvec_ref[...] = d_cvec
         high, low = halves(d_cvec)
         pair = jnp.concatenate([high, low], 0).astype(LOW)
+        dcvec_ref[...] = pair
         time_label = jnp.sum(dot_nt(pair, pair) * gram_t_ref[...])
         total = dot(pair, time_ref[...])
         swish_got[f] = total[:images_row] + total[images_row:]
         share(swish_got.at[f], swish_got, a_sems, "fsdp", nf)
         shared(swish_got.at[f], swish_got, a_sems, "fsdp", nf)
         d_act = slot_sum(swish_got, nf) * slope_a_ref[...]
-        dact_ref[...] = d_act
         high, low = halves(d_act)
         pair = jnp.concatenate([high, low], 0).astype(LOW)
+        dact_ref[...] = pair
         freq = jnp.sum(dot_nt(pair, pair) * gram_f_ref[...])
         cond = jnp.sum(gram[...] * gram_c_ref[...])
         stat_ref[...] = jnp.full(
@@ -981,7 +1029,7 @@
         small_end(core).start()
         part = jnp.sum(square[...]) / chips + jnp.sum(total * total) / (nt * chips)
         index = lax.broadcasted_iota(jnp.int32, stat_ref.shape, 0)
-        stat_ref[...] = jnp.where(index < 8, stat_ref[...] + part, loss_ref[0:1] / nt)
+        stat_ref[...] = jnp.where(index < 8, stat_ref[...] + part, jnp.sum(loss_ref[...]) / nt)
         for k, (axis, size) in enumerate((("ctx", nc), ("fsdp", nf), ("tp", nt))):
             me = lax.axis_index(axis)
             slots = stat_got.at[k]
@@ -1030,9 +1078,9 @@
         out_shape=[
             jax.ShapeDtypeStruct((layers, blocks, 2, half, local), LOW),
             jax.ShapeDtypeStruct((2, half, LANES), f32),
-            jax.ShapeDtypeStruct((nf, count, columns), f32),
-            jax.ShapeDtypeStruct((padded, shard), f32),
-            jax.ShapeDtypeStruct((padded, width), f32),
+            jax.ShapeDtypeStruct((-(-2 * images // 16) * 16, columns), LOW),
+            jax.ShapeDtypeStruct((2 * padded, shard), LOW),
+            jax.ShapeDtypeStruct((2 * padded, width), LOW),
             jax.ShapeDtypeStruct((16, LANES), f32),
         ],
         in_specs=[vmem] * 13 + [anywhere, per_layer(full), *(per_layer(s) for s in saved)],
@@ -1098,78 +1146,16 @@
     )(dh0, mods, dmods_end, loss, noisy, dpred, final_in, *slopes, *grams, time_low, cond, full, *saved)
 
 
-FIX = 1.0 / (1.0 - BETA**STEP)
+FIX = math.sqrt(1.0 / (1.0 - BETA**STEP))
 
 
 def update_block(weight, mean, square, grad, outs, where):
-    mean_next = BETA * mean[where] + (1.0 - BETA) * grad
-    square_next = BETA * square[where] + (1.0 - BETA) * (grad * grad)
-    moved = (mean_next * FIX) / (jnp.sqrt(square_next * FIX) + EPSILON)
-    outs[0][where] = weight[where] - RATE * (moved + DECAY * weight[where])
+    mean_next = BETA * mean[where] + grad
+    square_next = BETA * square[where] + (grad * grad) * (1.0 / (1.0 - BETA))
+    moved = mean_next / (jnp.sqrt(square_next) + EPSILON / FIX)
+    outs[0][where] = weight[where] * (1.0 - RATE * DECAY) - (RATE * FIX) * moved
     outs[1][where] = mean_next
     outs[2][where] = square_next
-
-
-def update_plain_kernel(clip_ref, grad_ref, weight, mean, square, *outs):
-    clip = clip_ref[0, 0]
-    rows = weight.shape[-2]
-    piece = min(64, rows)
-    for r in range(0, rows, piece):
-        where = (0, 0, pl.ds(r, piece))
-        update_block(weight, mean, square, grad_ref[where].astype(jnp.float32) * clip, outs, where)
-
-
-def update_mixed_kernel(clip_ref, grad_ref, weight, mean, square, *outs):
-    clip = clip_ref[0, 0]
-    _, blocks, rows, columns = grad_ref.shape
-    tiles = columns // LANES
-    size = blocks * tiles * 16
-    order = interleave(blocks, tiles)
-    for r in range(rows // 16):
-        parts = [
-            grad_ref[0, k, 16 * r : 16 * r + 16, n * LANES : (n + 1) * LANES]
-            for k in range(blocks)
-            for n in range(tiles)
-        ]
-        grad = dot(order, jnp.concatenate(parts, 0)) * clip
-        update_block(weight, mean, square, grad, outs, (0, pl.ds(r * size, size)))
-
-
-def update_rank_kernel(clip_ref, left_ref, right_ref, weight, mean, square, *outs):
-    clip = clip_ref[0, 0]
-    rows = weight.shape[0]
-    piece = min(64, rows)
-    for r in range(0, rows, piece):
-        where = (pl.ds(r, piece),)
-        grad = dot_tn(left_ref[:, r : r + piece], right_ref[...]) * clip
-        update_block(weight, mean, square, grad, outs, where)
-
-
-def update(kernel, clip, factors, factor_specs, trio, spec, grid, name):
-    shape = jax.ShapeDtypeStruct(trio[0].shape, jnp.float32)
-    size = trio[0].size
-    return pl.pallas_call(
-        kernel,
-        grid=grid,
-        out_shape=[shape] * 3,
-        in_specs=[pl.BlockSpec(memory_space=pltpu.SMEM), *factor_specs, spec, spec, spec],
-        out_specs=[spec] * 3,
-        compiler_params=pltpu.CompilerParams(vmem_limit_bytes=48 * 2**20),
-        cost_estimate=pl.CostEstimate(flops=20 * size, bytes_accessed=26 * size, transcendentals=2 * size),
-        name=name,
-    )(clip, *factors, *trio)
-
-
-def update_plain(clip, grads, trio, first):
-    trio = [jnp.swapaxes(a, 1, 2) for a in trio]
-    layers, blocks, rows, columns = trio[0].shape
-    block = (1, 1, rows, columns)
-    spec = pl.BlockSpec(block, lambda i, j: (i, j, 0, 0))
-    grad_spec = pl.BlockSpec(block, lambda i, j: (i, first + j, 0, 0))
-    outs = update(
-        update_plain_kernel, clip, [grads], [grad_spec], trio, spec, (layers, blocks), "update_plain"
-    )
-    return [jnp.swapaxes(a, 1, 2) for a in outs]
 
 
 def mixed(a):
@@ -1178,56 +1164,149 @@
     return jnp.swapaxes(a, 2, 3).reshape(layers, -1, LANES)
 
 
-def update_mixed(clip, grads, trio):
-    layers, rows, blocks, columns = trio[0].shape
+def update_kernel(
+    plan, clip_ref, grads_ref, small_ref, cond_left, cond_right, time_left, time_right, freq_left, freq_right,
+    label_left, label_right, *refs,
+):
+    clip = clip_ref[0, 0] * (1.0 - BETA)
+    step = pl.program_id(0) * pl.num_programs(1) + pl.program_id(1)
+    names = ("attend", "hidden", "output", "cond", "time", "freq", "label", "patch", "head")
+    trios = {name: refs[3 * k : 3 * k + 3] for k, name in enumerate(names)}
+    outs = {name: refs[27 + 3 * k : 30 + 3 * k] for k, name in enumerate(names)}
+
+    def change(name, grad, where):
+        update_block(*trios[name], grad * clip, outs[name], where)
+
+    for name, first in (("attend", QUERY), ("output", OUT)):
+        _, blocks, rows, _ = trios[name][0].shape
+        piece = min(64, rows)
+        for b in range(blocks):
+            for r in range(0, rows, piece):
+                grad = grads_ref[0, first + b, r : r + piece].astype(jnp.float32)
+                change(name, grad, (0, b, pl.ds(r, piece)))
+
+    _, _, rows, columns = grads_ref.shape
     tiles = columns // LANES
+    size = 4 * tiles * 16
+    order = interleave(4, tiles)
+    for r in range(rows // 16):
+        parts = [
+            grads_ref[0, HIDDEN + k, 16 * r : 16 * r + 16, n * LANES : (n + 1) * LANES]
+            for k in range(4)
+            for n in range(tiles)
+        ]
+        change("hidden", dot(order, jnp.concatenate(parts, 0)), (0, pl.ds(r * size, size)))
+
+    def outer(name, left, right):
+        first, count = plan[name]
+
+        @pl.when((step >= first) & (step < first + count))
+        def _():
+            rows = trios[name][0].shape[0]
+            for r in range(0, rows, 64):
+                high = min(r + 64, rows)
+                change(name, dot_tn(left[:, r:high], right[...]), (pl.ds(r, high - r),))
+
+    outer("cond", cond_left, cond_right)
+    outer("time", time_left, time_right)
+    outer("freq", freq_left, freq_right)
+    outer("label", label_left, label_right)
+
+    @pl.when(step == 0)
+    def _():
+        small = jnp.transpose(small_ref[...])
+        at = 0
+        for name in ("patch", "head"):
+            rows = trios[name][0].shape[0]
+            change(name, small[at : at + rows], (pl.ds(0, rows),))
+            at += rows
+
+
+def update(clip, grads, small, factors, trios):
+    attend, hidden, output, patch, freq, time, label, cond, head = trios
+    layers, _, rows, local = grads.shape
+    parts = 4
+    steps = layers * parts
+    inner = rows // parts
+
+    def turned(trio):
+        return [jnp.swapaxes(a, -1, -2) for a in trio]
+
+    def outward(trio):
+        return [jnp.swapaxes(a, 1, 2) for a in trio]
+
+    arrays = {
+        "attend": outward(attend),
+        "hidden": [mixed(a) for a in hidden],
+        "output": outward(output),
+        "cond": list(cond),
+        "time": list(time),
+        "freq": list(freq),
+        "label": turned(label),
+        "patch": turned(patch),
+        "head": turned(head),
+    }
+    chunks = {"cond": 512, "time": LANES, "freq": LANES, "label": min(LANES, rows)}
+    plan, specs = {}, {}
+    for name, width in chunks.items():
+        count = arrays[name][0].shape[1] // width
+        plan[name] = (0 if name == "cond" else steps - count, count)
+
+    def at(name):
+        first, count = plan[name]
+        return lambda i, j: (0, jnp.clip(i * parts + j - first, 0, count - 1))
+
+    for name, (array, *_) in arrays.items():
+        if name in chunks:
+            specs[name] = pl.BlockSpec((array.shape[0], chunks[name]), at(name))
+        elif name == "hidden":
+            specs[name] = pl.BlockSpec((1, array.shape[1] // parts, LANES), lambda i, j: (i, j, 0))
+        elif array.ndim == 4:
+            specs[name] = pl.BlockSpec((1, array.shape[1], inner, local), lambda i, j: (i, 0, j, 0))
+        else:
+            specs[name] = pl.BlockSpec(array.shape, lambda i, j: (0, 0))
+    factor_specs = []
+    for name in ("cond", "time", "freq", "label"):
+        left, right = factors[name]
+        factor_specs.append(pl.BlockSpec(left.shape, lambda i, j: (0, 0)))
+        factor_specs.append(pl.BlockSpec((right.shape[0], chunks[name]), at(name)))
+    whole = [specs[name] for name in arrays for _ in range(3)]
+    flat = [a for name in arrays for a in arrays[name]]
+    size = sum(a.size for a in flat) // 3
+    outs = pl.pallas_call(
+        functools.partial(update_kernel, plan),
+        grid=(layers, parts),
+        out_shape=[jax.ShapeDtypeStruct(a.shape, jnp.float32) for a in flat],
+        in_specs=[
+            pl.BlockSpec(memory_space=pltpu.SMEM),
+            pl.BlockSpec((1, grads.shape[1], inner, local), lambda i, j: (i, 0, j, 0)),
+            pl.BlockSpec(small.shape, lambda i, j: (0, 0)),
+            *factor_specs,
+            *whole,
+        ],
+        out_specs=whole,
+        compiler_params=pltpu.CompilerParams(vmem_limit_bytes=60 * 2**20),
+        cost_estimate=pl.CostEstimate(flops=20 * size, bytes_accessed=26 * size, transcendentals=2 * size),
+        name="update",
+    )(clip, grads, small, *(f for name in ("cond", "time", "freq", "label") for f in factors[name]), *flat)
+    made = {name: outs[3 * k : 3 * k + 3] for k, name in enumerate(arrays)}
+    blocks = hidden[0].shape[2]
 
     def back(a):
-        a = a.reshape(layers, rows, tiles, blocks, LANES)
-        return jnp.swapaxes(a, 2, 3).reshape(layers, rows, blocks, columns)
-
-    step = min(rows, 128)
-    spec = pl.BlockSpec((1, step * blocks * tiles, LANES), lambda i, j: (i, j, 0))
-    grad_spec = pl.BlockSpec((1, blocks, step, columns), lambda i, j: (i, 0, j, 0))
-    outs = update(
-        update_mixed_kernel,
-        clip,
-        [grads],
-        [grad_spec],
-        [mixed(a) for a in trio],
-        spec,
-        (layers, rows // step),
-        "update_mixed",
-    )
-    return [back(a) for a in outs]
-
-
-def update_rank(clip, left, right, trio):
-    rows, columns = trio[0].shape
-    step = 512 if columns % 512 == 0 else columns
-    spec = pl.BlockSpec((rows, step), lambda i: (0, i))
-    left_spec = pl.BlockSpec(left.shape, lambda i: (0, 0))
-    right_spec = pl.BlockSpec((right.shape[0], step), lambda i: (0, i))
-    return update(
-        update_rank_kernel,
-        clip,
-        [left, right],
-        [left_spec, right_spec],
-        trio,
-        spec,
-        (columns // step,),
-        "update_rank",
-    )
-
-
-def split_rows(value, other):
-    rounded = lax.reduce_precision(value, 8, 7)
-    high, low = rounded.astype(LOW), (value - rounded).astype(LOW)
-    pad = -2 * value.shape[0] % 16
-    return (
-        jnp.pad(jnp.concatenate([high, low]), ((0, pad), (0, 0))),
-        jnp.pad(jnp.concatenate([other, other]).astype(LOW), ((0, pad), (0, 0))),
-    )
+        a = a.reshape(layers, rows, local // LANES, blocks, LANES)
+        return jnp.swapaxes(a, 2, 3).reshape(layers, rows, blocks, local)
+
+    return [
+        *outward(made["attend"]),
+        *(back(a) for a in made["hidden"]),
+        *outward(made["output"]),
+        *turned(made["patch"]),
+        *made["freq"],
+        *made["time"],
+        *turned(made["label"]),
+        *made["cond"],
+        *turned(made["head"]),
+    ]
 
 
 def per_device(
@@ -1282,41 +1361,35 @@
     )
     cvec = temb + jnp.dot(onehot, label_table.astype(LOW).T, preferred_element_type=jnp.float32)
     cond_in = jax.nn.silu(cvec).astype(LOW)
-    cond_low = cond_weight.astype(LOW)
-    mods_part = jnp.dot(cond_in, cond_low, preferred_element_type=jnp.float32)
-    patch_head = lax.all_gather(
-        jnp.concatenate([patch_weight, head_weight], 1).astype(LOW), "fsdp", axis=0, tiled=True
-    )
-    patch_full, head_full = patch_head[:, :patch_in], patch_head[:, patch_in:]
-    width = patch_full.shape[0]
-
     level = noise_level(timesteps)[:, None, None]
     noisy = (jnp.sqrt(level) * latents + jnp.sqrt(1.0 - level) * noise).astype(LOW)
-    first = lax.axis_index("ctx") * rows
-    h = (
-        jnp.einsum("gsp,dp->gsd", noisy, patch_full, preferred_element_type=jnp.float32)
-        + positions(first, rows, width)[None]
-    )
-    h, flat_mods, full, *saved = forward(
+    images = freqs.shape[0]
+    width = time_weight.shape[1]
+    patch_out = head_weight.shape[1]
+    after = LANES - patch_in - patch_out
+
+    def twice(value, each):
+        value = jnp.pad(value.astype(LOW), ((0, each - images), (0, 0)))
+        return jnp.pad(jnp.concatenate([value, value]), ((0, -2 * each % 16), (0, 0)))
+
+    cond_parts = twice(cond_in, images)
+    noisy_wide = jnp.pad(noisy, ((0, 0), (0, 0), (0, LANES - patch_in)))
+    d_h, flat_mods, d_mods_end, loss_part, d_pred, final_in, full, *saved = forward(
         mesh,
-        h,
-        mods_part.reshape(-1, count, columns),
+        images,
+        (patch_in, patch_out),
+        cond_parts,
+        cond_weight,
+        jnp.pad(jnp.concatenate([patch_weight, head_weight], 1).astype(LOW), ((0, 0), (0, after))),
+        noisy_wide,
+        positions(lax.axis_index("ctx") * rows, rows, width),
+        jnp.pad(jnp.concatenate([noise, var_target], 2), ((0, 0), (0, 0), (patch_in, after))),
         mixed(hidden_weight),
         jnp.swapaxes(attend_weight, 1, 2),
         jnp.swapaxes(output_weight, 1, 2),
     )
     blocks = full.shape[1]
     full = full.reshape(layers, blocks, width, -1)
-    mods = flat_mods.reshape(count, -1, width)
-    final_in = modln(h, mods[:, 6 * layers, None], mods[:, 6 * layers + 1, None]).astype(LOW)
-    pred = jnp.einsum("gsd,dp->gsp", final_in, head_full, preferred_element_type=jnp.float32)
-    diff = pred - jnp.concatenate([noise, var_target], -1)
-    loss_part = jnp.full((8, LANES), jnp.sum(diff * diff))
-    d_pred = (2.0 * diff).astype(LOW)
-    d_final = jnp.einsum("gsp,dp->gsd", d_pred, head_full, preferred_element_type=jnp.float32)
-    _, norm_back = jax.vjp(modln, h, mods[:, 6 * layers, None], mods[:, 6 * layers + 1, None])
-    d_h, d_shift_f, d_scale_f = norm_back(d_final)
-    images = freqs.shape[0]
     padded = max(8, images) - images
     tokens = count * rows
 
@@ -1337,16 +1410,15 @@
         doubled(gram(swish) + gram(onehot)),
         doubled(gram(freqs)),
     )
-    patch_out = d_pred.shape[-1]
     grads, d_small, d_cols, d_cvec, d_act, stat = backward(
         mesh,
         images,
         d_h,
         flat_mods,
-        jnp.concatenate([d_shift_f, d_scale_f], 2).reshape(count, -1),
+        d_mods_end,
         loss_part,
-        jnp.pad(noisy.reshape(tokens, -1), ((0, 0), (0, LANES - patch_in))),
-        jnp.pad(d_pred.reshape(tokens, -1), ((0, 0), (patch_in, LANES - patch_in - patch_out))),
+        noisy_wide.reshape(tokens, -1),
+        d_pred.reshape(tokens, -1),
         final_in.reshape(tokens, -1),
         (slope(cvec), slope(act)),
         grams,
@@ -1357,36 +1429,34 @@
     )
     grads = grads.reshape(layers, blocks, shard, -1)
     d_small = d_small.reshape(shard, -1)
-    d_cols = d_cols.reshape(images, columns)
-    d_cvec = d_cvec[:images]
-    d_act = lax.dynamic_slice_in_dim(
-        d_act[:images], lax.axis_index("fsdp") * shard, shard, 1
-    )
+    d_act = lax.dynamic_slice_in_dim(d_act, lax.axis_index("fsdp") * shard, shard, 1)
     total_sq, loss = stat[0, 0], stat[8, 0]
     grad_norm = jnp.sqrt(total_sq)
     clip = jnp.minimum(1.0, CLIP / (grad_norm + 1e-06))
     factor = clip.reshape(1, 1)
-    cols_parts, cond_parts = split_rows(d_cols, cond_in)
-    cvec_parts, swish_parts = split_rows(d_cvec, swish)
-    act_parts, freq_parts = split_rows(d_act, freqs)
-    updated = [
-        *update_plain(factor, grads, (attend_weight, attend_mean, attend_square), QUERY),
-        *update_mixed(factor, grads, (hidden_weight, hidden_mean, hidden_square)),
-        *update_plain(factor, grads, (output_weight, output_mean, output_square), OUT),
-        *adamw(patch_weight, patch_mean, patch_square, d_small[:, :patch_in] * clip),
-        *update_rank(factor, act_parts, freq_parts, (freq_weight, freq_mean, freq_square)),
-        *update_rank(factor, cvec_parts, swish_parts, (time_weight, time_mean, time_square)),
-        *adamw(
-            label_table,
-            label_mean,
-            label_square,
-            rank_sum(d_cvec, onehot.astype(jnp.float32)) * clip,
+    each = max(8, images)
+    updated = update(
+        factor,
+        grads,
+        d_small,
+        {
+            "cond": (cond_parts, d_cols),
+            "time": (d_cvec, twice(swish, each)),
+            "freq": (d_act, twice(freqs, each)),
+            "label": (twice(onehot, each), d_cvec),
+        },
+        (
+            (attend_weight, attend_mean, attend_square),
+            (hidden_weight, hidden_mean, hidden_square),
+            (output_weight, output_mean, output_square),
+            (patch_weight, patch_mean, patch_square),
+            (freq_weight, freq_mean, freq_square),
+            (time_weight, time_mean, time_square),
+            (label_table, label_mean, label_square),
+            (cond_weight, cond_mean, cond_square),
+            (head_weight, head_mean, head_square),
         ),
-        *update_rank(factor, cond_parts, cols_parts, (cond_weight, cond_mean, cond_square)),
-        *adamw(
-            head_weight, head_mean, head_square, d_small[:, patch_in : patch_in + patch_out] * clip
-        ),
-    ]
+    )
     return (loss, grad_norm, *updated)
 
 

time: 546 us -> 496 us (0.908)
  Pallas kernels: 474 us -> 458 us
  other arithmetic: 19.3 us -> 8.82 us
  local copies, waits for them, and re-layouts: 21.4 us -> 12.8 us
  matrix products: 10.5 us -> 2.44 us
    pallas_call x7 -> x2, Pallas kernels: 270 us -> 256 us  [the longest x1 162 us: forward(): pl.pallas_call(functools.partial(forward_kernel, sizes, images, *target_a...]
    sub x3 -> x0, other arithmetic: 8.65 us -> none  [adamw(): weight - RATE * (fixed_mean / (jnp.sqrt(fixed_square) + EPSILON) + DECAY...]
    dot_general x4 -> x0, matrix products: 8.11 us -> none  [the longest x1 5.86 us: per_device(): mods_part = jnp.dot(cond_in, cond_low, preferred_element_type=jnp.float32)]
where the time goes in v5:
time: 496 us; the launch traced here: 495 us
  Pallas kernels  458 us (92%)
  local copies, waits for them, and re-layouts  12.8 us (3%)
  blocking collectives  9.56 us (2%)
  other arithmetic  8.82 us (2%)
    pallas_call x1, Pallas kernels, backward(): pl.pallas_call(functools.partial(backward_kernel, sizes, images), grid=(l...  202 us
    pallas_call x1, Pallas kernels, forward(): pl.pallas_call(functools.partial(forward_kernel, sizes, images, *target_a...  162 us
    pallas_call x1, Pallas kernels, update(): pl.pallas_call(functools.partial(update_kernel, plan), grid=(layers, part...  93.9 us

profile of v5, /device:TPU:0, one launch (start us, length us, event | category | flops | bytes accessed | tf_op | source)
XLA Modules:
  0.0 494.6 jit_solution(13930752452865344178)
XLA Ops:
  0.7 1.4 dynamic-slice
  2.7 0.9 dynamic-update-slice
  3.6 0.8 dynamic-update-slice.1
  4.4 5.2 %all-reduce.14 = (s32[4]{0:T(128)S(1)}, s32[4]{0:T(128)S(1)}) all-reduce(s32[4]{0:T(128)S(1)} %dynamic-update-slice, s32[4]{0:T(128)S(1)} %dynamic-update-slice.1), channel_id=1, replica_groups=mesh['fsdp'=2,'ctx'=4,'tp'=4] {'fsdp'}, use_global_device_ids=true, to_apply=%add.12 | all-reduce | flops 8 | bytes 64
  9.8 0.7 subtract_sqrt_fusion
  11.3 1.2 fusion.1
  12.5 4.4 all_gather.10
  17.3 0.7 tile.30.gram_t_ref
  18.0 0.7 tile.32.gram_f_ref
  19.9 0.8 convert.17
  21.3 0.8 convert.18
  22.1 0.8 copy.87
  22.9 0.8 copy.86
  24.4 0.8 copy.89
  25.2 0.7 select_maximum_fusion.target_ref
  26.1 0.7 pad.49.ends_ref
  27.3 0.7 pad_maximum_fusion.pos_ref
  28.0 1.7 convert_element_type.71.time_ref
  31.9 0.6 pad.54.gram_c_ref
  32.6 161.9 %forward_layers.1 = (f32[2,64,1024]{2,1,0:T(8,128)}, f32[2,26624]{1,0:T(2,128)}, f32[2,2048]{1,0:T(2,128)}, f32[8,128]{1,0:T(8,128)}, bf16[2,64,128]{2,1,0:T(8,1...) custom-call(bf16[16,512]{1,0:T(8,128)(2,1)} %fusion.8.cond_in_ref.co, ...), custom_call_target="tpu_custom_call" | custom-call | flops 3221225472 | bytes 50331648 | tf_op jit(solution)/shard_map/forward_layers/pallas_call | solution.py:566
  194.5 201.8 %backward_layers.1 = (bf16[4,12,2,256,256]{4,3,2,1,0:T(8,128)(2,1)}, f32[2,256,128]{2,1,0:T(8,128)}, bf16[16,6656]{1,0:T(8,128)(2,1)}, bf16[16,512]{1,0:T(8,128)...) custom-call(f32[2,64,1024]{2,1,0:T(8,128)} %get-tuple-element.78.dh0_ref, f32[2,26624]{1,0:T(2,128)} %get-tuple-element.79.mods_ref, ...), custom_call_target="tpu_custom_call" | custom-call | flops 6442450944 | bytes 50331648 | tf_op jit(solution)/shard_map/backward_layers/pallas_call | solution.py:1075
  396.3 1.2 fusion.16
  398.2 1.3 constant_dynamic-slice_fusion.freq_left
  399.5 93.9 %update.1 = (f32[4,3,512,256]{3,2,1,0:T(8,128)}, f32[4,3,512,256]{3,2,1,0:T(8,128)}, f32[4,3,512,256]{3,2,1,0:T(8,128)}, f32[4,4096,128]{2,1,0:T(8,128)}, f32[4,...) custom-call(f32[1,1]{1,0:T(1,128)} %bitcast.12.clip_ref, ...), custom_call_target="tpu_custom_call" | custom-call | flops 217835520 | bytes 283186176 | tf_op jit(solution)/shard_map/update/pallas_call | solution.py:1276
  (40 shorter events, 6.7 us)
Async XLA Ops:
  0.7 29.5 %copy-start.1 = (f32[512,1001]{0,1:T(8,128)S(1)}, f32[512,1001]{0,1:T(8,128)}, u32[]{:S(2)}) copy-start(f32[512,1001]{0,1:T(8,128)} %param.55) | copy-start | bytes 6150148
  29.8 164.7 %copy-start = (bf16[512,1024]{1,0:T(8,128)(2,1)}, bf16[512,1024]{1,0:T(8,128)(2,1)S(1)}, u32[]{:S(2)}) copy-start(bf16[512,1024]{1,0:T(8,128)(2,1)S(1)} %convert_element_type.71.time_ref) | copy-start | bytes 3145732

commit v6 on v5

--- a/solution.py
+++ b/solution.py
@@ -184,7 +184,7 @@
 
 
 def forward_kernel(
-    sizes, images, target_first, target_count, cond_in_ref, cond_ref, ends_ref, noisy_ref, pos_ref, target_ref, hidden_ref, attend_ref, output_ref,
+    sizes, images, target_first, target_count, cond_in_ref, cond_ref, patch_ref, head_ref, noisy_ref, pos_ref, target_ref, hidden_ref, attend_ref, output_ref,
     dh_out, mods_out, dmods_out, loss_out, dpred_out, final_out, full_ref,
     keep_h, keep_mid, keep_a, keep_m, keep_q, keep_kv, keep_p, keep_att, keep_pre,
     weights, stage_h, stage_a, stage_o, part_ref, cond_buf, ends, kv, h_ref, q_ref, mods_ref, mods_got, send_a, first_a, full_a, send_m, first_m, full_m,
@@ -369,7 +369,9 @@
         for copy in stage_copies(0):
             copy.start()
         cond_copy(0).start()
-        ends[f] = ends_ref[...]
+        used = jnp.concatenate([patch_ref[...], head_ref[...]], 0)
+        unused = jnp.zeros((LANES - used.shape[0], used.shape[1]), jnp.float32)
+        ends[f] = jnp.transpose(jnp.concatenate([used, unused], 0)).astype(LOW)
         meet(sizes)
         for ahead in range(1, nf):
             ends_copy(ahead, f).start()
@@ -528,7 +530,7 @@
         lax.fori_loop(0, layers, drain, 0)
 
 
-def forward(mesh, images, target_at, cond_in, cond, ends, noisy, pos, target, hidden, attend, output):
+def forward(mesh, images, target_at, cond_in, cond, patch, head, noisy, pos, target, hidden, attend, output):
     sizes = dict(mesh.shape)
     nf, nc, nt = sizes["fsdp"], sizes["ctx"], sizes["tp"]
     chips = nc // 2
@@ -576,7 +578,7 @@
             jax.ShapeDtypeStruct((layers, blocks, nf, chips, 2, quarter, local), LOW),
             *(shape for shape, _ in saves),
         ],
-        in_specs=[vmem, anywhere, *[vmem] * 4, anywhere, anywhere, anywhere],
+        in_specs=[vmem, anywhere, *[vmem] * 5, anywhere, anywhere, anywhere],
         out_specs=[*[vmem] * 6, anywhere, *(spec for _, spec in saves)],
         scratch_shapes=[
             pltpu.VMEM((layers, blocks, nf, chips, 2, quarter, local), LOW),
@@ -611,7 +613,7 @@
             transcendentals=0,
         ),
         name="forward_layers",
-    )(cond_in, cond, ends, noisy, pos, target, hidden, attend, output)
+    )(cond_in, cond, patch, head, noisy, pos, target, hidden, attend, output)
 
 
 def halves(value):
@@ -621,7 +623,7 @@
 
 def backward_kernel(
     sizes, images, dh0_ref, mods_ref, dmods_end_ref, loss_ref, noisy_ref, dpred_ref, final_ref,
-    slope_c_ref, slope_a_ref, gram_c_ref, gram_t_ref, gram_f_ref, time_ref, cond_ref,
+    slope_c_ref, slope_a_ref, cond_in_ref, swish_ref, onehot_ref, freqs_ref, time_ref, cond_ref,
     w_ref, keep_h, keep_mid, keep_a, keep_m, keep_q, keep_kv, keep_p, keep_att, keep_pre,
     grads_ref, small_ref, dcols_out, dcvec_ref, dact_ref, stat_ref,
     dh_ref, dmid_ref, h_ref, act_ref, dpre_ref, branch_ref, dba_ref, dqkv_ref, dm_ref,
@@ -953,6 +955,9 @@
 
     images_row = max(8, images)
 
+    def own_gram(ref):
+        return dot_nt(ref[...], ref[...])
+
     @pl.when(step == layers)
     def _():
         shared(dcols_ref.at[f], dcols_ref, f_sems, "fsdp", nf)
@@ -998,8 +1003,9 @@
         high, low = halves(d_cvec)
         pair = jnp.concatenate([high, low], 0).astype(LOW)
         dcvec_ref[...] = pair
-        time_label = jnp.sum(dot_nt(pair, pair) * gram_t_ref[...])
-        total = dot(pair, time_ref[...])
+        fixed = own_gram(swish_ref) + own_gram(onehot_ref)
+        time_label = jnp.sum(dot_nt(pair, pair) * fixed)
+        total = dot(pair, time_ref[...].astype(LOW))
         swish_got[f] = total[:images_row] + total[images_row:]
         share(swish_got.at[f], swish_got, a_sems, "fsdp", nf)
         shared(swish_got.at[f], swish_got, a_sems, "fsdp", nf)
@@ -1007,8 +1013,9 @@
         high, low = halves(d_act)
         pair = jnp.concatenate([high, low], 0).astype(LOW)
         dact_ref[...] = pair
-        freq = jnp.sum(dot_nt(pair, pair) * gram_f_ref[...])
-        cond = jnp.sum(gram[...] * gram_c_ref[...])
+        freq = jnp.sum(dot_nt(pair, pair) * own_gram(freqs_ref))
+        size = cond_in_ref.shape[0]
+        cond = jnp.sum(gram[:size, :size] * own_gram(cond_in_ref))
         stat_ref[...] = jnp.full(
             stat_ref.shape, cond / nc + time_label / (nt * nc) + freq / (nf * nt * nc), f32
         )
@@ -1044,7 +1051,7 @@
         small_end(1 - core).wait_recv()
 
 
-def backward(mesh, images, dh0, mods, dmods_end, loss, noisy, dpred, final_in, slopes, grams, time_low, cond, full, saved):
+def backward(mesh, images, dh0, mods, dmods_end, loss, noisy, dpred, final_in, slopes, rights, time, cond, full, saved):
     sizes = dict(mesh.shape)
     nf, nc, nt = sizes["fsdp"], sizes["ctx"], sizes["tp"]
     chips = nc // 2
@@ -1083,7 +1090,7 @@
             jax.ShapeDtypeStruct((2 * padded, width), LOW),
             jax.ShapeDtypeStruct((16, LANES), f32),
         ],
-        in_specs=[vmem] * 13 + [anywhere, per_layer(full), *(per_layer(s) for s in saved)],
+        in_specs=[vmem] * 14 + [anywhere, per_layer(full), *(per_layer(s) for s in saved)],
         out_specs=[anywhere, anywhere, vmem, vmem, vmem, vmem],
         scratch_shapes=[
             image, image, image, mlp, mlp, image_low, image_low,
@@ -1143,7 +1150,7 @@
             transcendentals=0,
         ),
         name="backward_layers",
-    )(dh0, mods, dmods_end, loss, noisy, dpred, final_in, *slopes, *grams, time_low, cond, full, *saved)
+    )(dh0, mods, dmods_end, loss, noisy, dpred, final_in, *slopes, *rights, time, cond, full, *saved)
 
 
 FIX = math.sqrt(1.0 / (1.0 - BETA**STEP))
@@ -1348,8 +1355,9 @@
     layers, shard = attend_weight.shape[:2]
     columns = cond_weight.shape[1]
 
-    steps_all = lax.all_gather(timesteps, "fsdp", axis=0, tiled=True)
-    labels_all = lax.all_gather(labels, "fsdp", axis=0, tiled=True)
+    own = jnp.pad(jnp.stack([timesteps, labels]).astype(jnp.float32), ((0, 6), (0, LANES - count)))
+    drawn = lax.all_gather(own, "fsdp", axis=0)[:, :2, :count]
+    steps_all, labels_all = (drawn[:, k].reshape(-1).astype(jnp.int32) for k in range(2))
     freqs = time_freqs(steps_all).astype(LOW)
     act = jnp.dot(freqs, freq_weight.astype(LOW).T, preferred_element_type=jnp.float32)
     act = lax.all_gather(act, "fsdp", axis=1, tiled=True)
@@ -1380,7 +1388,8 @@
         (patch_in, patch_out),
         cond_parts,
         cond_weight,
-        jnp.pad(jnp.concatenate([patch_weight, head_weight], 1).astype(LOW), ((0, 0), (0, after))),
+        patch_weight.T,
+        head_weight.T,
         noisy_wide,
         positions(lax.axis_index("ctx") * rows, rows, width),
         jnp.pad(jnp.concatenate([noise, var_target], 2), ((0, 0), (0, 0), (patch_in, after))),
@@ -1397,19 +1406,8 @@
         _, back = jax.vjp(jax.nn.silu, value)
         return jnp.pad(back(jnp.ones_like(value))[0], ((0, padded), (0, 0)))
 
-    def gram(value):
-        value = value.astype(jnp.float32)
-        return jnp.einsum("nd,md->nm", value, value, precision=HIGH)
-
-    def doubled(value):
-        return jnp.tile(jnp.pad(value, ((0, padded), (0, padded))), (2, 2))
-
-    beyond = LANES - 2 * images
-    grams = (
-        jnp.pad(jnp.tile(gram(cond_in), (2, 2)), ((0, beyond), (0, beyond))),
-        doubled(gram(swish) + gram(onehot)),
-        doubled(gram(freqs)),
-    )
+    each = max(8, images)
+    swish_parts, onehot_parts, freq_parts = (twice(v, each) for v in (swish, onehot, freqs))
     grads, d_small, d_cols, d_cvec, d_act, stat = backward(
         mesh,
         images,
@@ -1421,8 +1419,8 @@
         d_pred.reshape(tokens, -1),
         final_in.reshape(tokens, -1),
         (slope(cvec), slope(act)),
-        grams,
-        time_low,
+        (cond_parts, swish_parts, onehot_parts, freq_parts),
+        time_weight,
         cond_weight,
         full,
         saved,
@@ -1434,16 +1432,15 @@
     grad_norm = jnp.sqrt(total_sq)
     clip = jnp.minimum(1.0, CLIP / (grad_norm + 1e-06))
     factor = clip.reshape(1, 1)
-    each = max(8, images)
     updated = update(
         factor,
         grads,
         d_small,
         {
             "cond": (cond_parts, d_cols),
-            "time": (d_cvec, twice(swish, each)),
-            "freq": (d_act, twice(freqs, each)),
-            "label": (twice(onehot, each), d_cvec),
+            "time": (d_cvec, swish_parts),
+            "freq": (d_act, freq_parts),
+            "label": (onehot_parts, d_cvec),
         },
         (
             (attend_weight, attend_mean, attend_square),

time: 496 us -> 489 us (0.986)
  local copies, waits for them, and re-layouts: 12.8 us -> 6.98 us
    all_gather x0 -> x1, blocking collectives: none -> 5.23 us  [per_device(): drawn = lax.all_gather(own, 'fsdp', axis=0)[:, :2, :count]]
    unnamed x1 -> x0, blocking collectives: 5.19 us -> none
where the time goes in v6:
time: 489 us; the launch traced here: 488 us
  Pallas kernels  458 us (94%)
  blocking collectives  9.6 us (2%)
  local copies, waits for them, and re-layouts  6.98 us (1%)
  other arithmetic  6.15 us (1%)
  matrix products  5.06 us (1%)
    pallas_call x1, Pallas kernels, backward(): pl.pallas_call(functools.partial(backward_kernel, sizes, images), grid=(l...  203 us
    pallas_call x1, Pallas kernels, forward(): pl.pallas_call(functools.partial(forward_kernel, sizes, images, *target_a...  161 us
    pallas_call x1, Pallas kernels, update(): pl.pallas_call(functools.partial(update_kernel, plan), grid=(layers, part...  93.9 us

profile of v6, /device:TPU:0, one launch (start us, length us, event | category | flops | bytes accessed | tf_op | source)
XLA Modules:
  0.0 488.2 jit_solution(16714799448490539309)
XLA Ops:
  0.7 0.7 add_convert_fusion.2
  1.4 0.7 subtract_sqrt_fusion
  2.1 5.2 %all-gather = f32[16,128]{1,0:T(8,128)S(1)} all-gather(f32[8,128]{1,0:T(8,128)S(1)} %pad.37), channel_id=2, replica_groups=mesh['fsdp'=2,'ctx'=4,'tp'=4] {'fsdp'}, dimensions={0}, use_global_device_ids=true | all-gather | bytes 12288 | tf_op jit(solution)/shard_map/all_gather | solution.py:1359
  7.7 0.6 pad_maximum_fusion.2.freqs_ref.freq_right
  8.4 1.2 fusion.3
  9.6 4.4 all_gather.11
  14.0 2.0 fusion
  15.9 1.9 fusion.12
  17.8 0.6 pad.41.slope_c_ref
  18.5 0.6 fusion.10.cond_in_ref.cond_left
  19.1 0.6 pad_maximum_fusion.1.swish_ref.time_right
  19.7 0.6 pad.42.slope_a_ref
  20.3 0.6 add_convert_fusion.1.onehot_ref.label_left
  20.9 0.8 copy.77
  21.7 0.8 copy.76
  22.6 0.6 pad.39.noisy_ref
  23.2 0.8 copy.79
  24.0 0.7 select_maximum_fusion.target_ref
  25.3 0.7 pad_maximum_fusion.pos_ref
  26.0 160.9 %forward_layers.1 = (f32[2,64,1024]{2,1,0:T(8,128)}, f32[2,26624]{1,0:T(2,128)}, f32[2,2048]{1,0:T(2,128)}, f32[8,128]{1,0:T(8,128)}, bf16[2,64,128]{2,1,0:T(8,1...) custom-call(bf16[16,512]{1,0:T(8,128)(2,1)} %fusion.10.cond_in_ref.c, ...), custom_call_target="tpu_custom_call" | custom-call | flops 3221225472 | bytes 50331648 | tf_op jit(solution)/shard_map/forward_layers/pallas_call | solution.py:568
  186.9 203.0 %backward_layers.1 = (bf16[4,12,2,256,256]{4,3,2,1,0:T(8,128)(2,1)}, f32[2,256,128]{2,1,0:T(8,128)}, bf16[16,6656]{1,0:T(8,128)(2,1)}, bf16[16,512]{1,0:T(8,128)...) custom-call(f32[2,64,1024]{2,1,0:T(8,128)} %get-tuple-element.78.dh0_ref, f32[2,26624]{1,0:T(2,128)} %get-tuple-element.79.mods_ref, ...), custom_call_target="tpu_custom_call" | custom-call | flops 6442450944 | bytes 50331648 | tf_op jit(solution)/shard_map/backward_layers/pallas_call | solution.py:1082
  389.9 1.2 fusion.18
  391.9 1.3 constant_dynamic-slice_fusion.freq_left
  393.2 93.9 %update.1 = (f32[4,3,512,256]{3,2,1,0:T(8,128)}, f32[4,3,512,256]{3,2,1,0:T(8,128)}, f32[4,3,512,256]{3,2,1,0:T(8,128)}, f32[4,4096,128]{2,1,0:T(8,128)}, f32[4,...) custom-call(f32[1,1]{1,0:T(1,128)} %bitcast.16.clip_ref, ...), custom_call_target="tpu_custom_call" | custom-call | flops 217835520 | bytes 283186176 | tf_op jit(solution)/shard_map/update/pallas_call | solution.py:1283
  (18 shorter events, 1.1 us)

commit v7 on v6

--- a/solution.py
+++ b/solution.py
@@ -646,7 +646,7 @@
     count, rows, width = dh_ref.shape
     heads = local // HEAD_DIM
     scale = 1.0 / math.sqrt(HEAD_DIM)
-    piece = min(64, half)
+    piece = min(256, half)
     columns = cond_ref.shape[1]
     f32 = jnp.float32
     A, H, M = 0, 1, 2

time: 489 us -> 488 us (level)
  no operation moved by 1% of the time
where the time goes in v7:
time: 488 us; the launch traced here: 487 us
  Pallas kernels  457 us (94%)
  blocking collectives  9.6 us (2%)
  local copies, waits for them, and re-layouts  6.98 us (1%)
  other arithmetic  6.15 us (1%)
  matrix products  5.06 us (1%)
    pallas_call x1, Pallas kernels, backward(): pl.pallas_call(functools.partial(backward_kernel, sizes, images), grid=(l...  202 us
    pallas_call x1, Pallas kernels, forward(): pl.pallas_call(functools.partial(forward_kernel, sizes, images, *target_a...  161 us
    pallas_call x1, Pallas kernels, update(): pl.pallas_call(functools.partial(update_kernel, plan), grid=(layers, part...  93.9 us

profile of v7, /device:TPU:0, one launch (start us, length us, event | category | flops | bytes accessed | tf_op | source)
XLA Modules:
  0.0 487.4 jit_solution(17733322148755546903)
XLA Ops:
  0.7 0.7 add_convert_fusion.2
  1.4 0.7 subtract_sqrt_fusion
  2.1 5.2 %all-gather = f32[16,128]{1,0:T(8,128)S(1)} all-gather(f32[8,128]{1,0:T(8,128)S(1)} %pad.37), channel_id=2, replica_groups=mesh['fsdp'=2,'ctx'=4,'tp'=4] {'fsdp'}, dimensions={0}, use_global_device_ids=true | all-gather | bytes 12288 | tf_op jit(solution)/shard_map/all_gather | solution.py:1359
  7.7 0.6 pad_maximum_fusion.2.freqs_ref.freq_right
  8.4 1.2 fusion.3
  9.6 4.4 all_gather.11
  14.0 2.0 fusion
  15.9 1.9 fusion.12
  17.8 0.6 pad.41.slope_c_ref
  18.5 0.6 fusion.10.cond_in_ref.cond_left
  19.1 0.6 pad_maximum_fusion.1.swish_ref.time_right
  19.7 0.6 pad.42.slope_a_ref
  20.3 0.6 add_convert_fusion.1.onehot_ref.label_left
  20.9 0.8 copy.77
  21.7 0.8 copy.76
  22.6 0.6 pad.39.noisy_ref
  23.2 0.8 copy.79
  24.0 0.7 select_maximum_fusion.target_ref
  25.3 0.7 pad_maximum_fusion.pos_ref
  26.0 160.9 %forward_layers.1 = (f32[2,64,1024]{2,1,0:T(8,128)}, f32[2,26624]{1,0:T(2,128)}, f32[2,2048]{1,0:T(2,128)}, f32[8,128]{1,0:T(8,128)}, bf16[2,64,128]{2,1,0:T(8,1...) custom-call(bf16[16,512]{1,0:T(8,128)(2,1)} %fusion.10.cond_in_ref.c, ...), custom_call_target="tpu_custom_call" | custom-call | flops 3221225472 | bytes 50331648 | tf_op jit(solution)/shard_map/forward_layers/pallas_call | solution.py:568
  186.9 202.2 %backward_layers.1 = (bf16[4,12,2,256,256]{4,3,2,1,0:T(8,128)(2,1)}, f32[2,256,128]{2,1,0:T(8,128)}, bf16[16,6656]{1,0:T(8,128)(2,1)}, bf16[16,512]{1,0:T(8,128)...) custom-call(f32[2,64,1024]{2,1,0:T(8,128)} %get-tuple-element.78.dh0_ref, f32[2,26624]{1,0:T(2,128)} %get-tuple-element.79.mods_ref, ...), custom_call_target="tpu_custom_call" | custom-call | flops 6442450944 | bytes 50331648 | tf_op jit(solution)/shard_map/backward_layers/pallas_call | solution.py:1082
  389.1 1.2 fusion.18
  391.0 1.3 constant_dynamic-slice_fusion.freq_left
  392.3 93.9 %update.1 = (f32[4,3,512,256]{3,2,1,0:T(8,128)}, f32[4,3,512,256]{3,2,1,0:T(8,128)}, f32[4,3,512,256]{3,2,1,0:T(8,128)}, f32[4,4096,128]{2,1,0:T(8,128)}, f32[4,...) custom-call(f32[1,1]{1,0:T(1,128)} %bitcast.16.clip_ref, ...), custom_call_target="tpu_custom_call" | custom-call | flops 217835520 | bytes 283186176 | tf_op jit(solution)/shard_map/update/pallas_call | solution.py:1283
  (18 shorter events, 1.1 us)
